TPU v7x, 512 devices: a whole 4x8x8 slice. The times are simulated.
512 devices in a mesh: rep: 4 (over y_hi, core), row: 8 (over z), col: 16 (over y_lo, x).
Axes of the slice: x: 4, y: 8 (y_hi: 2, y_lo: 4; y = y_hi * 4 + y_lo), z: 8, core: 2. Of those that a mesh axis runs over, the one named last changes fastest.
Arguments:
- acts: bfloat16 [512, 16384], P('rep', 'row'), may hold values from -12 to 12
- grad_out: bfloat16 [512, 49152], P('rep', 'col'), may hold values from -32 to 32
- weight_slab: bfloat16 [4, 16384, 12288], P('rep', 'row', 'col'), may hold values from -0.02734375 to 0.02734375
Outputs:
- input_grad: bfloat16 [512, 16384], P(('rep', 'col'), 'row')
- left_stats: float32 [1024, 16384], P(('rep', 'col'), 'row')
- right_stats: float32 [1024, 49152], P(('rep', 'row'), 'col')
All inputs are finite; a program needn't handle non-finite values.
Results may differ from a plain program's by a relative error of at most 0.0047.
Values may be sent and summed in bfloat16 or wider, within the bound.
No kernel may reach another device: no remote copies, remote signals or barrier semaphores. Data moves between devices by JAX's collectives and lax.ppermute only.
A program may use at most 64 MiB of HBM per device.

v0:
```python
import jax
import jax.numpy as jnp
from jax import lax
from jax.sharding import PartitionSpec as P

D = 16384
FF = 49152
BLOCK = 1024


def body(acts, grad_out, weight_slab):
    tokens = acts.shape[0]
    width = acts.shape[1]
    hidden = grad_out.shape[1]
    quarter = weight_slab.shape[2]
    replicas = lax.axis_size("rep")
    columns = lax.axis_size("col")
    row_count = lax.axis_size("row")
    all_grads = lax.all_gather(grad_out, "rep", axis=0, tiled=True)
    grad_split = grad_out.reshape(tokens, replicas, quarter)
    partial_value = jnp.einsum(
        "tqk,qdk->td",
        grad_split,
        lax.all_gather(weight_slab, "rep", axis=0, tiled=True),
        preferred_element_type=jnp.float32,
    )
    summed = lax.psum_scatter(partial_value, "col", scatter_dimension=0, tiled=True)
    input_grad = summed.astype(jnp.bfloat16)
    left_part = lax.dot_general(
        grad_out, grad_out, (((1,), (1,)), ((), ())), preferred_element_type=jnp.float32
    )
    left_kernel = (lax.psum(left_part, "col") / FF).astype(jnp.bfloat16)
    right_part = lax.dot_general(
        acts, acts, (((1,), (1,)), ((), ())), preferred_element_type=jnp.float32
    )
    right_kernel = (lax.psum(right_part, "row") / D).astype(jnp.bfloat16)
    all_acts, left_all, right_all = (
        lax.all_gather(acts, "rep", axis=0, tiled=True),
        lax.all_gather(left_kernel, "rep", axis=0, tiled=True),
        lax.all_gather(right_kernel, "rep", axis=0, tiled=True),
    )
    stacked_acts = all_acts.reshape(replicas, tokens, width)
    left_mix = jnp.einsum(
        "pts,psd->ptd",
        left_all.reshape(replicas, tokens, tokens),
        stacked_acts,
        preferred_element_type=jnp.float32,
    ).astype(jnp.bfloat16)
    feature_blocks = width // BLOCK
    left_width = BLOCK // (replicas * columns)
    left_start = (lax.axis_index("rep") * columns + lax.axis_index("col")) * left_width
    acts_blocks = stacked_acts.reshape(replicas, tokens, feature_blocks, BLOCK)
    acts_picked = lax.dynamic_slice_in_dim(acts_blocks, left_start, left_width, 3)
    left_stats = jnp.einsum(
        "ptia,ptib->aib",
        acts_picked,
        left_mix.reshape(replicas, tokens, feature_blocks, BLOCK),
        preferred_element_type=jnp.float32,
    )
    left_stats = left_stats.reshape(left_width, width) / (replicas * tokens)
    stacked_grads = all_grads.reshape(replicas, tokens, hidden)
    right_mix = jnp.einsum(
        "pts,psf->ptf",
        right_all.reshape(replicas, tokens, tokens),
        stacked_grads,
        preferred_element_type=jnp.float32,
    ).astype(jnp.bfloat16)
    hidden_blocks = hidden // BLOCK
    right_width = BLOCK // (replicas * row_count)
    right_start = (lax.axis_index("rep") * row_count + lax.axis_index("row")) * right_width
    grad_blocks = stacked_grads.reshape(replicas, tokens, hidden_blocks, BLOCK)
    grads_picked = lax.dynamic_slice_in_dim(grad_blocks, right_start, right_width, 3)
    right_stats = jnp.einsum(
        "ptia,ptib->aib",
        grads_picked,
        right_mix.reshape(replicas, tokens, hidden_blocks, BLOCK),
        preferred_element_type=jnp.float32,
    )
    right_stats = right_stats.reshape(right_width, hidden) / (replicas * tokens)
    return (input_grad, left_stats, right_stats)


def solution(mesh):
    in_specs = (P("rep", "row"), P("rep", "col"), P("rep", "row", "col"))
    out_specs = (P(("rep", "col"), "row"), P(("rep", "col"), "row"), P(("rep", "row"), "col"))
    return jax.shard_map(body, mesh=mesh, in_specs=in_specs, out_specs=out_specs, check_vma=False)
```

profile of v0, /device:TPU:1, one launch (start us, length us, event | category | flops | bytes accessed | tf_op | source)
XLA Modules:
  0.0 596.2 jit_solution(5223191410952731075)
XLA Ops:
  7.2 0.7 all-gather.4.cloned.1.call-update
  8.3 1.0 fusion.18
  9.4 0.9 fusion.19
  11.6 167.2 %all-gather.4.cloned.1.call-done = bf16[4,2048,768]{2,1,0:T(8,128)(2,1)} async-done(((bf16[1,2048,768]{2,1,0:T(8,128)(2,1)}), bf16[4,2048,768]{2,1,0:T(8,128)(2,1)}) %all-gather.4.cloned.1.call-update) | async-done | bytes 12582928 | tf_op jit(solution)/shard_map/all_gather | solution.py:24
  178.8 9.7 %convolution_bitcast_fusion = f32[128,2048]{1,0:T(8,128)} fusion(bf16[4,2048,768]{2,1,0:T(8,128)(2,1)} %all-gather.4.cloned.1.call-done, bf16[16,4,8,768]{3,2,1,0:T(8,128)(2,1)S(1)} %bitcast.53), kind=kOutput, calls=%fused_computation.2 | convolution fusion | flops 1610612736 | bytes 14417920 | tf_op jit(solution)/shard_map/tqk,qdk->td/dot_general | solution.py:21
  188.5 134.5 %all-reduce.3.cloned.1.call-done = f32[128,128]{1,0:T(8,128)} async-done(((f32[128,128]{1,0:T(8,128)}), f32[128,128]{1,0:T(8,128)}) %all-reduce.3.cloned.1.call-update) | async-done | bytes 65552 | tf_op jit(solution)/shard_map/psum | solution.py:32
  323.0 0.8 multiply_convert_fusion.1
  323.9 18.2 %all_gather.16 = bf16[512,128]{1,0:T(8,128)(2,1)S(1)} all-gather(bf16[128,128]{1,0:T(8,128)(2,1)S(1)} %multiply_convert_fusion.1), channel_id=1, replica_groups=mesh['rep'=4,'row'=8,'col'=16] {'rep'}, dimensions={0}, use_global_device_ids=true | all-gather | bytes 163840 | tf_op jit(solution)/shard_map/all_gather | solution.py:39
  342.1 63.2 %all-reduce.5.cloned.1.call-done = f32[128,128]{1,0:T(8,128)} async-done(((f32[128,128]{1,0:T(8,128)}), f32[128,128]{1,0:T(8,128)}) %all-reduce.5.cloned.1.call-update) | async-done | bytes 65552 | tf_op jit(solution)/shard_map/psum | solution.py:36
  405.3 0.8 multiply_convert_fusion
  406.2 14.4 %all_gather.18 = bf16[512,128]{1,0:T(8,128)(2,1)S(1)} all-gather(bf16[128,128]{1,0:T(8,128)(2,1)S(1)} %multiply_convert_fusion), channel_id=1, replica_groups=mesh['rep'=4,'row'=8,'col'=16] {'rep'}, dimensions={0}, use_global_device_ids=true | all-gather | bytes 163840 | tf_op jit(solution)/shard_map/all_gather | solution.py:40
  420.6 35.6 %all-gather.6.cloned.1.call-done = bf16[512,2048]{1,0:T(8,128)(2,1)} async-done(((bf16[128,2048]{1,0:T(8,128)(2,1)}), bf16[512,2048]{1,0:T(8,128)(2,1)}) %all-gather.6.cloned.1.call-update) | async-done | bytes 2097168 | tf_op jit(solution)/shard_map/all_gather | solution.py:38
  456.2 4.6 reshape_reshape.6
  460.8 1.3 constant_dynamic-slice_fusion.1
  462.1 0.7 convolution_convert_fusion.1
  463.9 48.1 %all-gather.8.cloned.1.call-done = bf16[512,3072]{1,0:T(8,128)(2,1)} async-done(((bf16[128,3072]{1,0:T(8,128)(2,1)}), bf16[512,3072]{1,0:T(8,128)(2,1)}) %all-gather.8.cloned.1.call-update) | async-done | bytes 3145744 | tf_op jit(solution)/shard_map/all_gather | solution.py:19
  511.9 4.5 convolution_convert_fusion
  516.4 4.8 copy.22
  521.2 6.0 %reshape.43 = bf16[4,128,3,1024]{3,2,1,0:T(4,128)(2,1)} reshape(bf16[512,3072]{1,0:T(8,128)(2,1)S(1)} %copy-done) | data formatting | bytes 6291456 | tf_op jit(solution)/shard_map/reshape;reshape | solution.py:71
  527.3 1.4 constant_dynamic-slice_fusion
  528.7 2.9 fusion.4
  531.6 0.8 copy.36
  532.4 55.5 %reduce-scatter.2.cloned.1.call-done = f32[8,2048]{1,0:T(8,128)} async-done(((f32[128,2048]{1,0:T(8,128)}), f32[8,2048]{1,0:T(8,128)}) %reduce-scatter.2.cloned.1.call-update) | async-done | bytes 65552 | tf_op jit(solution)/shard_map/reduce_scatter | solution.py:27
  587.9 1.5 convert_element_type.15
  (23 shorter events, 2.8 us)
Async XLA Ops:
  7.2 1.1 copy-start.1
  7.2 2.2 copy-start.4
  7.2 171.6 %all-gather.4.cloned.1.call-start = ((), (), s32[]{:S(2)}) async-start(), calls=%async_computation.1 | async-start | bytes 15728640 | tf_op jit(solution)/shard_map/all_gather | solution.py:24
  7.2 171.5 %copy-start.2 = (bf16[128,3072]{1,0:T(8,128)(2,1)S(1)}, bf16[128,3072]{1,0:T(8,128)(2,1)}, u32[]{:S(2)}) copy-start(bf16[128,3072]{1,0:T(8,128)(2,1)} %param.4) | copy-start | bytes 2359300
  7.9 315.1 %all-reduce.3.cloned.1.call-start = ((), (), s32[]{:S(2)}) async-start(), calls=%async_computation.3 | async-start | bytes 131072 | tf_op jit(solution)/shard_map/psum | solution.py:32
  9.3 396.0 %all-reduce.5.cloned.1.call-start = ((), (), s32[]{:S(2)}) async-start(), calls=%async_computation.5 | async-start | bytes 131072 | tf_op jit(solution)/shard_map/psum | solution.py:36
  10.3 445.8 %all-gather.6.cloned.1.call-start = ((), (), s32[]{:S(2)}) async-start(), calls=%async_computation.4 | async-start | bytes 2621440 | tf_op jit(solution)/shard_map/all_gather | solution.py:38
  10.9 501.0 %all-gather.8.cloned.1.call-start = ((), (), s32[]{:S(2)}) async-start(), calls=%async_computation.6 | async-start | bytes 3932160 | tf_op jit(solution)/shard_map/all_gather | solution.py:19
  11.5 576.4 %reduce-scatter.2.cloned.1.call-start = ((), (), s32[]{:S(2)}) async-start(), calls=%async_computation.2 | async-start | bytes 1114112 | tf_op jit(solution)/shard_map/reduce_scatter | solution.py:27
  456.2 5.9 copy-start.3
  516.4 4.8 copy-start
Sparse Core Ops, SparseCore 0:
  10.1 168.5 all-gather.3
  182.2 140.7 all-reduce.2
  326.0 79.2 all-reduce.4
  407.3 48.8 all-gather.5
  458.1 53.7 all-gather.7
  514.6 73.2 reduce-scatter.1
where the time goes:
time: 606 us; the launch traced here: 596 us
  waiting for transfers between devices  506 us (83%)
  blocking collectives  32.7 us (5%)
  matrix products  20.1 us (3%)
  local copies, waits for them, and re-layouts  19.9 us (3%)
  between operations  14.2 us (2%)
    all_gather x1, waiting for transfers between devices, body(): lax.all_gather(weight_slab, 'rep', axis=0, tiled=True)  167 us
    psum x1, waiting for transfers between devices, body(): left_kernel = (lax.psum(left_part, 'col') / FF).astype(jnp.bfloat16)  135 us
    psum x1, waiting for transfers between devices, body(): right_kernel = (lax.psum(right_part, 'row') / D).astype(jnp.bfloat16)  63.2 us
    reduce_scatter x1, waiting for transfers between devices, body(): lax.psum_scatter(partial_value, 'col', scatter_dimension=0, tiled=True)  55.5 us
    all_gather x1, waiting for transfers between devices, body(): all_grads = lax.all_gather(grad_out, 'rep', axis=0, tiled=True)  48.1 us
    all_gather x1, waiting for transfers between devices, body(): lax.all_gather(acts, 'rep', axis=0, tiled=True)  35.6 us
    all_gather x1, blocking collectives, body(): lax.all_gather(left_kernel, 'rep', axis=0, tiled=True)  18.2 us
    all_gather x1, blocking collectives, body(): lax.all_gather(right_kernel, 'rep', axis=0, tiled=True)  14.4 us
  transfers between devices with their start and end apart: 6, of which 6 were waited for; matrix products, arithmetic and copies ran while one was open for 7% of the time, Pallas kernels for 0%

commit v1 on v0

v1 whole, which is shorter than its diff:
```python
import functools

import jax
import jax.numpy as jnp
from jax import lax
from jax.experimental import pallas as pl
from jax.experimental.pallas import tpu as pltpu
from jax.sharding import Mesh, PartitionSpec as P

D = 16384
FF = 49152
BLOCK = 1024
TOKENS = 512
NT = (((1,), (1,)), ((), ()))
BF = jnp.bfloat16
F32 = jnp.float32


def stats_kernel(place, total_ref, data_ref, keep_ref, send_ref, *, share, stride, norm):
    rows = 4 * share
    kernel = (total_ref[...] / norm).astype(BF)
    data = data_ref[...]
    mix = jnp.dot(kernel, data, preferred_element_type=F32).astype(BF)
    row = lax.broadcasted_iota(jnp.int32, (rows, BLOCK), 0)
    unit = lax.broadcasted_iota(jnp.int32, (rows, BLOCK), 1)
    peer = row // share
    rep = ((place[0] ^ (peer & 1)) * 2) + (place[1] ^ (peer >> 1))
    wanted = (rep * stride + place[2]) * share + (row % share)
    pick = jnp.where(unit == wanted, 1.0, 0.0).astype(BF)
    picked = lax.dot_general(pick, data, NT, preferred_element_type=F32).astype(BF)
    out = jnp.dot(picked, mix, preferred_element_type=F32) * (1.0 / TOKENS)
    keep_ref[...] = out[: rows // 2]
    send_ref[...] = out[rows // 2 :]


def stats_rows(place, total, data, share, stride, norm):
    tokens, width = data.shape
    half = 2 * share
    shape = jax.ShapeDtypeStruct((half, width), F32)
    spec = pl.BlockSpec((half, BLOCK), lambda j, place: (0, j))
    return pl.pallas_call(
        functools.partial(stats_kernel, share=share, stride=stride, norm=norm),
        out_shape=(shape, shape),
        grid_spec=pltpu.PrefetchScalarGridSpec(
            num_scalar_prefetch=1,
            grid=(width // BLOCK,),
            in_specs=[
                pl.BlockSpec((tokens, tokens), lambda j, place: (0, 0)),
                pl.BlockSpec((tokens, BLOCK), lambda j, place: (0, j)),
            ],
            out_specs=[spec, spec],
        ),
        compiler_params=pltpu.CompilerParams(vmem_limit_bytes=24 * 1024 * 1024),
    )(place, total, data)


def body(acts, grad_out, weight_slab):
    weight = weight_slab[0]
    width = acts.shape[1]
    hidden = grad_out.shape[1]
    quarter = weight.shape[1]
    yh, core, row, yl, xx = (lax.axis_index(n) for n in ("yh", "core", "row", "yl", "x"))
    reps = ("yh", "core")

    def swap(value, dy, dc):
        perm = [(i, i ^ (2 * dy + dc)) for i in range(4)]
        return lax.ppermute(value, reps, perm)

    def piece(dy, dc):
        q = (yh ^ dy) * 2 + (core ^ dc)
        return lax.dynamic_slice_in_dim(grad_out, q * quarter, quarter, 1)

    from_y = swap(piece(1, 0), 1, 0)
    from_yc = swap(piece(1, 1), 1, 1)
    from_c = swap(piece(0, 1), 0, 1)
    own = piece(0, 0)

    left_part = lax.dot_general(grad_out, grad_out, NT, preferred_element_type=F32)
    right_part = lax.dot_general(acts, acts, NT, preferred_element_type=F32)
    left_all = lax.all_to_all(
        jnp.broadcast_to(left_part[None], (16,) + left_part.shape), ("yl", "x"), 0, 0, tiled=True
    )
    left_sum = jnp.sum(left_all, axis=0)
    right_sum = right_part
    for step in (1, 2, 4):
        right_sum = right_sum + lax.ppermute(right_sum, "row", [(i, i ^ step) for i in range(8)])

    def product(tokens):
        return lax.dot_general(tokens, weight, NT, preferred_element_type=F32)

    halves = []
    for near, far in ((own, from_c), (from_y, from_yc)):
        other = swap(product(far), 0, 1)
        both = (product(near) + other).astype(BF)
        both = both.reshape(4, 4, 8, width).transpose(1, 0, 2, 3)
        got = lax.all_to_all(both, "x", 0, 0, tiled=True)
        halves.append(jnp.sum(got.astype(F32), axis=0).astype(BF))
    first = jnp.where(yh == 0, halves[0], halves[1])
    second = jnp.where(yh == 0, halves[1], halves[0])
    chunks = jnp.concatenate([first, second], axis=0)
    got = lax.all_to_all(chunks, ("yh", "yl"), 0, 0, tiled=True)
    input_grad = jnp.sum(got.astype(F32), axis=0).astype(BF)

    def stats(total, data, share, stride, offset, norm):
        place = jnp.stack([yh, core, offset]).astype(jnp.int32)
        keep, send = stats_rows(place, total, data, share, stride, norm)
        both = keep + swap(send, 0, 1)
        far = swap(both[share:].astype(BF), 1, 0)
        return both[:share] + far.astype(F32)

    left_stats = stats(left_sum, acts, 16, 16, yl * 4 + xx, FF)
    right_stats = stats(right_sum, grad_out, 32, 8, row, D)
    return input_grad, left_stats, right_stats


def solution(mesh):
    split = Mesh(mesh.devices.reshape(2, 2, 8, 4, 4), ("yh", "core", "row", "yl", "x"))
    rep, col = ("yh", "core"), ("yl", "x")
    in_specs = (P(rep, "row"), P(rep, col), P(rep, "row", col))
    out_specs = (P(rep + col, "row"), P(rep + col, "row"), P(rep + ("row",), col))
    return jax.shard_map(body, mesh=split, in_specs=in_specs, out_specs=out_specs, check_vma=False)
```

time: 606 us -> 156 us (0.26); the launches traced: 596 us -> 154 us
  waiting for transfers between devices: 506 us -> 37.7 us
  starting transfers between devices: 0.24 us -> 73.3 us
  blocking collectives: 32.7 us -> 0 us
  between operations: 14.2 us -> 0.93 us
  other arithmetic: 3.15 us -> 15.6 us
  local copies, waits for them, and re-layouts: 19.9 us -> 9.42 us
  matrix products: 20.1 us -> 11.9 us
    all_gather x3 -> x0, waiting for transfers between devices: 251 us -> none  [the longest x1 167 us: body(): lax.all_gather(weight_slab, 'rep', axis=0, tiled=True)]
    psum x2 -> x0, waiting for transfers between devices: 198 us -> none  [the longest x1 135 us: body(): left_kernel = (lax.psum(left_part, 'col') / FF).astype(jnp.bfloat16)]
    reduce_scatter x1 -> x0, waiting for transfers between devices: 55.5 us -> none  [body(): lax.psum_scatter(partial_value, 'col', scatter_dimension=0, tiled=True)]
    ppermute x0 -> x12, starting transfers between devices: none -> 55.5 us  [the longest x9 40.4 us: swap(): return lax.ppermute(value, reps, perm)]
    all_gather x2 -> x0, blocking collectives: 32.7 us -> none  [the longest x1 18.2 us: body(): lax.all_gather(left_kernel, 'rep', axis=0, tiled=True)]
    ppermute x0 -> x12, waiting for transfers between devices: none -> 24.3 us  [the longest x9 16.9 us: swap(): return lax.ppermute(value, reps, perm)]
    all_to_all x0 -> x4, starting transfers between devices: none -> 17.8 us  [the longest x2 8.28 us: body(): got = lax.all_to_all(both, 'x', 0, 0, tiled=True)]
    all_to_all x0 -> x4, waiting for transfers between devices: none -> 13.4 us  [the longest x2 11.8 us: body(): got = lax.all_to_all(both, 'x', 0, 0, tiled=True)]
  transfers between devices with their start and end apart: 6 -> 16, of which waited for: 6 -> 11; matrix products, arithmetic and copies ran while one was open for 7% -> 17% of each run, Pallas kernels for 0% -> 4%
where the time goes in v1:
time: 156 us; the launch traced here: 154 us
  starting transfers between devices  73.3 us (47%)
  waiting for transfers between devices  37.7 us (24%)
  other arithmetic  15.6 us (10%)
  matrix products  11.9 us (8%)
  local copies, waits for them, and re-layouts  9.42 us (6%)
  Pallas kernels  5.48 us (4%)
    ppermute x9, starting transfers between devices, swap(): return lax.ppermute(value, reps, perm)  40.4 us
    ppermute x9, waiting for transfers between devices, swap(): return lax.ppermute(value, reps, perm)  16.9 us
    ppermute x3, starting transfers between devices, body(): lax.ppermute(right_sum, 'row', [(i, i ^ step) for i in range(8)])  15.1 us
    all_to_all x2, waiting for transfers between devices, body(): got = lax.all_to_all(both, 'x', 0, 0, tiled=True)  11.8 us
    dot_general x4, matrix products, product(): return lax.dot_general(tokens, weight, NT, preferred_element_type=F32)  8.67 us
    all_to_all x2, starting transfers between devices, body(): got = lax.all_to_all(both, 'x', 0, 0, tiled=True)  8.28 us
    ppermute x3, waiting for transfers between devices, body(): lax.ppermute(right_sum, 'row', [(i, i ^ step) for i in range(8)])  7.41 us
    pallas_call x2, Pallas kernels, stats_rows(): pl.pallas_call(functools.partial(stats_kernel, share=share, stride=stride...  5.48 us
  transfers between devices with their start and end apart: 16, of which 11 were waited for; matrix products, arithmetic and copies ran while one was open for 17% of the time, Pallas kernels for 4%

profile of v1, /device:TPU:1, one launch (start us, length us, event | category | flops | bytes accessed | tf_op | source)
XLA Modules:
  0.0 154.4 jit_solution(11776402335357905155)
XLA Ops:
  2.0 8.8 %collective-permute-start = (bf16[128,768]{1,0:T(8,128)(2,1)S(1)}, bf16[128,768]{1,0:T(8,128)(2,1)S(1)}, u32[]{:S(2)}, u32[]{:S(2)}) collective-permute-start(bf16[128,768]{1,0:T(8,128)(2,1)S(1)} %get-tuple-element.11), channel_id=1, source_target_pairs={{0,128},{128,0},{256,384},{384,256},{1,129},{129,1},{257,385},{385... | collective-permute-start | bytes 589832 | tf_op jit(solution)/shard_map/ppermute | solution.py:67
  11.8 2.1 %fusion.4 = f32[128,2048]{1,0:T(8,128)} fusion(bf16[128,768]{1,0:T(8,128)(2,1)S(1)} %collective-permute-done, bf16[1,2048,768]{2,1,0:T(8,128)(2,1)S(1)} %copy-done), kind=kOutput, calls=%fused_computation.4 | convolution fusion | flops 402653184 | bytes 4390912 | tf_op jit(solution)/shard_map/dot_general | solution.py:89
  14.0 2.3 %collective-permute-start.1 = (f32[128,2048]{1,0:T(8,128)}, f32[128,2048]{1,0:T(8,128)}, u32[]{:S(2)}, u32[]{:S(2)}) collective-permute-start(f32[128,2048]{1,0:T(8,128)} %fusion.4), channel_id=1, source_target_pairs={{0,128},{128,0},{256,384},{384,256},{1,129},{129,1},{257,385},{385... | collective-permute-start | bytes 3145736 | tf_op jit(solution)/shard_map/ppermute | solution.py:67
  18.4 13.1 %collective-permute-done.3 = bf16[128,768]{1,0:T(8,128)(2,1)S(1)} collective-permute-done((bf16[128,768]{1,0:T(8,128)(2,1)S(1)}, bf16[128,768]{1,0:T(8,128)(2,1)S(1)}, u32[]{:S(2)}, u32[]{:S(2)}) %collective-permute-start.3) | collective-permute-done | bytes 196640 | tf_op jit(solution)/shard_map/ppermute | solution.py:67
  31.4 2.1 %fusion = f32[128,2048]{1,0:T(8,128)} fusion(bf16[128,768]{1,0:T(8,128)(2,1)S(1)} %collective-permute-done.3, bf16[1,2048,768]{2,1,0:T(8,128)(2,1)S(1)} %copy-done), kind=kOutput, calls=%fused_computation | convolution fusion | flops 402653184 | bytes 4390912 | tf_op jit(solution)/shard_map/dot_general | solution.py:89
  33.6 2.3 %collective-permute-start.4 = (f32[128,2048]{1,0:T(8,128)}, f32[128,2048]{1,0:T(8,128)}, u32[]{:S(2)}, u32[]{:S(2)}) collective-permute-start(f32[128,2048]{1,0:T(8,128)} %fusion), channel_id=1, source_target_pairs={{0,128},{128,0},{256,384},{384,256},{1,129},{129,1},{257,385},{385... | collective-permute-start | bytes 3145736 | tf_op jit(solution)/shard_map/ppermute | solution.py:67
  35.9 3.6 %collective-permute-start.2 = (bf16[128,768]{1,0:T(8,128)(2,1)S(1)}, bf16[128,768]{1,0:T(8,128)(2,1)S(1)}, u32[]{:S(2)}, u32[]{:S(2)}) collective-permute-start(bf16[128,768]{1,0:T(8,128)(2,1)S(1)} %get-tuple-element.13), channel_id=1, source_target_pairs={{0,256},{128,384},{256,0},{384,128},{1,257},{129,385},{257,1},{385... | collective-permute-start | bytes 589832 | tf_op jit(solution)/shard_map/ppermute | solution.py:67
  43.8 4.1 %all-to-all-start = ((bf16[4,4,8,2048]{3,2,1,0:T(8,128)(2,1)}), bf16[4,4,8,2048]{3,2,1,0:T(8,128)(2,1)}, u32[]{:S(2)}, u32[]{:S(2)}) async-start(bf16[4,4,8,2048]{3,2,1,0:T(8,128)(2,1)} %bitcast.34), calls=%async_computation | async-start | bytes 1048576 | tf_op jit(solution)/shard_map/all_to_all | solution.py:96
  48.2 2.4 %fusion.11 = bf16[128,2048]{1,0:T(8,128)(2,1)S(1)} fusion(f32[128,2048]{1,0:T(8,128)} %collective-permute-done.4, bf16[128,768]{1,0:T(8,128)(2,1)S(1)} %collective-permute-done.2, bf16[1,2048,768]{2,1,0:T(8,128)(2,1)S(1)} %copy-done), kind=kOutput, calls=%fused_computation.9 | convolution fusion | flops 403177472 | bytes 4915200 | tf_op jit(solution)/shard_map/dot_general | solution.py:89
  51.4 5.6 %all-to-all-done = bf16[4,4,8,2048]{3,2,1,0:T(8,128)(2,1)} async-done(((bf16[4,4,8,2048]{3,2,1,0:T(8,128)(2,1)}), bf16[4,4,8,2048]{3,2,1,0:T(8,128)(2,1)}, u32[]{:S(2)}, u32[]{:S(2)}) %all-to-all-start) | async-done | bytes 524320 | tf_op jit(solution)/shard_map/all_to_all | solution.py:96
  57.0 4.1 %all-to-all-start.1 = ((bf16[4,4,8,2048]{3,2,1,0:T(8,128)(2,1)}), bf16[4,4,8,2048]{3,2,1,0:T(8,128)(2,1)}, u32[]{:S(2)}, u32[]{:S(2)}) async-start(bf16[4,4,8,2048]{3,2,1,0:T(8,128)(2,1)} %bitcast.35), calls=%async_computation.1 | async-start | bytes 1048576 | tf_op jit(solution)/shard_map/all_to_all | solution.py:96
  62.9 6.1 %all-to-all-done.1 = bf16[4,4,8,2048]{3,2,1,0:T(8,128)(2,1)} async-done(((bf16[4,4,8,2048]{3,2,1,0:T(8,128)(2,1)}), bf16[4,4,8,2048]{3,2,1,0:T(8,128)(2,1)}, u32[]{:S(2)}, u32[]{:S(2)}) %all-to-all-start.1) | async-done | bytes 524320 | tf_op jit(solution)/shard_map/all_to_all | solution.py:96
  70.1 4.4 %all-to-all-start.3 = ((f32[16,128,128]{2,1,0:T(8,128)}), f32[16,128,128]{2,1,0:T(8,128)}, u32[]{:S(2)}, u32[]{:S(2)}) async-start(f32[16,128,128]{2,1,0:T(8,128)} %broadcast_in_dim.2), calls=%async_computation.3 | async-start | bytes 2097152 | tf_op jit(solution)/shard_map/all_to_all | solution.py:80
  78.1 3.3 %collective-permute-done.7 = f32[128,128]{1,0:T(8,128)S(1)} collective-permute-done((f32[128,128]{1,0:T(8,128)S(1)}, f32[128,128]{1,0:T(8,128)S(1)}, u32[]{:S(2)}, u32[]{:S(2)}) %collective-permute-start.7) | collective-permute-done | bytes 65568 | tf_op jit(solution)/shard_map/ppermute | solution.py:86
  81.4 4.5 %collective-permute-start.8 = (f32[128,128]{1,0:T(8,128)S(1)}, f32[128,128]{1,0:T(8,128)S(1)}, u32[]{:S(2)}, u32[]{:S(2)}) collective-permute-start(f32[128,128]{1,0:T(8,128)S(1)} %add.67), channel_id=1, source_target_pairs={{0,32},{16,48},{32,0},{48,16},{64,96},{80,112},{96,64},{112,80},{1... | collective-permute-start | bytes 196616 | tf_op jit(solution)/shard_map/ppermute | solution.py:86
  88.0 8.5 %collective-permute-start.9 = (f32[128,128]{1,0:T(8,128)S(1)}, f32[128,128]{1,0:T(8,128)S(1)}, u32[]{:S(2)}, u32[]{:S(2)}) collective-permute-start(f32[128,128]{1,0:T(8,128)S(1)} %add.68), channel_id=1, source_target_pairs={{0,64},{16,80},{32,96},{48,112},{64,0},{80,16},{96,32},{112,48},{1... | collective-permute-start | bytes 196616 | tf_op jit(solution)/shard_map/ppermute | solution.py:86
  99.8 3.2 %shard_map.59 = (f32[64,3072]{1,0:T(8,128)S(1)}, f32[64,3072]{1,0:T(8,128)}) custom-call(s32[3]{0:T(128)S(1)} %pad_add_fusion.2.place, f32[128,128]{1,0:T(8,128)S(1)} %add.69.total_ref, bf16[128,3072]{1,0:T(8,128)(2,1)S(1)} %copy-done.1), custom_call_target="tpu_custom_call" | custom-call | tf_op jit(solution)/shard_map/pallas_call | solution.py:41
  103.9 7.5 %collective-permute-start.10 = (f32[64,3072]{1,0:T(8,128)}, f32[64,3072]{1,0:T(8,128)}, u32[]{:S(2)}, u32[]{:S(2)}) collective-permute-start(f32[64,3072]{1,0:T(8,128)} %get-tuple-element.10), channel_id=1, source_target_pairs={{0,128},{128,0},{256,384},{384,256},{1,129},{129,1},{257,385},{385... | collective-permute-start | bytes 2359304 | tf_op jit(solution)/shard_map/ppermute | solution.py:67
  111.5 2.1 %collective-permute-done.10 = f32[64,3072]{1,0:T(8,128)} collective-permute-done((f32[64,3072]{1,0:T(8,128)}, f32[64,3072]{1,0:T(8,128)}, u32[]{:S(2)}, u32[]{:S(2)}) %collective-permute-start.10) | collective-permute-done | bytes 786464 | tf_op jit(solution)/shard_map/ppermute | solution.py:67
  116.7 4.1 %collective-permute-start.11 = (bf16[32,3072]{1,0:T(8,128)(2,1)}, bf16[32,3072]{1,0:T(8,128)(2,1)}, u32[]{:S(2)}, u32[]{:S(2)}) collective-permute-start(bf16[32,3072]{1,0:T(8,128)(2,1)} %slice.26), channel_id=1, source_target_pairs={{0,256},{128,384},{256,0},{384,128},{1,257},{129,385},{257,1},{385... | collective-permute-start | bytes 589832 | tf_op jit(solution)/shard_map/ppermute | solution.py:67
  126.7 2.3 %shard_map.58 = (f32[32,2048]{1,0:T(8,128)S(1)}, f32[32,2048]{1,0:T(8,128)}) custom-call(s32[3]{0:T(128)S(1)} %pad_add_fusion.place, f32[128,128]{1,0:T(8,128)S(1)} %reduce_sum.48.total_ref, bf16[128,2048]{1,0:T(8,128)(2,1)S(1)} %copy-done.2), custom_call_target="tpu_custom_call" | custom-call | tf_op jit(solution)/shard_map/pallas_call | solution.py:41
  128.9 2.5 %collective-permute-start.5 = (f32[32,2048]{1,0:T(8,128)}, f32[32,2048]{1,0:T(8,128)}, u32[]{:S(2)}, u32[]{:S(2)}) collective-permute-start(f32[32,2048]{1,0:T(8,128)} %get-tuple-element.8), channel_id=1, source_target_pairs={{0,128},{128,0},{256,384},{384,256},{1,129},{129,1},{257,385},{385... | collective-permute-start | bytes 786440 | tf_op jit(solution)/shard_map/ppermute | solution.py:67
  133.2 5.1 %all-to-all-start.2 = ((bf16[8,8,2048]{2,1,0:T(8,128)(2,1)}), bf16[8,8,2048]{2,1,0:T(8,128)(2,1)}, u32[]{:S(2)}, u32[]{:S(2)}) async-start(bf16[8,8,2048]{2,1,0:T(8,128)(2,1)} %pad_maximum_fusion), calls=%async_computation.2 | async-start | bytes 524288 | tf_op jit(solution)/shard_map/all_to_all | solution.py:101
  140.0 7.3 %collective-permute-start.6 = (bf16[16,2048]{1,0:T(8,128)(2,1)S(1)}, bf16[16,2048]{1,0:T(8,128)(2,1)S(1)}, u32[]{:S(2)}, u32[]{:S(2)}) collective-permute-start(bf16[16,2048]{1,0:T(8,128)(2,1)S(1)} %slice.27), channel_id=1, source_target_pairs={{0,256},{128,384},{256,0},{384,128},{1,257},{129,385},{257,1},{385... | collective-permute-start | bytes 196616 | tf_op jit(solution)/shard_map/ppermute | solution.py:67
  (50 shorter events, 42.0 us)
Async XLA Ops:
  0.6 11.2 %copy-start = (bf16[1,2048,768]{2,1,0:T(8,128)(2,1)S(1)}, bf16[1,2048,768]{2,1,0:T(8,128)(2,1)}, u32[]{:S(2)}) copy-start(bf16[1,2048,768]{2,1,0:T(8,128)(2,1)} %param.5) | copy-start | bytes 9437188
  2.0 9.8 %collective-permute-start = (bf16[128,768]{1,0:T(8,128)(2,1)S(1)}, bf16[128,768]{1,0:T(8,128)(2,1)S(1)}, u32[]{:S(2)}, u32[]{:S(2)}) collective-permute-start(bf16[128,768]{1,0:T(8,128)(2,1)S(1)} %get-tuple-element.11), channel_id=1, source_target_pairs={{0,128},{128,0},{256,384},{384,256},{1,129},{129,1},{257,385},{385... | collective-permute-start | bytes 589832 | tf_op jit(solution)/shard_map/ppermute | solution.py:67
  14.0 27.6 %collective-permute-start.1 = (f32[128,2048]{1,0:T(8,128)}, f32[128,2048]{1,0:T(8,128)}, u32[]{:S(2)}, u32[]{:S(2)}) collective-permute-start(f32[128,2048]{1,0:T(8,128)} %fusion.4), channel_id=1, source_target_pairs={{0,128},{128,0},{256,384},{384,256},{1,129},{129,1},{257,385},{385... | collective-permute-start | bytes 3145736 | tf_op jit(solution)/shard_map/ppermute | solution.py:67
  16.2 15.2 %collective-permute-start.3 = (bf16[128,768]{1,0:T(8,128)(2,1)S(1)}, bf16[128,768]{1,0:T(8,128)(2,1)S(1)}, u32[]{:S(2)}, u32[]{:S(2)}) collective-permute-start(bf16[128,768]{1,0:T(8,128)(2,1)S(1)} %get-tuple-element.12), channel_id=1, source_target_pairs={{0,384},{128,256},{256,128},{384,0},{1,385},{129,257},{257,129},{3... | collective-permute-start | bytes 589832 | tf_op jit(solution)/shard_map/ppermute | solution.py:67
  33.6 14.6 %collective-permute-start.4 = (f32[128,2048]{1,0:T(8,128)}, f32[128,2048]{1,0:T(8,128)}, u32[]{:S(2)}, u32[]{:S(2)}) collective-permute-start(f32[128,2048]{1,0:T(8,128)} %fusion), channel_id=1, source_target_pairs={{0,128},{128,0},{256,384},{384,256},{1,129},{129,1},{257,385},{385... | collective-permute-start | bytes 3145736 | tf_op jit(solution)/shard_map/ppermute | solution.py:67
  35.9 12.3 %collective-permute-start.2 = (bf16[128,768]{1,0:T(8,128)(2,1)S(1)}, bf16[128,768]{1,0:T(8,128)(2,1)S(1)}, u32[]{:S(2)}, u32[]{:S(2)}) collective-permute-start(bf16[128,768]{1,0:T(8,128)(2,1)S(1)} %get-tuple-element.13), channel_id=1, source_target_pairs={{0,256},{128,384},{256,0},{384,128},{1,257},{129,385},{257,1},{385... | collective-permute-start | bytes 589832 | tf_op jit(solution)/shard_map/ppermute | solution.py:67
  43.8 13.2 %all-to-all-start = ((bf16[4,4,8,2048]{3,2,1,0:T(8,128)(2,1)}), bf16[4,4,8,2048]{3,2,1,0:T(8,128)(2,1)}, u32[]{:S(2)}, u32[]{:S(2)}) async-start(bf16[4,4,8,2048]{3,2,1,0:T(8,128)(2,1)} %bitcast.34), calls=%async_computation | async-start | bytes 1048576 | tf_op jit(solution)/shard_map/all_to_all | solution.py:96
  57.0 12.0 %all-to-all-start.1 = ((bf16[4,4,8,2048]{3,2,1,0:T(8,128)(2,1)}), bf16[4,4,8,2048]{3,2,1,0:T(8,128)(2,1)}, u32[]{:S(2)}, u32[]{:S(2)}) async-start(bf16[4,4,8,2048]{3,2,1,0:T(8,128)(2,1)} %bitcast.35), calls=%async_computation.1 | async-start | bytes 1048576 | tf_op jit(solution)/shard_map/all_to_all | solution.py:96
  70.1 54.2 %all-to-all-start.3 = ((f32[16,128,128]{2,1,0:T(8,128)}), f32[16,128,128]{2,1,0:T(8,128)}, u32[]{:S(2)}, u32[]{:S(2)}) async-start(f32[16,128,128]{2,1,0:T(8,128)} %broadcast_in_dim.2), calls=%async_computation.3 | async-start | bytes 2097152 | tf_op jit(solution)/shard_map/all_to_all | solution.py:80
  76.0 5.4 %collective-permute-start.7 = (f32[128,128]{1,0:T(8,128)S(1)}, f32[128,128]{1,0:T(8,128)S(1)}, u32[]{:S(2)}, u32[]{:S(2)}) collective-permute-start(f32[128,128]{1,0:T(8,128)S(1)} %fusion.17), channel_id=1, source_target_pairs={{0,16},{16,0},{32,48},{48,32},{64,80},{80,64},{96,112},{112,96},{1... | collective-permute-start | bytes 196616 | tf_op jit(solution)/shard_map/ppermute | solution.py:86
  81.4 6.6 %collective-permute-start.8 = (f32[128,128]{1,0:T(8,128)S(1)}, f32[128,128]{1,0:T(8,128)S(1)}, u32[]{:S(2)}, u32[]{:S(2)}) collective-permute-start(f32[128,128]{1,0:T(8,128)S(1)} %add.67), channel_id=1, source_target_pairs={{0,32},{16,48},{32,0},{48,16},{64,96},{80,112},{96,64},{112,80},{1... | collective-permute-start | bytes 196616 | tf_op jit(solution)/shard_map/ppermute | solution.py:86
  88.0 10.7 %collective-permute-start.9 = (f32[128,128]{1,0:T(8,128)S(1)}, f32[128,128]{1,0:T(8,128)S(1)}, u32[]{:S(2)}, u32[]{:S(2)}) collective-permute-start(f32[128,128]{1,0:T(8,128)S(1)} %add.68), channel_id=1, source_target_pairs={{0,64},{16,80},{32,96},{48,112},{64,0},{80,16},{96,32},{112,48},{1... | collective-permute-start | bytes 196616 | tf_op jit(solution)/shard_map/ppermute | solution.py:86
  98.7 1.1 copy-start.1
  103.0 0.9 copy-start.3
  103.9 9.7 %collective-permute-start.10 = (f32[64,3072]{1,0:T(8,128)}, f32[64,3072]{1,0:T(8,128)}, u32[]{:S(2)}, u32[]{:S(2)}) collective-permute-start(f32[64,3072]{1,0:T(8,128)} %get-tuple-element.10), channel_id=1, source_target_pairs={{0,128},{128,0},{256,384},{384,256},{1,129},{129,1},{257,385},{385... | collective-permute-start | bytes 2359304 | tf_op jit(solution)/shard_map/ppermute | solution.py:67
  115.1 0.9 copy-start.4
  116.7 30.7 %collective-permute-start.11 = (bf16[32,3072]{1,0:T(8,128)(2,1)}, bf16[32,3072]{1,0:T(8,128)(2,1)}, u32[]{:S(2)}, u32[]{:S(2)}) collective-permute-start(bf16[32,3072]{1,0:T(8,128)(2,1)} %slice.26), channel_id=1, source_target_pairs={{0,256},{128,384},{256,0},{384,128},{1,257},{129,385},{257,1},{385... | collective-permute-start | bytes 589832 | tf_op jit(solution)/shard_map/ppermute | solution.py:67
  125.6 1.0 copy-start.2
  128.9 9.4 %collective-permute-start.5 = (f32[32,2048]{1,0:T(8,128)}, f32[32,2048]{1,0:T(8,128)}, u32[]{:S(2)}, u32[]{:S(2)}) collective-permute-start(f32[32,2048]{1,0:T(8,128)} %get-tuple-element.8), channel_id=1, source_target_pairs={{0,128},{128,0},{256,384},{384,256},{1,129},{129,1},{257,385},{385... | collective-permute-start | bytes 786440 | tf_op jit(solution)/shard_map/ppermute | solution.py:67
  133.2 17.6 %all-to-all-start.2 = ((bf16[8,8,2048]{2,1,0:T(8,128)(2,1)}), bf16[8,8,2048]{2,1,0:T(8,128)(2,1)}, u32[]{:S(2)}, u32[]{:S(2)}) async-start(bf16[8,8,2048]{2,1,0:T(8,128)(2,1)} %pad_maximum_fusion), calls=%async_computation.2 | async-start | bytes 524288 | tf_op jit(solution)/shard_map/all_to_all | solution.py:101
  139.3 0.7 copy-start.5
  140.0 12.8 %collective-permute-start.6 = (bf16[16,2048]{1,0:T(8,128)(2,1)S(1)}, bf16[16,2048]{1,0:T(8,128)(2,1)S(1)}, u32[]{:S(2)}, u32[]{:S(2)}) collective-permute-start(bf16[16,2048]{1,0:T(8,128)(2,1)S(1)} %slice.27), channel_id=1, source_target_pairs={{0,256},{128,384},{256,0},{384,128},{1,257},{129,385},{257,1},{385... | collective-permute-start | bytes 196616 | tf_op jit(solution)/shard_map/ppermute | solution.py:67

commit v2 on v1

v2 whole, which is shorter than its diff:
```python
import functools

import jax
import jax.numpy as jnp
from jax import lax
from jax.experimental import pallas as pl
from jax.experimental.pallas import tpu as pltpu
from jax.sharding import Mesh, PartitionSpec as P

D = 16384
FF = 49152
BLOCK = 1024
TOKENS = 512
NT = (((1,), (1,)), ((), ()))
BF = jnp.bfloat16
F32 = jnp.float32
MB = 1024 * 1024


def params(mb):
    return pltpu.CompilerParams(vmem_limit_bytes=mb * MB)


def cost(flops, moved):
    return pl.CostEstimate(flops=flops, bytes_accessed=moved, transcendentals=0)


def prepare_kernel(place, acts_hbm, grads_hbm, own_ref, other_ref, direct_ref, share_ref, left_ref, right_ref, acts_ref, grads_ref, sems):
    quarter = own_ref.shape[1]
    rows = share_ref.shape[0]
    chunk = BLOCK

    def lanes(y, c):
        q = y * 2 + c
        return pl.ds(pl.multiple_of(q * quarter, quarter), quarter)

    turn = pl.ds(pl.multiple_of(place[2] * rows, rows), rows)
    yh, core = place[0], place[1]
    pieces = [
        (grads_hbm.at[turn, lanes(1 - yh, 1 - core)], share_ref),
        (grads_hbm.at[:, lanes(1 - yh, core)], direct_ref),
        (grads_hbm.at[:, lanes(yh, core)], own_ref),
        (grads_hbm.at[:, lanes(yh, 1 - core)], other_ref),
    ]
    copies = [pltpu.make_async_copy(grads_hbm, grads_ref, sems.at[0]), pltpu.make_async_copy(acts_hbm, acts_ref, sems.at[1])]
    copies += [pltpu.make_async_copy(s, d, sems.at[2 + i]) for i, (s, d) in enumerate(pieces)]
    for copy in copies:
        copy.start()
    copies[0].wait()
    left = lax.dot_general(grads_ref[turn, :], grads_ref[...], NT, preferred_element_type=F32)
    for i in range(left_ref.shape[0]):
        left_ref[i] = left
    copies[1].wait()
    acts = acts_ref[...]
    right = lax.dot_general(acts, acts, NT, preferred_element_type=F32).astype(BF)
    for i in range(right.shape[0] // rows):
        right_ref[:, i * 128 : i * 128 + 128] = right[i * rows : i * rows + rows]
    for copy in copies[2:]:
        copy.wait()


def prepare(place, acts, grads, cols, rows):
    tokens, hidden = grads.shape
    quarter = hidden // 4
    share = tokens // rows
    piece = jax.ShapeDtypeStruct((tokens, quarter), BF)
    return pl.pallas_call(
        prepare_kernel,
        out_shape=(
            piece,
            piece,
            piece,
            jax.ShapeDtypeStruct((share, quarter), BF),
            jax.ShapeDtypeStruct((cols, share, tokens), F32),
            jax.ShapeDtypeStruct((share, rows * tokens), BF),
        ),
        in_specs=[
            pl.BlockSpec(memory_space=pltpu.SMEM),
            pl.BlockSpec(memory_space=pltpu.HBM),
            pl.BlockSpec(memory_space=pltpu.HBM),
        ],
        out_specs=[pl.BlockSpec(memory_space=pltpu.VMEM)] * 6,
        scratch_shapes=[pltpu.VMEM(acts.shape, BF), pltpu.VMEM(grads.shape, BF), pltpu.SemaphoreType.DMA((6,))],
        compiler_params=params(56),
        cost_estimate=cost(2 * tokens * tokens * (hidden + acts.shape[1]), 3 * MB),
    )(place, acts, grads)


def pack_kernel(left_ref, right_ref, share_ref, out_ref):
    quarter = share_ref.shape[1]
    products = right_ref.shape[1]
    left = left_ref[0]
    for i in range(1, left_ref.shape[0]):
        left = left + left_ref[i]
    left = (left / FF).astype(BF)
    for z in range(out_ref.shape[0]):
        out_ref[z, :, :quarter] = share_ref[...]
        out_ref[z, :, quarter : quarter + products] = right_ref[...]
        out_ref[z, :, quarter + products :] = left


def pack(left, right, share, rows):
    width = share.shape[1] + right.shape[1] + left.shape[2]
    vmem = pl.BlockSpec(memory_space=pltpu.VMEM)
    return pl.pallas_call(
        pack_kernel,
        out_shape=jax.ShapeDtypeStruct((rows, share.shape[0], width), BF),
        in_specs=[vmem] * 3,
        out_specs=vmem,
        compiler_params=params(16),
        cost_estimate=cost(MB, MB),
    )(left, right, share)


def product_kernel(place, own_ref, other_ref, near_lo, near_hi, far_lo, far_hi, *rest):
    outs, low, high = rest[:4], rest[4], rest[5]
    own = own_ref[...]
    other = other_ref[...].reshape(own.shape)

    def dot(near, far):
        return lax.dot_general(own, near[...], NT, preferred_element_type=F32) + lax.dot_general(
            other, far[...], NT, preferred_element_type=F32
        )

    low[...] = dot(near_lo, far_lo)
    high[...] = dot(near_hi, far_hi)
    for r in range(4):
        for y in range(4):
            rows = pl.ds(pl.multiple_of((y * 4 + (place[4] ^ r)) * 8, 8), 8)
            pair = jnp.concatenate([low[rows, :], high[rows, :]], axis=0)
            outs[r][y * 16 : y * 16 + 16, :] = pair.astype(BF)


def product(place, own, other, weight, weight_far):
    count = own.shape[0]
    features, quarter = weight.shape
    half = features // 2
    step = 256
    steps = half // step
    low = pl.BlockSpec((step, quarter), lambda j, place: (j, 0))
    high = pl.BlockSpec((step, quarter), lambda j, place: (j + steps, 0))
    if other.ndim == 3:
        second = pl.BlockSpec(other.shape[:2] + (quarter,), lambda j, place: (0, 0, 0))
    else:
        second = pl.BlockSpec((count, quarter), lambda j, place: (0, 0))
    shape = jax.ShapeDtypeStruct((count // 2, half), BF)
    return pl.pallas_call(
        product_kernel,
        out_shape=(shape,) * 4,
        grid_spec=pltpu.PrefetchScalarGridSpec(
            num_scalar_prefetch=1,
            grid=(steps,),
            in_specs=[pl.BlockSpec((count, quarter), lambda j, place: (0, 0)), second, low, high, low, high],
            out_specs=[pl.BlockSpec((count // 2, step), lambda j, place: (0, j))] * 4,
            scratch_shapes=[pltpu.VMEM((count, step), F32)] * 2,
        ),
        compiler_params=params(16),
        cost_estimate=cost(4 * count * features * quarter, 7 * MB),
    )(place, own, other, weight, weight, weight_far, weight_far)


def x_sum_kernel(place, *refs):
    out_ref = refs[-1]

    def total(parts):
        value = parts[0][...].astype(F32)
        for part in parts[1:]:
            value = value + part[...].astype(F32)
        return value.astype(BF)

    out_ref[place[0]] = total(refs[:4])
    out_ref[1 - place[0]] = total(refs[4:8])


def x_sum(place, near, far):
    rows, width = near[0].shape
    vmem = pl.BlockSpec(memory_space=pltpu.VMEM)
    return pl.pallas_call(
        x_sum_kernel,
        out_shape=jax.ShapeDtypeStruct((2, rows, width), BF),
        in_specs=[pl.BlockSpec(memory_space=pltpu.SMEM)] + [vmem] * 8,
        out_specs=vmem,
        compiler_params=params(16),
        cost_estimate=cost(8 * rows * width, 2 * MB),
    )(place, *near, *far)


def y_sum_kernel(got_ref, out_ref):
    value = got_ref[0].astype(F32)
    for i in range(1, got_ref.shape[0]):
        value = value + got_ref[i].astype(F32)
    out_ref[...] = jnp.concatenate([value[:8], value[8:]], axis=1).astype(BF)


def y_sum(got):
    width = got.shape[2]
    return pl.pallas_call(
        y_sum_kernel,
        out_shape=jax.ShapeDtypeStruct((8, 2 * width), BF),
        in_specs=[pl.BlockSpec(memory_space=pltpu.VMEM)],
        out_specs=pl.BlockSpec(memory_space=pltpu.VMEM),
        compiler_params=params(16),
        cost_estimate=cost(128 * width, MB // 2),
    )(got)


def picker(place, offset, share, stride):
    shape = (4 * share, BLOCK)
    row = lax.broadcasted_iota(jnp.int32, shape, 0)
    unit = lax.broadcasted_iota(jnp.int32, shape, 1)
    peer = row // share
    rep = (place[0] ^ (peer & 1)) * 2 + (place[1] ^ (peer >> 1))
    wanted = (rep * stride + offset) * share + (row % share)
    return jnp.where(unit == wanted, 1.0, 0.0).astype(BF)


def stats_kernel(place, got_ref, acts_hbm, grads_hbm, keep_ref, send_ref, acts_ref, grads_ref, sems):
    hidden = grads_ref.shape[1]
    width = acts_ref.shape[1]
    tokens = acts_ref.shape[0]
    copies = []
    for j in range((hidden + width) // BLOCK):
        source, target, at = (grads_hbm, grads_ref, j) if j < hidden // BLOCK else (acts_hbm, acts_ref, j - hidden // BLOCK)
        lanes = slice(at * BLOCK, (at + 1) * BLOCK)
        copies.append(pltpu.make_async_copy(source.at[:, lanes], target.at[:, lanes], sems.at[j]))
        copies[-1].start()

    def rows(pick, token_kernel, data):
        mix = jnp.dot(token_kernel, data, preferred_element_type=F32).astype(BF)
        picked = lax.dot_general(pick, data, NT, preferred_element_type=F32).astype(BF)
        return jnp.dot(picked, mix, preferred_element_type=F32) * (1.0 / TOKENS)

    count, share, total = got_ref.shape
    products = slice(total - tokens - count * tokens, total - tokens)
    right = got_ref[0, :, products].astype(F32)
    for z in range(1, count):
        right = right + got_ref[z, :, products].astype(F32)
    right = jnp.concatenate([right[:, i * tokens : (i + 1) * tokens] for i in range(count)], axis=0)
    right = (right / D).astype(BF)
    pick = picker(place, place[2], 32, 8)
    for j in range(hidden // BLOCK):
        lanes = slice(j * BLOCK, (j + 1) * BLOCK)
        copies[j].wait()
        out = rows(pick, right, grads_ref[:, lanes])
        keep_ref[:, lanes] = out[:64]
        send_ref[:, lanes] = out[64:]
    left = jnp.concatenate([got_ref[z, :, total - tokens :] for z in range(count)], axis=0)
    pick = picker(place, place[3], 16, 16)
    for j in range(width // BLOCK):
        copies[hidden // BLOCK + j].wait()
        out = rows(pick, left, acts_ref[:, j * BLOCK : (j + 1) * BLOCK])
        for dy in range(2):
            at = slice(dy * 32 + j * 16, dy * 32 + j * 16 + 16)
            keep_ref[at, hidden:] = out[dy * 16 : dy * 16 + 16]
            send_ref[at, hidden:] = out[32 + dy * 16 : 32 + dy * 16 + 16]


def stats(place, got, acts, grads):
    shape = jax.ShapeDtypeStruct((64, grads.shape[1] + BLOCK), F32)
    vmem = pl.BlockSpec(memory_space=pltpu.VMEM)
    hbm = pl.BlockSpec(memory_space=pltpu.HBM)
    return pl.pallas_call(
        stats_kernel,
        out_shape=(shape, shape),
        in_specs=[pl.BlockSpec(memory_space=pltpu.SMEM), vmem, hbm, hbm],
        out_specs=[vmem, vmem],
        scratch_shapes=[
            pltpu.VMEM(acts.shape, BF),
            pltpu.VMEM(grads.shape, BF),
            pltpu.SemaphoreType.DMA(((acts.shape[1] + grads.shape[1]) // BLOCK,)),
        ],
        compiler_params=params(16),
        cost_estimate=cost(1000 * MB, 5 * MB),
    )(place, got, acts, grads)


def core_sum_kernel(keep_ref, got_ref, near_ref, far_ref):
    half = near_ref.shape[0]
    near_ref[...] = keep_ref[:half] + got_ref[:half]
    far_ref[...] = (keep_ref[half:] + got_ref[half:]).astype(BF)


def core_sum(keep, got):
    rows, width = keep.shape
    vmem = pl.BlockSpec(memory_space=pltpu.VMEM)
    return pl.pallas_call(
        core_sum_kernel,
        out_shape=(
            jax.ShapeDtypeStruct((rows // 2, width), F32),
            jax.ShapeDtypeStruct((rows // 2, width), BF),
        ),
        in_specs=[vmem, vmem],
        out_specs=[vmem, vmem],
        compiler_params=params(16),
        cost_estimate=cost(rows * width, 3 * MB),
    )(keep, got)


def last_sum_kernel(near_ref, far_ref, left_ref, right_ref):
    hidden = right_ref.shape[1]
    right_ref[...] = near_ref[:, :hidden] + far_ref[:, :hidden].astype(F32)
    for j in range(left_ref.shape[1] // BLOCK):
        rows = slice(j * 16, j * 16 + 16)
        left_ref[:, j * BLOCK : (j + 1) * BLOCK] = near_ref[rows, hidden:] + far_ref[rows, hidden:].astype(F32)


def last_sum(near, far, hidden, width):
    vmem = pl.BlockSpec(memory_space=pltpu.VMEM)
    return pl.pallas_call(
        last_sum_kernel,
        out_shape=(
            jax.ShapeDtypeStruct((16, width), F32),
            jax.ShapeDtypeStruct((32, hidden), F32),
        ),
        in_specs=[vmem, vmem],
        out_specs=[vmem, vmem],
        compiler_params=params(16),
        cost_estimate=cost(32 * 4096, 2 * MB),
    )(near, far)


def body(acts, grad_out, weight_slab):
    weight = weight_slab[0]
    width = acts.shape[1]
    hidden = grad_out.shape[1]
    yh, core, row, yl, xx = (lax.axis_index(n) for n in ("yh", "core", "row", "yl", "x"))
    place = jnp.stack([yh, core, row, yl * 4 + xx, xx]).astype(jnp.int32)

    def swap(value, axis):
        return lax.ppermute(value, axis, [(0, 1), (1, 0)])

    def to_x_peers(parts):
        return [parts[0]] + [
            lax.ppermute(parts[r], "x", [(i, i ^ r) for i in range(4)]) for r in (2, 1, 3)
        ]

    own, other, direct, share, left_part, right_part = prepare(place, acts, grad_out, 16, 8)
    share = swap(share, "yh")
    left_part, weight, direct = lax.optimization_barrier((left_part, weight, direct))
    left_rows = lax.all_to_all(left_part, ("yl", "x"), 0, 0, tiled=True)
    direct = swap(direct, "yh")
    weight_far = swap(weight, "core")

    packed = pack(left_rows, right_part, share, 8)
    got = lax.all_to_all(packed, "row", 0, 0, tiled=True)

    near = to_x_peers(product(place, own, other, weight, weight_far))

    keep, send = stats(place, got, acts, grad_out)
    near_rows, far_rows = core_sum(keep, swap(send, "core"))
    far_rows = swap(far_rows, "yh")

    far = to_x_peers(product(place, direct, got, weight, weight_far))
    chunks = x_sum(place, near, far)
    chunks = chunks.reshape(8, -1, chunks.shape[2])
    input_grad = y_sum(lax.all_to_all(chunks, ("yh", "yl"), 0, 0, tiled=True))

    left_stats, right_stats = last_sum(near_rows, far_rows, hidden, width)
    return input_grad, left_stats, right_stats


def solution(mesh):
    split = Mesh(mesh.devices.reshape(2, 2, 8, 4, 4), ("yh", "core", "row", "yl", "x"))
    rep, col = ("yh", "core"), ("yl", "x")
    in_specs = (P(rep, "row"), P(rep, col), P(rep, "row", col))
    out_specs = (P(rep + col, "row"), P(rep + col, "row"), P(rep + ("row",), col))
    return jax.shard_map(body, mesh=split, in_specs=in_specs, out_specs=out_specs, check_vma=False)
```

time: 156 us -> 130 us (0.83)
  blocking collectives: 0 us -> 22.8 us
  starting transfers between devices: 73.3 us -> 55 us
  Pallas kernels: 5.48 us -> 22.4 us
  other arithmetic: 15.6 us -> 0 us
  waiting for transfers between devices: 37.7 us -> 23.5 us
  matrix products: 11.9 us -> 0 us
  local copies, waits for them, and re-layouts: 9.42 us -> 4.86 us
    all_to_all x0 -> x1, blocking collectives: none -> 22.8 us  [body(): got = lax.all_to_all(packed, 'row', 0, 0, tiled=True)]
    pallas_call x2 -> x9, Pallas kernels: 5.48 us -> 22.4 us  [the longest x2 9.94 us: product(): pl.pallas_call(product_kernel, out_shape=(shape,) * 4, grid_spec=pltpu.Pr...]
    all_to_all x4 -> x2, waiting for transfers between devices: 13.4 us -> 0.01 us  [the longest x1 0.01 us: body(): input_grad = y_sum(lax.all_to_all(chunks, ('yh', 'yl'), 0, 0, tiled=True))]
    dot_general x6 -> x0, matrix products: 11.9 us -> none  [the longest x4 8.67 us: product(): return lax.dot_general(tokens, weight, NT, preferred_element_type=F32)]
    all_to_all x4 -> x2, starting transfers between devices: 17.8 us -> 7.76 us  [the longest x1 4.24 us: body(): input_grad = y_sum(lax.all_to_all(chunks, ('yh', 'yl'), 0, 0, tiled=True))]
    ppermute x12 -> x11, starting transfers between devices: 55.5 us -> 47.3 us  [the longest x5 29.1 us: swap(): return lax.ppermute(value, axis, [(0, 1), (1, 0)])]
    reduce_sum x4 -> x0, other arithmetic: 6.51 us -> none  [the longest x2 3.61 us: body(): halves.append(jnp.sum(got.astype(F32), axis=0).astype(BF))]
    add x7 -> x0, other arithmetic: 5.86 us -> none  [the longest x2 3.4 us: stats(): return both[:share] + far.astype(F32)]
  transfers between devices with their start and end apart: 16 -> 13, of which waited for: 11 -> 4; matrix products, arithmetic and copies ran while one was open for 17% -> 0% of each run, Pallas kernels for 4% -> 14%
where the time goes in v2:
time: 130 us
  starting transfers between devices  55 us (42%)
  waiting for transfers between devices  23.5 us (18%)
  blocking collectives  22.8 us (18%)
  Pallas kernels  22.4 us (17%)
  local copies, waits for them, and re-layouts  4.86 us (4%)
    ppermute x5, starting transfers between devices, swap(): return lax.ppermute(value, axis, [(0, 1), (1, 0)])  29.1 us
    all_to_all x1, blocking collectives, body(): got = lax.all_to_all(packed, 'row', 0, 0, tiled=True)  22.8 us
    ppermute x5, waiting for transfers between devices, swap(): return lax.ppermute(value, axis, [(0, 1), (1, 0)])  19.1 us
    ppermute x6, starting transfers between devices, to_x_peers(): lax.ppermute(parts[r], 'x', [(i, i ^ r) for i in range(4)])  18.2 us
    pallas_call x2, Pallas kernels, product(): pl.pallas_call(product_kernel, out_shape=(shape,) * 4, grid_spec=pltpu.Pr...  9.94 us
    pallas_call x1, Pallas kernels, stats(): pl.pallas_call(stats_kernel, out_shape=(shape, shape), in_specs=[pl.Block...  4.53 us
    ppermute x6, waiting for transfers between devices, to_x_peers(): lax.ppermute(parts[r], 'x', [(i, i ^ r) for i in range(4)])  4.39 us
    all_to_all x1, starting transfers between devices, body(): input_grad = y_sum(lax.all_to_all(chunks, ('yh', 'yl'), 0, 0, tiled=True))  4.24 us
  transfers between devices with their start and end apart: 13, of which 4 were waited for; matrix products, arithmetic and copies ran while one was open for 0% of the time, Pallas kernels for 14%

profile of v2, /device:TPU:1, one launch (start us, length us, event | category | flops | bytes accessed | tf_op | source)
XLA Modules:
  0.0 129.5 jit_solution(5553454337265965825)
XLA Ops:
  1.3 3.7 %shard_map.58 = (bf16[128,768]{1,0:T(8,128)(2,1)}, bf16[128,768]{1,0:T(8,128)(2,1)}, bf16[128,768]{1,0:T(8,128)(2,1)}, bf16[16,768]{1,0:T(8,128)(2,1)}, f32[16,1...) custom-call(s32[5]{0:T(128)} %stack.23.place, bf16[128,2048]{1,0:T(8,128)(2,1)} %acts_hbm.3, bf16[128,3072]{1,0:T(8,128)(2,1)} %grads_hbm.3), custom_call_target="tpu_custom_call" | custom-call | flops 167772160 | bytes 3145728 | tf_op jit(solution)/shard_map/pallas_call | solution.py:67
  5.0 9.1 %collective-permute-start = (bf16[2048,768]{1,0:T(8,128)(2,1)}, bf16[2048,768]{1,0:T(8,128)(2,1)}, u32[]{:S(2)}, u32[]{:S(2)}) collective-permute-start(bf16[2048,768]{1,0:T(8,128)(2,1)} %bitcast.7), channel_id=1, source_target_pairs={{0,128},{128,0},{1,129},{129,1},{2,130},{130,2},{3,131},{131,3},{4... | collective-permute-start | bytes 9437192 | tf_op jit(solution)/shard_map/ppermute | solution.py:330
  14.1 3.5 %all-to-all-start = ((f32[16,16,128]{2,1,0:T(8,128)}), f32[16,16,128]{2,1,0:T(8,128)S(1)}, u32[]{:S(2)}, u32[]{:S(2)}) async-start(f32[16,16,128]{2,1,0:T(8,128)} %get-tuple-element.36), calls=%async_computation | async-start | bytes 262144 | tf_op jit(solution)/shard_map/all_to_all | solution.py:340
  17.6 3.0 %collective-permute-start.5 = (bf16[16,768]{1,0:T(8,128)(2,1)}, bf16[16,768]{1,0:T(8,128)(2,1)S(1)}, u32[]{:S(2)}, u32[]{:S(2)}) collective-permute-start(bf16[16,768]{1,0:T(8,128)(2,1)} %get-tuple-element.38), channel_id=1, source_target_pairs={{0,256},{256,0},{1,257},{257,1},{2,258},{258,2},{3,259},{259,3},{4... | collective-permute-start | bytes 73736 | tf_op jit(solution)/shard_map/ppermute | solution.py:330
  20.6 5.9 %collective-permute-done.5.share_ref = bf16[16,768]{1,0:T(8,128)(2,1)S(1)} collective-permute-done((bf16[16,768]{1,0:T(8,128)(2,1)}, bf16[16,768]{1,0:T(8,128)(2,1)S(1)}, u32[]{:S(2)}, u32[]{:S(2)}) %collective-permute-start.5) | collective-permute-done | bytes 24608 | tf_op jit(solution)/shard_map/ppermute | solution.py:330
  27.4 22.8 %all_to_all.15.other_ref.got_ref = bf16[8,16,1920]{2,1,0:T(8,128)(2,1)S(1)} all-to-all(bf16[8,16,1920]{2,1,0:T(8,128)(2,1)S(1)} %shard_map.60), channel_id=1, replica_groups=mesh['yh'=2,'core'=2,'row'=8,'yl'=4,'x'=4] {'row'}, dimensions={0} | all-to-all | bytes 983040 | tf_op jit(solution)/shard_map/all_to_all | solution.py:345
  52.4 4.5 %shard_map.64 = (f32[64,4096]{1,0:T(8,128)S(1)}, f32[64,4096]{1,0:T(8,128)}) custom-call(s32[5]{0:T(128)S(1)} %copy-done.8, bf16[8,16,1920]{2,1,0:T(8,128)(2,1)S(1)} %all_to_all.15.other_ref.got_ref, bf16[128,2048]{1,0:T(8,128)(2,1)S(1)} %copy-done.4, bf16[128,3072]{1,0:T(8,128)(2,1)S(1)} %copy-done.3), custom_call_target="tpu_custom_call" | custom-call | flops 1048576000 | bytes 5242880 | tf_op jit(solution)/shard_map/pallas_call | solution.py:262
  56.9 4.9 %collective-permute-start.9 = (f32[64,4096]{1,0:T(8,128)}, f32[64,4096]{1,0:T(8,128)}, u32[]{:S(2)}, u32[]{:S(2)}) collective-permute-start(f32[64,4096]{1,0:T(8,128)} %get-tuple-element.44), channel_id=1, source_target_pairs={{0,128},{128,0},{1,129},{129,1},{2,130},{130,2},{3,131},{131,3},{4... | collective-permute-start | bytes 3145736 | tf_op jit(solution)/shard_map/ppermute | solution.py:330
  61.9 4.8 %collective-permute-start.4 = (bf16[128,768]{1,0:T(8,128)(2,1)S(1)}, bf16[128,768]{1,0:T(8,128)(2,1)S(1)}, u32[]{:S(2)}, u32[]{:S(2)}) collective-permute-start(bf16[128,768]{1,0:T(8,128)(2,1)S(1)} %copy-done.9), channel_id=1, source_target_pairs={{0,256},{256,0},{1,257},{257,1},{2,258},{258,2},{3,259},{259,3},{4... | collective-permute-start | bytes 589832 | tf_op jit(solution)/shard_map/ppermute | solution.py:330
  66.7 5.0 %shard_map.59 = (bf16[64,1024]{1,0:T(8,128)(2,1)S(1)}, bf16[64,1024]{1,0:T(8,128)(2,1)S(1)}, bf16[64,1024]{1,0:T(8,128)(2,1)S(1)}, bf16[64,1024]{1,0:T(8,128)(2,1)S(1)}) custom-call(s32[5]{0:T(128)S(1)} %copy-done.8, bf16[128,768]{1,0:T(8,128)(2,1)S(1)} %copy-done.5, bf16[128,768]{1,0:T(8,128)(2,1)S(1)} %copy-done.6, bf16[2048,768]{1,0:T(8,128)(2,1)S(1)} %bitcast.8, ...), custom_call_target="tpu_custom_call" | custom-call | flops 805306368 | bytes 7340032 | tf_op jit(solution)/shard_map/pallas_call | solution.py:147
  71.7 4.5 %collective-permute-start.1 = (bf16[64,1024]{1,0:T(8,128)(2,1)S(1)}, bf16[64,1024]{1,0:T(8,128)(2,1)S(1)}, u32[]{:S(2)}, u32[]{:S(2)}) collective-permute-start(bf16[64,1024]{1,0:T(8,128)(2,1)S(1)} %get-tuple-element.32), channel_id=1, source_target_pairs={{0,2},{1,3},{2,0},{3,1},{4,6},{5,7},{6,4},{7,5},{8,10},{9,11},{10,... | collective-permute-start | bytes 393224 | tf_op jit(solution)/shard_map/ppermute | solution.py:334
  76.2 2.2 %collective-permute-start.2 = (bf16[64,1024]{1,0:T(8,128)(2,1)S(1)}, bf16[64,1024]{1,0:T(8,128)(2,1)S(1)}, u32[]{:S(2)}, u32[]{:S(2)}) collective-permute-start(bf16[64,1024]{1,0:T(8,128)(2,1)S(1)} %get-tuple-element.33), channel_id=1, source_target_pairs={{0,1},{1,0},{2,3},{3,2},{4,5},{5,4},{6,7},{7,6},{8,9},{9,8},{10,11... | collective-permute-start | bytes 393224 | tf_op jit(solution)/shard_map/ppermute | solution.py:334
  78.4 2.5 %collective-permute-start.3 = (bf16[64,1024]{1,0:T(8,128)(2,1)S(1)}, bf16[64,1024]{1,0:T(8,128)(2,1)S(1)}, u32[]{:S(2)}, u32[]{:S(2)}) collective-permute-start(bf16[64,1024]{1,0:T(8,128)(2,1)S(1)} %get-tuple-element.34), channel_id=1, source_target_pairs={{0,3},{1,2},{2,1},{3,0},{4,7},{5,6},{6,5},{7,4},{8,11},{9,10},{10,... | collective-permute-start | bytes 393224 | tf_op jit(solution)/shard_map/ppermute | solution.py:334
  80.9 5.0 %shard_map.61 = (bf16[64,1024]{1,0:T(8,128)(2,1)S(1)}, bf16[64,1024]{1,0:T(8,128)(2,1)S(1)}, bf16[64,1024]{1,0:T(8,128)(2,1)S(1)}, bf16[64,1024]{1,0:T(8,128)(2,1)S(1)}) custom-call(s32[5]{0:T(128)S(1)} %copy-done.8, bf16[128,768]{1,0:T(8,128)(2,1)S(1)} %collective-permute-done.4.own_ref, bf16[8,16,1920]{2,1,0:T(8,128)(2,1)S(1)} %all_to_all.15.other_ref.got_ref, ...), custom_call_target="tpu_custom_call" | custom-call | flops 805306368 | bytes 7340032 | tf_op jit(solution)/shard_map/pallas_call | solution.py:147
  85.9 4.3 %collective-permute-start.6 = (bf16[64,1024]{1,0:T(8,128)(2,1)S(1)}, bf16[64,1024]{1,0:T(8,128)(2,1)S(1)}, u32[]{:S(2)}, u32[]{:S(2)}) collective-permute-start(bf16[64,1024]{1,0:T(8,128)(2,1)S(1)} %get-tuple-element.40), channel_id=1, source_target_pairs={{0,2},{1,3},{2,0},{3,1},{4,6},{5,7},{6,4},{7,5},{8,10},{9,11},{10,... | collective-permute-start | bytes 393224 | tf_op jit(solution)/shard_map/ppermute | solution.py:334
  90.2 2.2 %collective-permute-start.7 = (bf16[64,1024]{1,0:T(8,128)(2,1)S(1)}, bf16[64,1024]{1,0:T(8,128)(2,1)S(1)}, u32[]{:S(2)}, u32[]{:S(2)}) collective-permute-start(bf16[64,1024]{1,0:T(8,128)(2,1)S(1)} %get-tuple-element.41), channel_id=1, source_target_pairs={{0,1},{1,0},{2,3},{3,2},{4,5},{5,4},{6,7},{7,6},{8,9},{9,8},{10,11... | collective-permute-start | bytes 393224 | tf_op jit(solution)/shard_map/ppermute | solution.py:334
  92.4 2.5 %collective-permute-start.8 = (bf16[64,1024]{1,0:T(8,128)(2,1)S(1)}, bf16[64,1024]{1,0:T(8,128)(2,1)S(1)}, u32[]{:S(2)}, u32[]{:S(2)}) collective-permute-start(bf16[64,1024]{1,0:T(8,128)(2,1)S(1)} %get-tuple-element.42), channel_id=1, source_target_pairs={{0,3},{1,2},{2,1},{3,0},{4,7},{5,6},{6,5},{7,4},{8,11},{9,10},{10,... | collective-permute-start | bytes 393224 | tf_op jit(solution)/shard_map/ppermute | solution.py:334
  95.9 3.4 %collective-permute-done.8.refs_7_ = bf16[64,1024]{1,0:T(8,128)(2,1)S(1)} collective-permute-done((bf16[64,1024]{1,0:T(8,128)(2,1)S(1)}, bf16[64,1024]{1,0:T(8,128)(2,1)S(1)}, u32[]{:S(2)}, u32[]{:S(2)}) %collective-permute-start.8) | collective-permute-done | bytes 131104 | tf_op jit(solution)/shard_map/ppermute | solution.py:334
  99.4 1.4 %shard_map.62 = bf16[2,64,1024]{2,1,0:T(8,128)(2,1)} custom-call(s32[5]{0:T(128)S(1)} %copy-done.8, bf16[64,1024]{1,0:T(8,128)(2,1)S(1)} %get-tuple-element.31.refs_0_, bf16[64,1024]{1,0:T(8,128)(2,1)S(1)} %collective-permute-done.1.refs_1_, bf16[64,1024]{1,0:T(8,128)(2,1)S(1)} %collective-permute-done.2.refs_2_, ...), custom_call_target="tpu_custom_call" | custom-call | flops 524288 | bytes 2097152 | tf_op jit(solution)/shard_map/pallas_call | solution.py:178
  100.7 4.2 %all-to-all-start.2 = ((bf16[8,16,1024]{2,1,0:T(8,128)(2,1)}), bf16[8,16,1024]{2,1,0:T(8,128)(2,1)S(1)}, u32[]{:S(2)}, u32[]{:S(2)}) async-start(bf16[8,16,1024]{2,1,0:T(8,128)(2,1)} %bitcast.6), calls=%async_computation.2 | async-start | bytes 524288 | tf_op jit(solution)/shard_map/all_to_all | solution.py:356
  105.0 1.2 copy-done.2
  106.2 1.4 %shard_map.65 = (f32[32,4096]{1,0:T(8,128)S(1)}, bf16[32,4096]{1,0:T(8,128)(2,1)S(1)}) custom-call(f32[64,4096]{1,0:T(8,128)S(1)} %copy-done.2, f32[64,4096]{1,0:T(8,128)} %collective-permute-done.9.got_ref), custom_call_target="tpu_custom_call" | custom-call | flops 262144 | bytes 3145728 | tf_op jit(solution)/shard_map/pallas_call | solution.py:286
  107.6 7.3 %collective-permute-start.10 = (bf16[32,4096]{1,0:T(8,128)(2,1)S(1)}, bf16[32,4096]{1,0:T(8,128)(2,1)S(1)}, u32[]{:S(2)}, u32[]{:S(2)}) collective-permute-start(bf16[32,4096]{1,0:T(8,128)(2,1)S(1)} %get-tuple-element.46), channel_id=1, source_target_pairs={{0,256},{256,0},{1,257},{257,1},{2,258},{258,2},{3,259},{259,3},{4... | collective-permute-start | bytes 786440 | tf_op jit(solution)/shard_map/ppermute | solution.py:330
  114.9 13.2 %collective-permute-done.10.far_ref = bf16[32,4096]{1,0:T(8,128)(2,1)S(1)} collective-permute-done((bf16[32,4096]{1,0:T(8,128)(2,1)S(1)}, bf16[32,4096]{1,0:T(8,128)(2,1)S(1)}, u32[]{:S(2)}, u32[]{:S(2)}) %collective-permute-start.10) | collective-permute-done | bytes 262176 | tf_op jit(solution)/shard_map/ppermute | solution.py:330
  (33 shorter events, 6.1 us)
Async XLA Ops:
  1.3 48.9 %copy-start.8 = (s32[5]{0:T(128)S(1)}, s32[5]{0:T(128)}, u32[]{:S(2)}) copy-start(s32[5]{0:T(128)} %stack.23.place) | copy-start | bytes 64
  5.0 61.7 %copy-start = (bf16[1,2048,768]{2,1,0:T(8,128)(2,1)S(1)}, bf16[1,2048,768]{2,1,0:T(8,128)(2,1)}, u32[]{:S(2)}) copy-start(bf16[1,2048,768]{2,1,0:T(8,128)(2,1)} %param.5) | copy-start | bytes 9437188
  5.0 61.7 %collective-permute-start = (bf16[2048,768]{1,0:T(8,128)(2,1)}, bf16[2048,768]{1,0:T(8,128)(2,1)}, u32[]{:S(2)}, u32[]{:S(2)}) collective-permute-start(bf16[2048,768]{1,0:T(8,128)(2,1)} %bitcast.7), channel_id=1, source_target_pairs={{0,128},{128,0},{1,129},{129,1},{2,130},{130,2},{3,131},{131,3},{4... | collective-permute-start | bytes 9437192 | tf_op jit(solution)/shard_map/ppermute | solution.py:330
  14.1 12.5 %all-to-all-start = ((f32[16,16,128]{2,1,0:T(8,128)}), f32[16,16,128]{2,1,0:T(8,128)S(1)}, u32[]{:S(2)}, u32[]{:S(2)}) async-start(f32[16,16,128]{2,1,0:T(8,128)} %get-tuple-element.36), calls=%async_computation | async-start | bytes 262144 | tf_op jit(solution)/shard_map/all_to_all | solution.py:340
  17.6 9.0 %collective-permute-start.5 = (bf16[16,768]{1,0:T(8,128)(2,1)}, bf16[16,768]{1,0:T(8,128)(2,1)S(1)}, u32[]{:S(2)}, u32[]{:S(2)}) collective-permute-start(bf16[16,768]{1,0:T(8,128)(2,1)} %get-tuple-element.38), channel_id=1, source_target_pairs={{0,256},{256,0},{1,257},{257,1},{2,258},{258,2},{3,259},{259,3},{4... | collective-permute-start | bytes 73736 | tf_op jit(solution)/shard_map/ppermute | solution.py:330
  26.6 0.8 copy-start.7
  50.2 1.1 copy-start.3
  51.4 1.0 copy-start.4
  52.4 9.5 %copy-start.9 = (bf16[128,768]{1,0:T(8,128)(2,1)S(1)}, bf16[128,768]{1,0:T(8,128)(2,1)}, u32[]{:S(2)}) copy-start(bf16[128,768]{1,0:T(8,128)(2,1)} %get-tuple-element.35) | copy-start | bytes 589828
  52.4 14.3 %copy-start.5 = (bf16[128,768]{1,0:T(8,128)(2,1)S(1)}, bf16[128,768]{1,0:T(8,128)(2,1)}, u32[]{:S(2)}) copy-start(bf16[128,768]{1,0:T(8,128)(2,1)} %get-tuple-element.26.own_ref) | copy-start | bytes 589828
  52.4 14.3 %copy-start.6 = (bf16[128,768]{1,0:T(8,128)(2,1)S(1)}, bf16[128,768]{1,0:T(8,128)(2,1)}, u32[]{:S(2)}) copy-start(bf16[128,768]{1,0:T(8,128)(2,1)} %get-tuple-element.27.other_ref) | copy-start | bytes 589828
  56.9 14.7 %copy-start.1 = (f32[64,4096]{1,0:T(8,128)}, f32[64,4096]{1,0:T(8,128)S(1)}, u32[]{:S(2)}) copy-start(f32[64,4096]{1,0:T(8,128)S(1)} %get-tuple-element.43.keep_ref) | copy-start | bytes 3145732
  56.9 48.0 %collective-permute-start.9 = (f32[64,4096]{1,0:T(8,128)}, f32[64,4096]{1,0:T(8,128)}, u32[]{:S(2)}, u32[]{:S(2)}) collective-permute-start(f32[64,4096]{1,0:T(8,128)} %get-tuple-element.44), channel_id=1, source_target_pairs={{0,128},{128,0},{1,129},{129,1},{2,130},{130,2},{3,131},{131,3},{4... | collective-permute-start | bytes 3145736 | tf_op jit(solution)/shard_map/ppermute | solution.py:330
  61.9 19.0 %collective-permute-start.4 = (bf16[128,768]{1,0:T(8,128)(2,1)S(1)}, bf16[128,768]{1,0:T(8,128)(2,1)S(1)}, u32[]{:S(2)}, u32[]{:S(2)}) collective-permute-start(bf16[128,768]{1,0:T(8,128)(2,1)S(1)} %copy-done.9), channel_id=1, source_target_pairs={{0,256},{256,0},{1,257},{257,1},{2,258},{258,2},{3,259},{259,3},{4... | collective-permute-start | bytes 589832 | tf_op jit(solution)/shard_map/ppermute | solution.py:330
  71.7 18.5 %collective-permute-start.1 = (bf16[64,1024]{1,0:T(8,128)(2,1)S(1)}, bf16[64,1024]{1,0:T(8,128)(2,1)S(1)}, u32[]{:S(2)}, u32[]{:S(2)}) collective-permute-start(bf16[64,1024]{1,0:T(8,128)(2,1)S(1)} %get-tuple-element.32), channel_id=1, source_target_pairs={{0,2},{1,3},{2,0},{3,1},{4,6},{5,7},{6,4},{7,5},{8,10},{9,11},{10,... | collective-permute-start | bytes 393224 | tf_op jit(solution)/shard_map/ppermute | solution.py:334
  76.2 16.2 %collective-permute-start.2 = (bf16[64,1024]{1,0:T(8,128)(2,1)S(1)}, bf16[64,1024]{1,0:T(8,128)(2,1)S(1)}, u32[]{:S(2)}, u32[]{:S(2)}) collective-permute-start(bf16[64,1024]{1,0:T(8,128)(2,1)S(1)} %get-tuple-element.33), channel_id=1, source_target_pairs={{0,1},{1,0},{2,3},{3,2},{4,5},{5,4},{6,7},{7,6},{8,9},{9,8},{10,11... | collective-permute-start | bytes 393224 | tf_op jit(solution)/shard_map/ppermute | solution.py:334
  78.4 16.6 %collective-permute-start.3 = (bf16[64,1024]{1,0:T(8,128)(2,1)S(1)}, bf16[64,1024]{1,0:T(8,128)(2,1)S(1)}, u32[]{:S(2)}, u32[]{:S(2)}) collective-permute-start(bf16[64,1024]{1,0:T(8,128)(2,1)S(1)} %get-tuple-element.34), channel_id=1, source_target_pairs={{0,3},{1,2},{2,1},{3,0},{4,7},{5,6},{6,5},{7,4},{8,11},{9,10},{10,... | collective-permute-start | bytes 393224 | tf_op jit(solution)/shard_map/ppermute | solution.py:334
  85.9 9.0 %collective-permute-start.6 = (bf16[64,1024]{1,0:T(8,128)(2,1)S(1)}, bf16[64,1024]{1,0:T(8,128)(2,1)S(1)}, u32[]{:S(2)}, u32[]{:S(2)}) collective-permute-start(bf16[64,1024]{1,0:T(8,128)(2,1)S(1)} %get-tuple-element.40), channel_id=1, source_target_pairs={{0,2},{1,3},{2,0},{3,1},{4,6},{5,7},{6,4},{7,5},{8,10},{9,11},{10,... | collective-permute-start | bytes 393224 | tf_op jit(solution)/shard_map/ppermute | solution.py:334
  90.2 5.7 %collective-permute-start.7 = (bf16[64,1024]{1,0:T(8,128)(2,1)S(1)}, bf16[64,1024]{1,0:T(8,128)(2,1)S(1)}, u32[]{:S(2)}, u32[]{:S(2)}) collective-permute-start(bf16[64,1024]{1,0:T(8,128)(2,1)S(1)} %get-tuple-element.41), channel_id=1, source_target_pairs={{0,1},{1,0},{2,3},{3,2},{4,5},{5,4},{6,7},{7,6},{8,9},{9,8},{10,11... | collective-permute-start | bytes 393224 | tf_op jit(solution)/shard_map/ppermute | solution.py:334
  92.4 6.9 %collective-permute-start.8 = (bf16[64,1024]{1,0:T(8,128)(2,1)S(1)}, bf16[64,1024]{1,0:T(8,128)(2,1)S(1)}, u32[]{:S(2)}, u32[]{:S(2)}) collective-permute-start(bf16[64,1024]{1,0:T(8,128)(2,1)S(1)} %get-tuple-element.42), channel_id=1, source_target_pairs={{0,3},{1,2},{2,1},{3,0},{4,7},{5,6},{6,5},{7,4},{8,11},{9,10},{10,... | collective-permute-start | bytes 393224 | tf_op jit(solution)/shard_map/ppermute | solution.py:334
  100.7 28.1 %all-to-all-start.2 = ((bf16[8,16,1024]{2,1,0:T(8,128)(2,1)}), bf16[8,16,1024]{2,1,0:T(8,128)(2,1)S(1)}, u32[]{:S(2)}, u32[]{:S(2)}) async-start(bf16[8,16,1024]{2,1,0:T(8,128)(2,1)} %bitcast.6), calls=%async_computation.2 | async-start | bytes 524288 | tf_op jit(solution)/shard_map/all_to_all | solution.py:356
  105.0 1.2 copy-start.2
  107.6 20.4 %collective-permute-start.10 = (bf16[32,4096]{1,0:T(8,128)(2,1)S(1)}, bf16[32,4096]{1,0:T(8,128)(2,1)S(1)}, u32[]{:S(2)}, u32[]{:S(2)}) collective-permute-start(bf16[32,4096]{1,0:T(8,128)(2,1)S(1)} %get-tuple-element.46), channel_id=1, source_target_pairs={{0,256},{256,0},{1,257},{257,1},{2,258},{258,2},{3,259},{259,3},{4... | collective-permute-start | bytes 786440 | tf_op jit(solution)/shard_map/ppermute | solution.py:330

commit v3 on v2

--- a/solution.py
+++ b/solution.py
@@ -113,7 +113,7 @@
 
 
 def product_kernel(place, own_ref, other_ref, near_lo, near_hi, far_lo, far_hi, *rest):
-    outs, low, high = rest[:4], rest[4], rest[5]
+    outs, low, high = rest[:-2], rest[-2], rest[-1]
     own = own_ref[...]
     other = other_ref[...].reshape(own.shape)
 
@@ -126,12 +126,16 @@
     high[...] = dot(near_hi, far_hi)
     for r in range(4):
         for y in range(4):
-            rows = pl.ds(pl.multiple_of((y * 4 + (place[4] ^ r)) * 8, 8), 8)
-            pair = jnp.concatenate([low[rows, :], high[rows, :]], axis=0)
-            outs[r][y * 16 : y * 16 + 16, :] = pair.astype(BF)
-
-
-def product(place, own, other, weight, weight_far):
+            x = place[4] ^ r if len(outs) == 4 else r
+            rows = pl.ds(pl.multiple_of((y * 4 + x) * 8, 8), 8)
+            pair = jnp.concatenate([low[rows, :], high[rows, :]], axis=0).astype(BF)
+            if len(outs) == 4:
+                outs[r][y * 16 : y * 16 + 16, :] = pair
+            else:
+                outs[0][r, y * 16 : y * 16 + 16, :] = pair
+
+
+def product(place, own, other, weight, weight_far, by_peer):
     count = own.shape[0]
     features, quarter = weight.shape
     half = features // 2
@@ -143,15 +147,20 @@
         second = pl.BlockSpec(other.shape[:2] + (quarter,), lambda j, place: (0, 0, 0))
     else:
         second = pl.BlockSpec((count, quarter), lambda j, place: (0, 0))
-    shape = jax.ShapeDtypeStruct((count // 2, half), BF)
+    if by_peer:
+        shape = (jax.ShapeDtypeStruct((count // 2, half), BF),) * 4
+        out_specs = [pl.BlockSpec((count // 2, step), lambda j, place: (0, j))] * 4
+    else:
+        shape = jax.ShapeDtypeStruct((4, count // 2, half), BF)
+        out_specs = pl.BlockSpec((4, count // 2, step), lambda j, place: (0, 0, j))
     return pl.pallas_call(
         product_kernel,
-        out_shape=(shape,) * 4,
+        out_shape=shape,
         grid_spec=pltpu.PrefetchScalarGridSpec(
             num_scalar_prefetch=1,
             grid=(steps,),
             in_specs=[pl.BlockSpec((count, quarter), lambda j, place: (0, 0)), second, low, high, low, high],
-            out_specs=[pl.BlockSpec((count // 2, step), lambda j, place: (0, j))] * 4,
+            out_specs=out_specs,
             scratch_shapes=[pltpu.VMEM((count, step), F32)] * 2,
         ),
         compiler_params=params(16),
@@ -159,17 +168,15 @@
     )(place, own, other, weight, weight, weight_far, weight_far)
 
 
-def x_sum_kernel(place, *refs):
-    out_ref = refs[-1]
-
+def x_sum_kernel(place, own_ref, near1_ref, near2_ref, near3_ref, far_ref, out_ref):
     def total(parts):
-        value = parts[0][...].astype(F32)
+        value = parts[0].astype(F32)
         for part in parts[1:]:
-            value = value + part[...].astype(F32)
+            value = value + part.astype(F32)
         return value.astype(BF)
 
-    out_ref[place[0]] = total(refs[:4])
-    out_ref[1 - place[0]] = total(refs[4:8])
+    out_ref[place[0]] = total([own_ref[...], near1_ref[...], near2_ref[...], near3_ref[...]])
+    out_ref[1 - place[0]] = total([far_ref[i] for i in range(far_ref.shape[0])])
 
 
 def x_sum(place, near, far):
@@ -178,11 +185,11 @@
     return pl.pallas_call(
         x_sum_kernel,
         out_shape=jax.ShapeDtypeStruct((2, rows, width), BF),
-        in_specs=[pl.BlockSpec(memory_space=pltpu.SMEM)] + [vmem] * 8,
+        in_specs=[pl.BlockSpec(memory_space=pltpu.SMEM)] + [vmem] * 5,
         out_specs=vmem,
         compiler_params=params(16),
         cost_estimate=cost(8 * rows * width, 2 * MB),
-    )(place, *near, *far)
+    )(place, *near, far)
 
 
 def y_sum_kernel(got_ref, out_ref):
@@ -334,23 +341,30 @@
             lax.ppermute(parts[r], "x", [(i, i ^ r) for i in range(4)]) for r in (2, 1, 3)
         ]
 
+    barrier = lax.optimization_barrier
     own, other, direct, share, left_part, right_part = prepare(place, acts, grad_out, 16, 8)
     share = swap(share, "yh")
-    left_part, weight, direct = lax.optimization_barrier((left_part, weight, direct))
+    left_part, weight_sent, direct = barrier((left_part, weight, direct))
     left_rows = lax.all_to_all(left_part, ("yl", "x"), 0, 0, tiled=True)
     direct = swap(direct, "yh")
-    weight_far = swap(weight, "core")
-
-    packed = pack(left_rows, right_part, share, 8)
+    weight_far = swap(weight_sent, "core")
+
+    left_rows, share, weight_far = barrier((left_rows, share, weight_far))
+    packed, own = barrier((pack(left_rows, right_part, share, 8), own))
     got = lax.all_to_all(packed, "row", 0, 0, tiled=True)
-
-    near = to_x_peers(product(place, own, other, weight, weight_far))
+    near = to_x_peers(product(place, own, other, weight, weight_far, True))
+    got, direct, near = barrier((got, direct, near))
 
     keep, send = stats(place, got, acts, grad_out)
-    near_rows, far_rows = core_sum(keep, swap(send, "core"))
+    send, direct = barrier((send, direct))
+    back = swap(send, "core")
+    far = product(place, direct, got, weight, weight_far, False)
+    back, far = barrier((back, far))
+    near_rows, far_rows = core_sum(keep, back)
+    far = lax.all_to_all(far, "x", 0, 0, tiled=True)
+    far, near_rows, far_rows = barrier((far, near_rows, far_rows))
     far_rows = swap(far_rows, "yh")
 
-    far = to_x_peers(product(place, direct, got, weight, weight_far))
     chunks = x_sum(place, near, far)
     chunks = chunks.reshape(8, -1, chunks.shape[2])
     input_grad = y_sum(lax.all_to_all(chunks, ("yh", "yl"), 0, 0, tiled=True))

time: 130 us -> 127 us (0.977)
  blocking collectives: 22.8 us -> 0 us
  local copies, waits for them, and re-layouts: 4.86 us -> 13.9 us
  waiting for transfers between devices: 23.5 us -> 31.6 us
  starting transfers between devices: 55 us -> 58.5 us
  Pallas kernels: 22.4 us -> 20.6 us
    all_to_all x1 -> x0, blocking collectives: 22.8 us -> none  [body(): got = lax.all_to_all(packed, 'row', 0, 0, tiled=True)]
    all_to_all x0 -> x2, starting transfers between devices: none -> 11.8 us  [the longest x1 8.31 us: body(): got = lax.all_to_all(packed, 'row', 0, 0, tiled=True)]
    unnamed x20 -> x40, local copies, waits for them, and re-layouts: 4.18 us -> 13.3 us
    ppermute x6 -> x3, starting transfers between devices: 18.2 us -> 9.22 us  [to_x_peers(): lax.ppermute(parts[r], 'x', [(i, i ^ r) for i in range(4)])]
    all_to_all x0 -> x2, waiting for transfers between devices: none -> 7.05 us  [the longest x1 7.05 us: body(): far = lax.all_to_all(far, 'x', 0, 0, tiled=True)]
    ppermute x5, waiting for transfers between devices: 19.1 us -> 21.5 us  [swap(): return lax.ppermute(value, axis, [(0, 1), (1, 0)])]
    ppermute x6 -> x3, waiting for transfers between devices: 4.39 us -> 3.06 us  [to_x_peers(): lax.ppermute(parts[r], 'x', [(i, i ^ r) for i in range(4)])]
  transfers between devices with their start and end apart: 13 -> 12, of which waited for: 4 -> 5; matrix products, arithmetic and copies ran while one was open for 0% -> 0% of each run, Pallas kernels for 14% -> 9%
where the time goes in v3:
time: 127 us; the launch traced here: 126 us
  starting transfers between devices  58.5 us (46%)
  waiting for transfers between devices  31.6 us (25%)
  Pallas kernels  20.6 us (16%)
  local copies, waits for them, and re-layouts  13.9 us (11%)
    ppermute x5, starting transfers between devices, swap(): return lax.ppermute(value, axis, [(0, 1), (1, 0)])  29.7 us
    ppermute x5, waiting for transfers between devices, swap(): return lax.ppermute(value, axis, [(0, 1), (1, 0)])  21.5 us
    unnamed x40, local copies, waits for them, and re-layouts  13.3 us
    pallas_call x2, Pallas kernels, product(): pl.pallas_call(product_kernel, out_shape=shape, grid_spec=pltpu.PrefetchS...  9.83 us
    ppermute x3, starting transfers between devices, to_x_peers(): lax.ppermute(parts[r], 'x', [(i, i ^ r) for i in range(4)])  9.22 us
    all_to_all x1, starting transfers between devices, body(): got = lax.all_to_all(packed, 'row', 0, 0, tiled=True)  8.31 us
    all_to_all x1, waiting for transfers between devices, body(): far = lax.all_to_all(far, 'x', 0, 0, tiled=True)  7.05 us
    all_to_all x1, starting transfers between devices, body(): input_grad = y_sum(lax.all_to_all(chunks, ('yh', 'yl'), 0, 0, tiled=True))  4.23 us
  transfers between devices with their start and end apart: 12, of which 5 were waited for; matrix products, arithmetic and copies ran while one was open for 0% of the time, Pallas kernels for 9%

profile of v3, /device:TPU:1, one launch (start us, length us, event | category | flops | bytes accessed | tf_op | source)
XLA Modules:
  0.0 125.5 jit_solution(57315046772022235)
XLA Ops:
  1.2 3.7 %shard_map.58 = (bf16[128,768]{1,0:T(8,128)(2,1)}, bf16[128,768]{1,0:T(8,128)(2,1)}, bf16[128,768]{1,0:T(8,128)(2,1)}, bf16[16,768]{1,0:T(8,128)(2,1)}, f32[16,1...) custom-call(s32[5]{0:T(128)} %stack.23.place, bf16[128,2048]{1,0:T(8,128)(2,1)} %acts_hbm.3, bf16[128,3072]{1,0:T(8,128)(2,1)} %grads_hbm.3), custom_call_target="tpu_custom_call" | custom-call | flops 167772160 | bytes 3145728 | tf_op jit(solution)/shard_map/pallas_call | solution.py:67
  5.0 8.8 %collective-permute-start.1 = (bf16[2048,768]{1,0:T(8,128)(2,1)}, bf16[2048,768]{1,0:T(8,128)(2,1)}, u32[]{:S(2)}, u32[]{:S(2)}) collective-permute-start(bf16[2048,768]{1,0:T(8,128)(2,1)} %bitcast.7), channel_id=1, source_target_pairs={{0,128},{128,0},{1,129},{129,1},{2,130},{130,2},{3,131},{131,3},{4... | collective-permute-start | bytes 9437192 | tf_op jit(solution)/shard_map/ppermute | solution.py:337
  13.8 3.5 %all-to-all-start = ((f32[16,16,128]{2,1,0:T(8,128)}), f32[16,16,128]{2,1,0:T(8,128)S(1)}, u32[]{:S(2)}, u32[]{:S(2)}) async-start(f32[16,16,128]{2,1,0:T(8,128)} %get-tuple-element.42), calls=%async_computation | async-start | bytes 262144 | tf_op jit(solution)/shard_map/all_to_all | solution.py:348
  17.3 3.0 %collective-permute-start = (bf16[16,768]{1,0:T(8,128)(2,1)}, bf16[16,768]{1,0:T(8,128)(2,1)S(1)}, u32[]{:S(2)}, u32[]{:S(2)}) collective-permute-start(bf16[16,768]{1,0:T(8,128)(2,1)} %get-tuple-element.43), channel_id=1, source_target_pairs={{0,256},{256,0},{1,257},{257,1},{2,258},{258,2},{3,259},{259,3},{4... | collective-permute-start | bytes 73736 | tf_op jit(solution)/shard_map/ppermute | solution.py:337
  20.4 5.9 %collective-permute-done.share_ref = bf16[16,768]{1,0:T(8,128)(2,1)S(1)} collective-permute-done((bf16[16,768]{1,0:T(8,128)(2,1)}, bf16[16,768]{1,0:T(8,128)(2,1)S(1)}, u32[]{:S(2)}, u32[]{:S(2)}) %collective-permute-start) | collective-permute-done | bytes 24608 | tf_op jit(solution)/shard_map/ppermute | solution.py:337
  27.9 8.3 %all-to-all-start.1 = ((bf16[8,16,1920]{2,1,0:T(8,128)(2,1)}), bf16[8,16,1920]{2,1,0:T(8,128)(2,1)}, u32[]{:S(2)}, u32[]{:S(2)}) async-start(bf16[8,16,1920]{2,1,0:T(8,128)(2,1)} %copy-done.2), calls=%async_computation.1 | async-start | bytes 983040 | tf_op jit(solution)/shard_map/all_to_all | solution.py:354
  36.2 4.7 %collective-permute-start.2 = (bf16[128,768]{1,0:T(8,128)(2,1)}, bf16[128,768]{1,0:T(8,128)(2,1)S(1)}, u32[]{:S(2)}, u32[]{:S(2)}) collective-permute-start(bf16[128,768]{1,0:T(8,128)(2,1)} %get-tuple-element.50), channel_id=1, source_target_pairs={{0,256},{256,0},{1,257},{257,1},{2,258},{258,2},{3,259},{259,3},{4... | collective-permute-start | bytes 589832 | tf_op jit(solution)/shard_map/ppermute | solution.py:337
  43.4 4.9 %shard_map.60 = (bf16[64,1024]{1,0:T(8,128)(2,1)S(1)}, bf16[64,1024]{1,0:T(8,128)(2,1)S(1)}, bf16[64,1024]{1,0:T(8,128)(2,1)S(1)}, bf16[64,1024]{1,0:T(8,128)(2,1)S(1)}) custom-call(s32[5]{0:T(128)S(1)} %copy-done.18, bf16[128,768]{1,0:T(8,128)(2,1)S(1)} %copy-done.9, bf16[128,768]{1,0:T(8,128)(2,1)S(1)} %copy-done.10, bf16[2048,768]{1,0:T(8,128)(2,1)S(1)} %bitcast.8, ...), custom_call_target="tpu_custom_call" | custom-call | flops 805306368 | bytes 7340032 | tf_op jit(solution)/shard_map/pallas_call | solution.py:156
  48.3 4.5 %collective-permute-start.3 = (bf16[64,1024]{1,0:T(8,128)(2,1)S(1)}, bf16[64,1024]{1,0:T(8,128)(2,1)S(1)}, u32[]{:S(2)}, u32[]{:S(2)}) collective-permute-start(bf16[64,1024]{1,0:T(8,128)(2,1)S(1)} %get-tuple-element.55), channel_id=1, source_target_pairs={{0,2},{1,3},{2,0},{3,1},{4,6},{5,7},{6,4},{7,5},{8,10},{9,11},{10,... | collective-permute-start | bytes 393224 | tf_op jit(solution)/shard_map/ppermute | solution.py:341
  52.9 2.2 %collective-permute-start.4 = (bf16[64,1024]{1,0:T(8,128)(2,1)S(1)}, bf16[64,1024]{1,0:T(8,128)(2,1)S(1)}, u32[]{:S(2)}, u32[]{:S(2)}) collective-permute-start(bf16[64,1024]{1,0:T(8,128)(2,1)S(1)} %get-tuple-element.56), channel_id=1, source_target_pairs={{0,1},{1,0},{2,3},{3,2},{4,5},{5,4},{6,7},{7,6},{8,9},{9,8},{10,11... | collective-permute-start | bytes 393224 | tf_op jit(solution)/shard_map/ppermute | solution.py:341
  55.1 2.5 %collective-permute-start.5 = (bf16[64,1024]{1,0:T(8,128)(2,1)S(1)}, bf16[64,1024]{1,0:T(8,128)(2,1)S(1)}, u32[]{:S(2)}, u32[]{:S(2)}) collective-permute-start(bf16[64,1024]{1,0:T(8,128)(2,1)S(1)} %get-tuple-element.57), channel_id=1, source_target_pairs={{0,3},{1,2},{2,1},{3,0},{4,7},{5,6},{6,5},{7,4},{8,11},{9,10},{10,... | collective-permute-start | bytes 393224 | tf_op jit(solution)/shard_map/ppermute | solution.py:341
  58.3 1.4 %collective-permute-done.4.near2_ref = bf16[64,1024]{1,0:T(8,128)(2,1)S(1)} collective-permute-done((bf16[64,1024]{1,0:T(8,128)(2,1)S(1)}, bf16[64,1024]{1,0:T(8,128)(2,1)S(1)}, u32[]{:S(2)}, u32[]{:S(2)}) %collective-permute-start.4) | collective-permute-done | bytes 131104 | tf_op jit(solution)/shard_map/ppermute | solution.py:341
  60.3 1.7 %collective-permute-done.5.near3_ref = bf16[64,1024]{1,0:T(8,128)(2,1)S(1)} collective-permute-done((bf16[64,1024]{1,0:T(8,128)(2,1)S(1)}, bf16[64,1024]{1,0:T(8,128)(2,1)S(1)}, u32[]{:S(2)}, u32[]{:S(2)}) %collective-permute-start.5) | collective-permute-done | bytes 131104 | tf_op jit(solution)/shard_map/ppermute | solution.py:341
  64.8 4.1 %shard_map.61 = (f32[64,4096]{1,0:T(8,128)S(1)}, f32[64,4096]{1,0:T(8,128)S(1)}) custom-call(s32[5]{0:T(128)S(1)} %copy-done.19, bf16[8,16,1920]{2,1,0:T(8,128)(2,1)} %all-to-all-done.1.got_ref.other_ref, bf16[128,2048]{1,0:T(8,128)(2,1)S(1)} %copy-done.8, bf16[128,3072]{1,0:T(8,128)(2,1)S(1)} %copy-done.7), custom_call_target="tpu_custom_call" | custom-call | flops 1048576000 | bytes 5242880 | tf_op jit(solution)/shard_map/pallas_call | solution.py:269
  69.9 5.9 %collective-permute-start.6 = (f32[64,4096]{1,0:T(8,128)S(1)}, f32[64,4096]{1,0:T(8,128)S(1)}, u32[]{:S(2)}, u32[]{:S(2)}) collective-permute-start(f32[64,4096]{1,0:T(8,128)S(1)} %get-tuple-element.65), channel_id=1, source_target_pairs={{0,128},{128,0},{1,129},{129,1},{2,130},{130,2},{3,131},{131,3},{4... | collective-permute-start | bytes 3145736 | tf_op jit(solution)/shard_map/ppermute | solution.py:337
  75.8 4.9 %shard_map.62 = bf16[4,64,1024]{2,1,0:T(8,128)(2,1)S(1)} custom-call(s32[5]{0:T(128)S(1)} %copy-done.19, bf16[128,768]{1,0:T(8,128)(2,1)S(1)} %collective-permute-done.2.own_ref, bf16[8,16,1920]{2,1,0:T(8,128)(2,1)} %all-to-all-done.1.got_ref.other_ref, bf16[2048,768]{1,0:T(8,128)(2,1)S(1)} %bitcast.10, bf16[2048,768]{1,0:T(8,128)(2,1)S(1)} %bitcast.11, ...), custom_call_target="tpu_custom_call" | custom-call | flops 805306368 | bytes 7340032 | tf_op jit(solution)/shard_map/pallas_call | solution.py:156
  82.5 3.5 %all-to-all-start.2 = ((bf16[4,64,1024]{2,1,0:T(8,128)(2,1)}), bf16[4,64,1024]{2,1,0:T(8,128)(2,1)S(1)}, u32[]{:S(2)}, u32[]{:S(2)}) async-start(bf16[4,64,1024]{2,1,0:T(8,128)(2,1)} %copy-done.1), calls=%async_computation.2 | async-start | bytes 1048576 | tf_op jit(solution)/shard_map/all_to_all | solution.py:364
  86.0 1.2 copy-done.4
  87.2 1.2 copy-done.6
  88.5 7.1 %all-to-all-done.2.far_ref = bf16[4,64,1024]{2,1,0:T(8,128)(2,1)S(1)} async-done(((bf16[4,64,1024]{2,1,0:T(8,128)(2,1)}), bf16[4,64,1024]{2,1,0:T(8,128)(2,1)S(1)}, u32[]{:S(2)}, u32[]{:S(2)}) %all-to-all-start.2) | async-done | bytes 524320 | tf_op jit(solution)/shard_map/all_to_all | solution.py:364
  95.6 1.4 %shard_map.64 = bf16[2,64,1024]{2,1,0:T(8,128)(2,1)} custom-call(s32[5]{0:T(128)S(1)} %copy-done.19, bf16[64,1024]{1,0:T(8,128)(2,1)S(1)} %get-tuple-element.58.own_ref, bf16[64,1024]{1,0:T(8,128)(2,1)S(1)} %copy-done.12, bf16[64,1024]{1,0:T(8,128)(2,1)S(1)} %copy-done.14, bf16[64,1024]{1,0:T(8,128)(2,1)S(1)} %copy-done.16, ...), custom_call_target="tpu_custom_call" | custom-call | flops 524288 | bytes 2097152 | tf_op jit(solution)/shard_map/pallas_call | solution.py:185
  97.0 4.2 %all-to-all-start.3 = ((bf16[8,16,1024]{2,1,0:T(8,128)(2,1)}), bf16[8,16,1024]{2,1,0:T(8,128)(2,1)S(1)}, u32[]{:S(2)}, u32[]{:S(2)}) async-start(bf16[8,16,1024]{2,1,0:T(8,128)(2,1)} %bitcast.6), calls=%async_computation.3 | async-start | bytes 524288 | tf_op jit(solution)/shard_map/all_to_all | solution.py:370
  101.2 7.3 %collective-permute-start.7 = (bf16[32,4096]{1,0:T(8,128)(2,1)S(1)}, bf16[32,4096]{1,0:T(8,128)(2,1)S(1)}, u32[]{:S(2)}, u32[]{:S(2)}) collective-permute-start(bf16[32,4096]{1,0:T(8,128)(2,1)S(1)} %get-tuple-element.74), channel_id=1, source_target_pairs={{0,256},{256,0},{1,257},{257,1},{2,258},{258,2},{3,259},{259,3},{4... | collective-permute-start | bytes 786440 | tf_op jit(solution)/shard_map/ppermute | solution.py:337
  108.5 15.5 %collective-permute-done.7.far_ref = bf16[32,4096]{1,0:T(8,128)(2,1)S(1)} collective-permute-done((bf16[32,4096]{1,0:T(8,128)(2,1)S(1)}, bf16[32,4096]{1,0:T(8,128)(2,1)S(1)}, u32[]{:S(2)}, u32[]{:S(2)}) %collective-permute-start.7) | collective-permute-done | bytes 262176 | tf_op jit(solution)/shard_map/ppermute | solution.py:337
  (50 shorter events, 13.1 us)
Async XLA Ops:
  0.6 40.3 %copy-start = (bf16[1,2048,768]{2,1,0:T(8,128)(2,1)S(1)}, bf16[1,2048,768]{2,1,0:T(8,128)(2,1)}, u32[]{:S(2)}) copy-start(bf16[1,2048,768]{2,1,0:T(8,128)(2,1)} %param.5) | copy-start | bytes 9437188
  5.0 21.3 %collective-permute-start.1 = (bf16[2048,768]{1,0:T(8,128)(2,1)}, bf16[2048,768]{1,0:T(8,128)(2,1)}, u32[]{:S(2)}, u32[]{:S(2)}) collective-permute-start(bf16[2048,768]{1,0:T(8,128)(2,1)} %bitcast.7), channel_id=1, source_target_pairs={{0,128},{128,0},{1,129},{129,1},{2,130},{130,2},{3,131},{131,3},{4... | collective-permute-start | bytes 9437192 | tf_op jit(solution)/shard_map/ppermute | solution.py:337
  13.8 12.5 %all-to-all-start = ((f32[16,16,128]{2,1,0:T(8,128)}), f32[16,16,128]{2,1,0:T(8,128)S(1)}, u32[]{:S(2)}, u32[]{:S(2)}) async-start(f32[16,16,128]{2,1,0:T(8,128)} %get-tuple-element.42), calls=%async_computation | async-start | bytes 262144 | tf_op jit(solution)/shard_map/all_to_all | solution.py:348
  17.3 9.0 %collective-permute-start = (bf16[16,768]{1,0:T(8,128)(2,1)}, bf16[16,768]{1,0:T(8,128)(2,1)S(1)}, u32[]{:S(2)}, u32[]{:S(2)}) collective-permute-start(bf16[16,768]{1,0:T(8,128)(2,1)} %get-tuple-element.43), channel_id=1, source_target_pairs={{0,256},{256,0},{1,257},{257,1},{2,258},{258,2},{3,259},{259,3},{4... | collective-permute-start | bytes 73736 | tf_op jit(solution)/shard_map/ppermute | solution.py:337
  27.9 34.8 %all-to-all-start.1 = ((bf16[8,16,1920]{2,1,0:T(8,128)(2,1)}), bf16[8,16,1920]{2,1,0:T(8,128)(2,1)}, u32[]{:S(2)}, u32[]{:S(2)}) async-start(bf16[8,16,1920]{2,1,0:T(8,128)(2,1)} %copy-done.2), calls=%async_computation.1 | async-start | bytes 983040 | tf_op jit(solution)/shard_map/all_to_all | solution.py:354
  36.2 21.4 %collective-permute-start.2 = (bf16[128,768]{1,0:T(8,128)(2,1)}, bf16[128,768]{1,0:T(8,128)(2,1)S(1)}, u32[]{:S(2)}, u32[]{:S(2)}) collective-permute-start(bf16[128,768]{1,0:T(8,128)(2,1)} %get-tuple-element.50), channel_id=1, source_target_pairs={{0,256},{256,0},{1,257},{257,1},{2,258},{258,2},{3,259},{259,3},{4... | collective-permute-start | bytes 589832 | tf_op jit(solution)/shard_map/ppermute | solution.py:337
  41.0 0.9 copy-start.9
  43.4 19.2 %copy-start.19 = (s32[5]{0:T(128)S(1)}, s32[5]{0:T(128)}, u32[]{:S(2)}) copy-start(s32[5]{0:T(128)} %stack.23.place) | copy-start | bytes 64
  48.3 9.3 %collective-permute-start.3 = (bf16[64,1024]{1,0:T(8,128)(2,1)S(1)}, bf16[64,1024]{1,0:T(8,128)(2,1)S(1)}, u32[]{:S(2)}, u32[]{:S(2)}) collective-permute-start(bf16[64,1024]{1,0:T(8,128)(2,1)S(1)} %get-tuple-element.55), channel_id=1, source_target_pairs={{0,2},{1,3},{2,0},{3,1},{4,6},{5,7},{6,4},{7,5},{8,10},{9,11},{10,... | collective-permute-start | bytes 393224 | tf_op jit(solution)/shard_map/ppermute | solution.py:341
  52.9 6.8 %collective-permute-start.4 = (bf16[64,1024]{1,0:T(8,128)(2,1)S(1)}, bf16[64,1024]{1,0:T(8,128)(2,1)S(1)}, u32[]{:S(2)}, u32[]{:S(2)}) collective-permute-start(bf16[64,1024]{1,0:T(8,128)(2,1)S(1)} %get-tuple-element.56), channel_id=1, source_target_pairs={{0,1},{1,0},{2,3},{3,2},{4,5},{5,4},{6,7},{7,6},{8,9},{9,8},{10,11... | collective-permute-start | bytes 393224 | tf_op jit(solution)/shard_map/ppermute | solution.py:341
  55.1 6.9 %collective-permute-start.5 = (bf16[64,1024]{1,0:T(8,128)(2,1)S(1)}, bf16[64,1024]{1,0:T(8,128)(2,1)S(1)}, u32[]{:S(2)}, u32[]{:S(2)}) collective-permute-start(bf16[64,1024]{1,0:T(8,128)(2,1)S(1)} %get-tuple-element.57), channel_id=1, source_target_pairs={{0,3},{1,2},{2,1},{3,0},{4,7},{5,6},{6,5},{7,4},{8,11},{9,10},{10,... | collective-permute-start | bytes 393224 | tf_op jit(solution)/shard_map/ppermute | solution.py:341
  62.6 1.1 copy-start.7
  63.8 1.0 copy-start.8
  68.9 1.0 copy-start.3
  69.9 11.6 %collective-permute-start.6 = (f32[64,4096]{1,0:T(8,128)S(1)}, f32[64,4096]{1,0:T(8,128)S(1)}, u32[]{:S(2)}, u32[]{:S(2)}) collective-permute-start(f32[64,4096]{1,0:T(8,128)S(1)} %get-tuple-element.65), channel_id=1, source_target_pairs={{0,128},{128,0},{1,129},{129,1},{2,130},{130,2},{3,131},{131,3},{4... | collective-permute-start | bytes 3145736 | tf_op jit(solution)/shard_map/ppermute | solution.py:337
  81.5 14.1 %copy-start.12 = (bf16[64,1024]{1,0:T(8,128)(2,1)S(1)}, bf16[64,1024]{1,0:T(8,128)(2,1)}, u32[]{:S(2)}) copy-start(bf16[64,1024]{1,0:T(8,128)(2,1)} %copy-done.11) | copy-start | bytes 393220
  81.5 14.1 %copy-start.14 = (bf16[64,1024]{1,0:T(8,128)(2,1)S(1)}, bf16[64,1024]{1,0:T(8,128)(2,1)}, u32[]{:S(2)}) copy-start(bf16[64,1024]{1,0:T(8,128)(2,1)} %copy-done.13) | copy-start | bytes 393220
  81.5 14.1 %copy-start.16 = (bf16[64,1024]{1,0:T(8,128)(2,1)S(1)}, bf16[64,1024]{1,0:T(8,128)(2,1)}, u32[]{:S(2)}) copy-start(bf16[64,1024]{1,0:T(8,128)(2,1)} %copy-done.15) | copy-start | bytes 393220
  81.5 1.0 copy-start.5
  82.5 13.1 %all-to-all-start.2 = ((bf16[4,64,1024]{2,1,0:T(8,128)(2,1)}), bf16[4,64,1024]{2,1,0:T(8,128)(2,1)S(1)}, u32[]{:S(2)}, u32[]{:S(2)}) async-start(bf16[4,64,1024]{2,1,0:T(8,128)(2,1)} %copy-done.1), calls=%async_computation.2 | async-start | bytes 1048576 | tf_op jit(solution)/shard_map/all_to_all | solution.py:364
  86.0 1.2 copy-start.4
  87.2 1.2 copy-start.6
  97.0 27.9 %all-to-all-start.3 = ((bf16[8,16,1024]{2,1,0:T(8,128)(2,1)}), bf16[8,16,1024]{2,1,0:T(8,128)(2,1)S(1)}, u32[]{:S(2)}, u32[]{:S(2)}) async-start(bf16[8,16,1024]{2,1,0:T(8,128)(2,1)} %bitcast.6), calls=%async_computation.3 | async-start | bytes 524288 | tf_op jit(solution)/shard_map/all_to_all | solution.py:370
  101.2 22.8 %collective-permute-start.7 = (bf16[32,4096]{1,0:T(8,128)(2,1)S(1)}, bf16[32,4096]{1,0:T(8,128)(2,1)S(1)}, u32[]{:S(2)}, u32[]{:S(2)}) collective-permute-start(bf16[32,4096]{1,0:T(8,128)(2,1)S(1)} %get-tuple-element.74), channel_id=1, source_target_pairs={{0,256},{256,0},{1,257},{257,1},{2,258},{258,2},{3,259},{259,3},{4... | collective-permute-start | bytes 786440 | tf_op jit(solution)/shard_map/ppermute | solution.py:337
  (8 other events, 5.8 us)

commit v4 on v3

--- a/solution.py
+++ b/solution.py
@@ -25,63 +25,31 @@
     return pl.CostEstimate(flops=flops, bytes_accessed=moved, transcendentals=0)
 
 
-def prepare_kernel(place, acts_hbm, grads_hbm, own_ref, other_ref, direct_ref, share_ref, left_ref, right_ref, acts_ref, grads_ref, sems):
-    quarter = own_ref.shape[1]
-    rows = share_ref.shape[0]
-    chunk = BLOCK
-
-    def lanes(y, c):
-        q = y * 2 + c
-        return pl.ds(pl.multiple_of(q * quarter, quarter), quarter)
-
+def prepare_kernel(place, acts_ref, grads_ref, left_ref, right_ref):
+    rows = right_ref.shape[0]
     turn = pl.ds(pl.multiple_of(place[2] * rows, rows), rows)
-    yh, core = place[0], place[1]
-    pieces = [
-        (grads_hbm.at[turn, lanes(1 - yh, 1 - core)], share_ref),
-        (grads_hbm.at[:, lanes(1 - yh, core)], direct_ref),
-        (grads_hbm.at[:, lanes(yh, core)], own_ref),
-        (grads_hbm.at[:, lanes(yh, 1 - core)], other_ref),
-    ]
-    copies = [pltpu.make_async_copy(grads_hbm, grads_ref, sems.at[0]), pltpu.make_async_copy(acts_hbm, acts_ref, sems.at[1])]
-    copies += [pltpu.make_async_copy(s, d, sems.at[2 + i]) for i, (s, d) in enumerate(pieces)]
-    for copy in copies:
-        copy.start()
-    copies[0].wait()
     left = lax.dot_general(grads_ref[turn, :], grads_ref[...], NT, preferred_element_type=F32)
     for i in range(left_ref.shape[0]):
         left_ref[i] = left
-    copies[1].wait()
     acts = acts_ref[...]
     right = lax.dot_general(acts, acts, NT, preferred_element_type=F32).astype(BF)
     for i in range(right.shape[0] // rows):
         right_ref[:, i * 128 : i * 128 + 128] = right[i * rows : i * rows + rows]
-    for copy in copies[2:]:
-        copy.wait()
 
 
 def prepare(place, acts, grads, cols, rows):
     tokens, hidden = grads.shape
-    quarter = hidden // 4
     share = tokens // rows
-    piece = jax.ShapeDtypeStruct((tokens, quarter), BF)
+    vmem = pl.BlockSpec(memory_space=pltpu.VMEM)
     return pl.pallas_call(
         prepare_kernel,
         out_shape=(
-            piece,
-            piece,
-            piece,
-            jax.ShapeDtypeStruct((share, quarter), BF),
             jax.ShapeDtypeStruct((cols, share, tokens), F32),
             jax.ShapeDtypeStruct((share, rows * tokens), BF),
         ),
-        in_specs=[
-            pl.BlockSpec(memory_space=pltpu.SMEM),
-            pl.BlockSpec(memory_space=pltpu.HBM),
-            pl.BlockSpec(memory_space=pltpu.HBM),
-        ],
-        out_specs=[pl.BlockSpec(memory_space=pltpu.VMEM)] * 6,
-        scratch_shapes=[pltpu.VMEM(acts.shape, BF), pltpu.VMEM(grads.shape, BF), pltpu.SemaphoreType.DMA((6,))],
-        compiler_params=params(56),
+        in_specs=[pl.BlockSpec(memory_space=pltpu.SMEM), vmem, vmem],
+        out_specs=[vmem] * 2,
+        compiler_params=params(60),
         cost_estimate=cost(2 * tokens * tokens * (hidden + acts.shape[1]), 3 * MB),
     )(place, acts, grads)
 
@@ -107,15 +75,22 @@
         out_shape=jax.ShapeDtypeStruct((rows, share.shape[0], width), BF),
         in_specs=[vmem] * 3,
         out_specs=vmem,
-        compiler_params=params(16),
+        compiler_params=params(60),
         cost_estimate=cost(MB, MB),
     )(left, right, share)
 
 
-def product_kernel(place, own_ref, other_ref, near_lo, near_hi, far_lo, far_hi, *rest):
+def product_kernel(place, tokens_ref, near_lo, near_hi, far_lo, far_hi, *rest):
     outs, low, high = rest[:-2], rest[-2], rest[-1]
-    own = own_ref[...]
-    other = other_ref[...].reshape(own.shape)
+    quarter = near_lo.shape[1]
+
+    def piece(core):
+        lanes = pl.ds(pl.multiple_of(core * quarter, quarter), quarter)
+        if len(tokens_ref.shape) == 3:
+            return tokens_ref[:, :, lanes].reshape(-1, quarter)
+        return tokens_ref[:, lanes]
+
+    own, other = piece(place[1]), piece(1 - place[1])
 
     def dot(near, far):
         return lax.dot_general(own, near[...], NT, preferred_element_type=F32) + lax.dot_general(
@@ -135,18 +110,19 @@
                 outs[0][r, y * 16 : y * 16 + 16, :] = pair
 
 
-def product(place, own, other, weight, weight_far, by_peer):
-    count = own.shape[0]
+def product(place, tokens, weight, weight_far, by_peer):
     features, quarter = weight.shape
     half = features // 2
     step = 256
     steps = half // step
     low = pl.BlockSpec((step, quarter), lambda j, place: (j, 0))
     high = pl.BlockSpec((step, quarter), lambda j, place: (j + steps, 0))
-    if other.ndim == 3:
-        second = pl.BlockSpec(other.shape[:2] + (quarter,), lambda j, place: (0, 0, 0))
+    if tokens.ndim == 3:
+        count = tokens.shape[0] * tokens.shape[1]
+        token_spec = pl.BlockSpec(tokens.shape[:2] + (2 * quarter,), lambda j, place: (0, 0, 0))
     else:
-        second = pl.BlockSpec((count, quarter), lambda j, place: (0, 0))
+        count = tokens.shape[0]
+        token_spec = pl.BlockSpec((count, 2 * quarter), lambda j, place: (0, place[0]))
     if by_peer:
         shape = (jax.ShapeDtypeStruct((count // 2, half), BF),) * 4
         out_specs = [pl.BlockSpec((count // 2, step), lambda j, place: (0, j))] * 4
@@ -159,13 +135,13 @@
         grid_spec=pltpu.PrefetchScalarGridSpec(
             num_scalar_prefetch=1,
             grid=(steps,),
-            in_specs=[pl.BlockSpec((count, quarter), lambda j, place: (0, 0)), second, low, high, low, high],
+            in_specs=[token_spec, low, high, low, high],
             out_specs=out_specs,
             scratch_shapes=[pltpu.VMEM((count, step), F32)] * 2,
         ),
-        compiler_params=params(16),
+        compiler_params=params(60),
         cost_estimate=cost(4 * count * features * quarter, 7 * MB),
-    )(place, own, other, weight, weight, weight_far, weight_far)
+    )(place, tokens, weight, weight, weight_far, weight_far)
 
 
 def x_sum_kernel(place, own_ref, near1_ref, near2_ref, near3_ref, far_ref, out_ref):
@@ -187,7 +163,7 @@
         out_shape=jax.ShapeDtypeStruct((2, rows, width), BF),
         in_specs=[pl.BlockSpec(memory_space=pltpu.SMEM)] + [vmem] * 5,
         out_specs=vmem,
-        compiler_params=params(16),
+        compiler_params=params(60),
         cost_estimate=cost(8 * rows * width, 2 * MB),
     )(place, *near, far)
 
@@ -206,7 +182,7 @@
         out_shape=jax.ShapeDtypeStruct((8, 2 * width), BF),
         in_specs=[pl.BlockSpec(memory_space=pltpu.VMEM)],
         out_specs=pl.BlockSpec(memory_space=pltpu.VMEM),
-        compiler_params=params(16),
+        compiler_params=params(60),
         cost_estimate=cost(128 * width, MB // 2),
     )(got)
 
@@ -276,7 +252,7 @@
             pltpu.VMEM(grads.shape, BF),
             pltpu.SemaphoreType.DMA(((acts.shape[1] + grads.shape[1]) // BLOCK,)),
         ],
-        compiler_params=params(16),
+        compiler_params=params(60),
         cost_estimate=cost(1000 * MB, 5 * MB),
     )(place, got, acts, grads)
 
@@ -298,7 +274,7 @@
         ),
         in_specs=[vmem, vmem],
         out_specs=[vmem, vmem],
-        compiler_params=params(16),
+        compiler_params=params(60),
         cost_estimate=cost(rows * width, 3 * MB),
     )(keep, got)
 
@@ -321,7 +297,7 @@
         ),
         in_specs=[vmem, vmem],
         out_specs=[vmem, vmem],
-        compiler_params=params(16),
+        compiler_params=params(60),
         cost_estimate=cost(32 * 4096, 2 * MB),
     )(near, far)
 
@@ -342,31 +318,31 @@
         ]
 
     barrier = lax.optimization_barrier
-    own, other, direct, share, left_part, right_part = prepare(place, acts, grad_out, 16, 8)
+    share = lax.dynamic_slice(grad_out, (row * 16, (1 - yh) * (hidden // 2)), (16, hidden // 2))
     share = swap(share, "yh")
-    left_part, weight_sent, direct = barrier((left_part, weight, direct))
+    left_part, right_part = prepare(place, acts, grad_out, 16, 8)
     left_rows = lax.all_to_all(left_part, ("yl", "x"), 0, 0, tiled=True)
-    direct = swap(direct, "yh")
-    weight_far = swap(weight_sent, "core")
+    weight_far = swap(weight, "core")
 
     left_rows, share, weight_far = barrier((left_rows, share, weight_far))
-    packed, own = barrier((pack(left_rows, right_part, share, 8), own))
+    packed, near_tokens = barrier((pack(left_rows, right_part, share, 8), grad_out))
     got = lax.all_to_all(packed, "row", 0, 0, tiled=True)
-    near = to_x_peers(product(place, own, other, weight, weight_far, True))
-    got, direct, near = barrier((got, direct, near))
+    near = to_x_peers(product(place, near_tokens, weight, weight_far, True))
+    got, near = barrier((got, near))
 
     keep, send = stats(place, got, acts, grad_out)
-    send, direct = barrier((send, direct))
+    send, far_tokens = barrier((send, got))
     back = swap(send, "core")
-    far = product(place, direct, got, weight, weight_far, False)
+    far = product(place, far_tokens, weight, weight_far, False)
     back, far = barrier((back, far))
     near_rows, far_rows = core_sum(keep, back)
+    far, far_rows = barrier((far, far_rows))
+    far_rows = swap(far_rows, "yh")
     far = lax.all_to_all(far, "x", 0, 0, tiled=True)
-    far, near_rows, far_rows = barrier((far, near_rows, far_rows))
-    far_rows = swap(far_rows, "yh")
 
     chunks = x_sum(place, near, far)
     chunks = chunks.reshape(8, -1, chunks.shape[2])
+    chunks, far_rows = barrier((chunks, far_rows))
     input_grad = y_sum(lax.all_to_all(chunks, ("yh", "yl"), 0, 0, tiled=True))
 
     left_stats, right_stats = last_sum(near_rows, far_rows, hidden, width)

time: 127 us -> 122 us (0.961)
  Pallas kernels: 20.6 us -> 31.8 us
  local copies, waits for them, and re-layouts: 13.9 us -> 4.65 us
  waiting for transfers between devices: 31.6 us -> 26.3 us
  starting transfers between devices: 58.5 us -> 56.5 us
    ppermute x5 -> x4, waiting for transfers between devices: 21.5 us -> 7.6 us  [swap(): return lax.ppermute(value, axis, [(0, 1), (1, 0)])]
    unnamed x40 -> x20, local copies, waits for them, and re-layouts: 13.3 us -> 3.16 us
    all_to_all x1, waiting for transfers between devices: 0.01 us -> 8.86 us  [body(): input_grad = y_sum(lax.all_to_all(chunks, ('yh', 'yl'), 0, 0, tiled=True))]
    ppermute x5 -> x4, starting transfers between devices: 29.7 us -> 21.8 us  [swap(): return lax.ppermute(value, axis, [(0, 1), (1, 0)])]
    all_to_all x1, starting transfers between devices: 4.23 us -> 10.4 us  [body(): input_grad = y_sum(lax.all_to_all(chunks, ('yh', 'yl'), 0, 0, tiled=True))]
    pallas_call x2, Pallas kernels: 9.83 us -> 12.9 us  [product(): pl.pallas_call(product_kernel, out_shape=shape, grid_spec=pltpu.PrefetchS...]
    pallas_call x1, Pallas kernels: 0.1 us -> 2.47 us  [core_sum(): pl.pallas_call(core_sum_kernel, out_shape=(jax.ShapeDtypeStruct((rows //...]
    pallas_call x1, Pallas kernels: 4.07 us -> 6.27 us  [stats(): pl.pallas_call(stats_kernel, out_shape=(shape, shape), in_specs=[pl.Block...]
  transfers between devices with their start and end apart: 12 -> 11, of which waited for: 5 -> 6; matrix products, arithmetic and copies ran while one was open for 0% -> 1% of each run, Pallas kernels for 9% -> 16%
where the time goes in v4:
time: 122 us; the launch traced here: 120 us
  starting transfers between devices  56.5 us (46%)
  Pallas kernels  31.8 us (26%)
  waiting for transfers between devices  26.3 us (22%)
  local copies, waits for them, and re-layouts  4.65 us (4%)
    ppermute x4, starting transfers between devices, swap(): return lax.ppermute(value, axis, [(0, 1), (1, 0)])  21.8 us
    pallas_call x2, Pallas kernels, product(): pl.pallas_call(product_kernel, out_shape=shape, grid_spec=pltpu.PrefetchS...  12.9 us
    all_to_all x1, starting transfers between devices, body(): input_grad = y_sum(lax.all_to_all(chunks, ('yh', 'yl'), 0, 0, tiled=True))  10.4 us
    ppermute x3, starting transfers between devices, to_x_peers(): lax.ppermute(parts[r], 'x', [(i, i ^ r) for i in range(4)])  9.49 us
    all_to_all x1, waiting for transfers between devices, body(): input_grad = y_sum(lax.all_to_all(chunks, ('yh', 'yl'), 0, 0, tiled=True))  8.86 us
    all_to_all x1, starting transfers between devices, body(): got = lax.all_to_all(packed, 'row', 0, 0, tiled=True)  7.92 us
    ppermute x4, waiting for transfers between devices, swap(): return lax.ppermute(value, axis, [(0, 1), (1, 0)])  7.6 us
    pallas_call x1, Pallas kernels, stats(): pl.pallas_call(stats_kernel, out_shape=(shape, shape), in_specs=[pl.Block...  6.27 us
  transfers between devices with their start and end apart: 11, of which 6 were waited for; matrix products, arithmetic and copies ran while one was open for 1% of the time, Pallas kernels for 16%

profile of v4, /device:TPU:1, one launch (start us, length us, event | category | flops | bytes accessed | tf_op | source)
XLA Modules:
  0.0 120.2 jit_solution(14884049704021909852)
XLA Ops:
  0.6 8.8 %collective-permute-start.1 = (bf16[2048,768]{1,0:T(8,128)(2,1)}, bf16[2048,768]{1,0:T(8,128)(2,1)S(1)}, u32[]{:S(2)}, u32[]{:S(2)}) collective-permute-start(bf16[2048,768]{1,0:T(8,128)(2,1)} %bitcast.7), channel_id=1, source_target_pairs={{0,128},{128,0},{1,129},{129,1},{2,130},{130,2},{3,131},{131,3},{4... | collective-permute-start | bytes 9437192 | tf_op jit(solution)/shard_map/ppermute | solution.py:313
  10.1 2.4 %shard_map.58 = (f32[16,16,128]{2,1,0:T(8,128)}, bf16[16,1024]{1,0:T(8,128)(2,1)}) custom-call(s32[5]{0:T(128)} %stack.23.place, bf16[128,2048]{1,0:T(8,128)(2,1)} %acts_hbm.1, bf16[128,3072]{1,0:T(8,128)(2,1)} %grads_hbm.1), custom_call_target="tpu_custom_call" | custom-call | flops 167772160 | bytes 3145728 | tf_op jit(solution)/shard_map/pallas_call | solution.py:44
  12.5 3.5 %all-to-all-start = ((f32[16,16,128]{2,1,0:T(8,128)}), f32[16,16,128]{2,1,0:T(8,128)S(1)}, u32[]{:S(2)}, u32[]{:S(2)}) async-start(f32[16,16,128]{2,1,0:T(8,128)} %get-tuple-element.33), calls=%async_computation | async-start | bytes 262144 | tf_op jit(solution)/shard_map/all_to_all | solution.py:324
  16.9 3.0 %collective-permute-start = (bf16[16,1536]{1,0:T(8,128)(2,1)S(1)}, bf16[16,1536]{1,0:T(8,128)(2,1)S(1)}, u32[]{:S(2)}, u32[]{:S(2)}) collective-permute-start(bf16[16,1536]{1,0:T(8,128)(2,1)S(1)} %dynamic_slice.3), channel_id=1, source_target_pairs={{0,256},{256,0},{1,257},{257,1},{2,258},{258,2},{3,259},{259,3},{4... | collective-permute-start | bytes 147464 | tf_op jit(solution)/shard_map/ppermute | solution.py:313
  19.9 6.1 %collective-permute-done.share_ref = bf16[16,1536]{1,0:T(8,128)(2,1)S(1)} collective-permute-done((bf16[16,1536]{1,0:T(8,128)(2,1)S(1)}, bf16[16,1536]{1,0:T(8,128)(2,1)S(1)}, u32[]{:S(2)}, u32[]{:S(2)}) %collective-permute-start) | collective-permute-done | bytes 49184 | tf_op jit(solution)/shard_map/ppermute | solution.py:313
  26.7 2.0 %shard_map.59 = bf16[8,16,2688]{2,1,0:T(8,128)(2,1)} custom-call(f32[16,16,128]{2,1,0:T(8,128)} %copy-done.4, bf16[16,1024]{1,0:T(8,128)(2,1)} %get-tuple-element.35.right_ref, bf16[16,1536]{1,0:T(8,128)(2,1)} %copy-done.9), custom_call_target="tpu_custom_call" | custom-call | flops 1048576 | bytes 1048576 | tf_op jit(solution)/shard_map/pallas_call | solution.py:73
  28.7 7.9 %all-to-all-start.1 = ((bf16[8,16,2688]{2,1,0:T(8,128)(2,1)}), bf16[8,16,2688]{2,1,0:T(8,128)(2,1)}, u32[]{:S(2)}, u32[]{:S(2)}) async-start(bf16[8,16,2688]{2,1,0:T(8,128)(2,1)} %shard_map.59), calls=%async_computation.1 | async-start | bytes 1376256 | tf_op jit(solution)/shard_map/all_to_all | solution.py:329
  36.7 6.5 %shard_map.60 = (bf16[64,1024]{1,0:T(8,128)(2,1)}, bf16[64,1024]{1,0:T(8,128)(2,1)}, bf16[64,1024]{1,0:T(8,128)(2,1)}, bf16[64,1024]{1,0:T(8,128)(2,1)}) custom-call(s32[5]{0:T(128)} %stack.23.place, bf16[128,3072]{1,0:T(8,128)(2,1)} %grads_hbm.1, bf16[2048,768]{1,0:T(8,128)(2,1)} %bitcast.8, bf16[2048,768]{1,0:T(8,128)(2,1)} %bitcast.9, ...), custom_call_target="tpu_custom_call" | custom-call | flops 805306368 | bytes 7340032 | tf_op jit(solution)/shard_map/pallas_call | solution.py:132
  43.2 4.8 %collective-permute-start.2 = (bf16[64,1024]{1,0:T(8,128)(2,1)}, bf16[64,1024]{1,0:T(8,128)(2,1)S(1)}, u32[]{:S(2)}, u32[]{:S(2)}) collective-permute-start(bf16[64,1024]{1,0:T(8,128)(2,1)} %get-tuple-element.41), channel_id=1, source_target_pairs={{0,2},{1,3},{2,0},{3,1},{4,6},{5,7},{6,4},{7,5},{8,10},{9,11},{10,... | collective-permute-start | bytes 393224 | tf_op jit(solution)/shard_map/ppermute | solution.py:317
  48.0 2.2 %collective-permute-start.3 = (bf16[64,1024]{1,0:T(8,128)(2,1)}, bf16[64,1024]{1,0:T(8,128)(2,1)S(1)}, u32[]{:S(2)}, u32[]{:S(2)}) collective-permute-start(bf16[64,1024]{1,0:T(8,128)(2,1)} %get-tuple-element.42), channel_id=1, source_target_pairs={{0,1},{1,0},{2,3},{3,2},{4,5},{5,4},{6,7},{7,6},{8,9},{9,8},{10,11... | collective-permute-start | bytes 393224 | tf_op jit(solution)/shard_map/ppermute | solution.py:317
  50.2 2.5 %collective-permute-start.4 = (bf16[64,1024]{1,0:T(8,128)(2,1)}, bf16[64,1024]{1,0:T(8,128)(2,1)S(1)}, u32[]{:S(2)}, u32[]{:S(2)}) collective-permute-start(bf16[64,1024]{1,0:T(8,128)(2,1)} %get-tuple-element.43), channel_id=1, source_target_pairs={{0,3},{1,2},{2,1},{3,0},{4,7},{5,6},{6,5},{7,4},{8,11},{9,10},{10,... | collective-permute-start | bytes 393224 | tf_op jit(solution)/shard_map/ppermute | solution.py:317
  52.7 2.0 %collective-permute-done.3.near2_ref = bf16[64,1024]{1,0:T(8,128)(2,1)S(1)} collective-permute-done((bf16[64,1024]{1,0:T(8,128)(2,1)}, bf16[64,1024]{1,0:T(8,128)(2,1)S(1)}, u32[]{:S(2)}, u32[]{:S(2)}) %collective-permute-start.3) | collective-permute-done | bytes 131104 | tf_op jit(solution)/shard_map/ppermute | solution.py:317
  54.7 3.0 %collective-permute-done.4.near3_ref = bf16[64,1024]{1,0:T(8,128)(2,1)S(1)} collective-permute-done((bf16[64,1024]{1,0:T(8,128)(2,1)}, bf16[64,1024]{1,0:T(8,128)(2,1)S(1)}, u32[]{:S(2)}, u32[]{:S(2)}) %collective-permute-start.4) | collective-permute-done | bytes 131104 | tf_op jit(solution)/shard_map/ppermute | solution.py:317
  57.7 6.3 %shard_map.61 = (f32[64,4096]{1,0:T(8,128)}, f32[64,4096]{1,0:T(8,128)}) custom-call(s32[5]{0:T(128)} %stack.23.place, bf16[8,16,2688]{2,1,0:T(8,128)(2,1)} %all-to-all-done.1.got_ref.tokens_ref, bf16[128,2048]{1,0:T(8,128)(2,1)} %acts_hbm.1, bf16[128,3072]{1,0:T(8,128)(2,1)} %grads_hbm.1), custom_call_target="tpu_custom_call" | custom-call | flops 1048576000 | bytes 5242880 | tf_op jit(solution)/shard_map/pallas_call | solution.py:245
  64.0 5.2 %collective-permute-start.5 = (f32[64,4096]{1,0:T(8,128)}, f32[64,4096]{1,0:T(8,128)S(1)}, u32[]{:S(2)}, u32[]{:S(2)}) collective-permute-start(f32[64,4096]{1,0:T(8,128)} %get-tuple-element.50), channel_id=1, source_target_pairs={{0,128},{128,0},{1,129},{129,1},{2,130},{130,2},{3,131},{131,3},{4... | collective-permute-start | bytes 3145736 | tf_op jit(solution)/shard_map/ppermute | solution.py:313
  69.2 6.5 %shard_map.62 = bf16[4,64,1024]{2,1,0:T(8,128)(2,1)} custom-call(s32[5]{0:T(128)} %stack.23.place, bf16[8,16,2688]{2,1,0:T(8,128)(2,1)} %all-to-all-done.1.got_ref.tokens_ref, bf16[2048,768]{1,0:T(8,128)(2,1)} %bitcast.10, bf16[2048,768]{1,0:T(8,128)(2,1)} %bitcast.11, bf16[2048,768]{1,0:T(8,128)(2,1)} %copy-done, bf16[2048,768]{1,0:T(8,128)(2,1)} %copy-done), custom_call_target="tpu_custom_call" | custom-call | flops 805306368 | bytes 7340032 | tf_op jit(solution)/shard_map/pallas_call | solution.py:132
  76.7 2.5 %shard_map.63 = (f32[32,4096]{1,0:T(8,128)}, bf16[32,4096]{1,0:T(8,128)(2,1)}) custom-call(f32[64,4096]{1,0:T(8,128)} %get-tuple-element.53.keep_ref, f32[64,4096]{1,0:T(8,128)} %copy-done.2), custom_call_target="tpu_custom_call" | custom-call | flops 262144 | bytes 3145728 | tf_op jit(solution)/shard_map/pallas_call | solution.py:269
  79.2 3.5 %all-to-all-start.2 = ((bf16[4,64,1024]{2,1,0:T(8,128)(2,1)}), bf16[4,64,1024]{2,1,0:T(8,128)(2,1)S(1)}, u32[]{:S(2)}, u32[]{:S(2)}) async-start(bf16[4,64,1024]{2,1,0:T(8,128)(2,1)} %shard_map.62), calls=%async_computation.2 | async-start | bytes 1048576 | tf_op jit(solution)/shard_map/all_to_all | solution.py:341
  82.6 4.7 %collective-permute-start.6 = (bf16[32,4096]{1,0:T(8,128)(2,1)}, bf16[32,4096]{1,0:T(8,128)(2,1)S(1)}, u32[]{:S(2)}, u32[]{:S(2)}) collective-permute-start(bf16[32,4096]{1,0:T(8,128)(2,1)} %get-tuple-element.57), channel_id=1, source_target_pairs={{0,256},{256,0},{1,257},{257,1},{2,258},{258,2},{3,259},{259,3},{4... | collective-permute-start | bytes 786440 | tf_op jit(solution)/shard_map/ppermute | solution.py:313
  87.4 4.9 %all-to-all-done.2.far_ref = bf16[4,64,1024]{2,1,0:T(8,128)(2,1)S(1)} async-done(((bf16[4,64,1024]{2,1,0:T(8,128)(2,1)}), bf16[4,64,1024]{2,1,0:T(8,128)(2,1)S(1)}, u32[]{:S(2)}, u32[]{:S(2)}) %all-to-all-start.2) | async-done | bytes 524320 | tf_op jit(solution)/shard_map/all_to_all | solution.py:341
  93.1 2.2 %shard_map.64 = bf16[2,64,1024]{2,1,0:T(8,128)(2,1)} custom-call(s32[5]{0:T(128)} %stack.23.place, bf16[64,1024]{1,0:T(8,128)(2,1)} %get-tuple-element.44.own_ref, bf16[64,1024]{1,0:T(8,128)(2,1)} %copy-done.6, bf16[64,1024]{1,0:T(8,128)(2,1)} %copy-done.7, bf16[64,1024]{1,0:T(8,128)(2,1)} %copy-done.8, bf16[4,64,1024]{2,1,0:T(8,128)(2,1)} %copy-done.1), custom_call_target="tpu_custom_call" | custom-call | flops 524288 | bytes 2097152 | tf_op jit(solution)/shard_map/pallas_call | solution.py:161
  96.7 10.4 %all-to-all-start.3 = ((bf16[8,16,1024]{2,1,0:T(8,128)(2,1)}), bf16[8,16,1024]{2,1,0:T(8,128)(2,1)S(1)}, u32[]{:S(2)}, u32[]{:S(2)}) async-start(bf16[8,16,1024]{2,1,0:T(8,128)(2,1)} %bitcast.12), calls=%async_computation.3 | async-start | bytes 524288 | tf_op jit(solution)/shard_map/all_to_all | solution.py:346
  107.1 1.9 %shard_map.66 = (f32[16,2048]{1,0:T(8,128)}, f32[32,3072]{1,0:T(8,128)}) custom-call(f32[32,4096]{1,0:T(8,128)} %get-tuple-element.59.near_ref, bf16[32,4096]{1,0:T(8,128)(2,1)} %copy-done.5), custom_call_target="tpu_custom_call" | custom-call | flops 131072 | bytes 2097152 | tf_op jit(solution)/shard_map/pallas_call | solution.py:292
  109.0 8.9 %all-to-all-done.3.got_ref = bf16[8,16,1024]{2,1,0:T(8,128)(2,1)S(1)} async-done(((bf16[8,16,1024]{2,1,0:T(8,128)(2,1)}), bf16[8,16,1024]{2,1,0:T(8,128)(2,1)S(1)}, u32[]{:S(2)}, u32[]{:S(2)}) %all-to-all-start.3) | async-done | bytes 262176 | tf_op jit(solution)/shard_map/all_to_all | solution.py:346
  (29 shorter events, 7.7 us)
Async XLA Ops:
  0.6 25.4 %collective-permute-start.1 = (bf16[2048,768]{1,0:T(8,128)(2,1)}, bf16[2048,768]{1,0:T(8,128)(2,1)S(1)}, u32[]{:S(2)}, u32[]{:S(2)}) collective-permute-start(bf16[2048,768]{1,0:T(8,128)(2,1)} %bitcast.7), channel_id=1, source_target_pairs={{0,128},{128,0},{1,129},{129,1},{2,130},{130,2},{3,131},{131,3},{4... | collective-permute-start | bytes 9437192 | tf_op jit(solution)/shard_map/ppermute | solution.py:313
  12.5 13.5 %all-to-all-start = ((f32[16,16,128]{2,1,0:T(8,128)}), f32[16,16,128]{2,1,0:T(8,128)S(1)}, u32[]{:S(2)}, u32[]{:S(2)}) async-start(f32[16,16,128]{2,1,0:T(8,128)} %get-tuple-element.33), calls=%async_computation | async-start | bytes 262144 | tf_op jit(solution)/shard_map/all_to_all | solution.py:324
  16.9 9.2 %collective-permute-start = (bf16[16,1536]{1,0:T(8,128)(2,1)S(1)}, bf16[16,1536]{1,0:T(8,128)(2,1)S(1)}, u32[]{:S(2)}, u32[]{:S(2)}) collective-permute-start(bf16[16,1536]{1,0:T(8,128)(2,1)S(1)} %dynamic_slice.3), channel_id=1, source_target_pairs={{0,256},{256,0},{1,257},{257,1},{2,258},{258,2},{3,259},{259,3},{4... | collective-permute-start | bytes 147464 | tf_op jit(solution)/shard_map/ppermute | solution.py:313
  26.0 0.6 copy-start.9
  26.0 0.7 copy-start.4
  26.0 10.6 %copy-start = (bf16[2048,768]{1,0:T(8,128)(2,1)}, bf16[2048,768]{1,0:T(8,128)(2,1)S(1)}, u32[]{:S(2)}) copy-start(bf16[2048,768]{1,0:T(8,128)(2,1)S(1)} %collective-permute-done.1.far_lo.far_hi) | copy-start | bytes 9437188
  28.7 29.0 %all-to-all-start.1 = ((bf16[8,16,2688]{2,1,0:T(8,128)(2,1)}), bf16[8,16,2688]{2,1,0:T(8,128)(2,1)}, u32[]{:S(2)}, u32[]{:S(2)}) async-start(bf16[8,16,2688]{2,1,0:T(8,128)(2,1)} %shard_map.59), calls=%async_computation.1 | async-start | bytes 1376256 | tf_op jit(solution)/shard_map/all_to_all | solution.py:329
  43.2 9.5 %collective-permute-start.2 = (bf16[64,1024]{1,0:T(8,128)(2,1)}, bf16[64,1024]{1,0:T(8,128)(2,1)S(1)}, u32[]{:S(2)}, u32[]{:S(2)}) collective-permute-start(bf16[64,1024]{1,0:T(8,128)(2,1)} %get-tuple-element.41), channel_id=1, source_target_pairs={{0,2},{1,3},{2,0},{3,1},{4,6},{5,7},{6,4},{7,5},{8,10},{9,11},{10,... | collective-permute-start | bytes 393224 | tf_op jit(solution)/shard_map/ppermute | solution.py:317
  48.0 6.7 %collective-permute-start.3 = (bf16[64,1024]{1,0:T(8,128)(2,1)}, bf16[64,1024]{1,0:T(8,128)(2,1)S(1)}, u32[]{:S(2)}, u32[]{:S(2)}) collective-permute-start(bf16[64,1024]{1,0:T(8,128)(2,1)} %get-tuple-element.42), channel_id=1, source_target_pairs={{0,1},{1,0},{2,3},{3,2},{4,5},{5,4},{6,7},{7,6},{8,9},{9,8},{10,11... | collective-permute-start | bytes 393224 | tf_op jit(solution)/shard_map/ppermute | solution.py:317
  50.2 7.5 %collective-permute-start.4 = (bf16[64,1024]{1,0:T(8,128)(2,1)}, bf16[64,1024]{1,0:T(8,128)(2,1)S(1)}, u32[]{:S(2)}, u32[]{:S(2)}) collective-permute-start(bf16[64,1024]{1,0:T(8,128)(2,1)} %get-tuple-element.43), channel_id=1, source_target_pairs={{0,3},{1,2},{2,1},{3,0},{4,7},{5,6},{6,5},{7,4},{8,11},{9,10},{10,... | collective-permute-start | bytes 393224 | tf_op jit(solution)/shard_map/ppermute | solution.py:317
  52.7 23.0 %copy-start.6 = (bf16[64,1024]{1,0:T(8,128)(2,1)}, bf16[64,1024]{1,0:T(8,128)(2,1)S(1)}, u32[]{:S(2)}) copy-start(bf16[64,1024]{1,0:T(8,128)(2,1)S(1)} %collective-permute-done.2.near1_ref) | copy-start | bytes 393220
  54.7 21.0 %copy-start.7 = (bf16[64,1024]{1,0:T(8,128)(2,1)}, bf16[64,1024]{1,0:T(8,128)(2,1)S(1)}, u32[]{:S(2)}) copy-start(bf16[64,1024]{1,0:T(8,128)(2,1)S(1)} %collective-permute-done.3.near2_ref) | copy-start | bytes 393220
  57.7 18.0 %copy-start.8 = (bf16[64,1024]{1,0:T(8,128)(2,1)}, bf16[64,1024]{1,0:T(8,128)(2,1)S(1)}, u32[]{:S(2)}) copy-start(bf16[64,1024]{1,0:T(8,128)(2,1)S(1)} %collective-permute-done.4.near3_ref) | copy-start | bytes 393220
  64.0 11.7 %collective-permute-start.5 = (f32[64,4096]{1,0:T(8,128)}, f32[64,4096]{1,0:T(8,128)S(1)}, u32[]{:S(2)}, u32[]{:S(2)}) collective-permute-start(f32[64,4096]{1,0:T(8,128)} %get-tuple-element.50), channel_id=1, source_target_pairs={{0,128},{128,0},{1,129},{129,1},{2,130},{130,2},{3,131},{131,3},{4... | collective-permute-start | bytes 3145736 | tf_op jit(solution)/shard_map/ppermute | solution.py:313
  75.7 1.0 copy-start.2
  79.2 13.1 %all-to-all-start.2 = ((bf16[4,64,1024]{2,1,0:T(8,128)(2,1)}), bf16[4,64,1024]{2,1,0:T(8,128)(2,1)S(1)}, u32[]{:S(2)}, u32[]{:S(2)}) async-start(bf16[4,64,1024]{2,1,0:T(8,128)(2,1)} %shard_map.62), calls=%async_computation.2 | async-start | bytes 1048576 | tf_op jit(solution)/shard_map/all_to_all | solution.py:341
  82.6 14.0 %collective-permute-start.6 = (bf16[32,4096]{1,0:T(8,128)(2,1)}, bf16[32,4096]{1,0:T(8,128)(2,1)S(1)}, u32[]{:S(2)}, u32[]{:S(2)}) collective-permute-start(bf16[32,4096]{1,0:T(8,128)(2,1)} %get-tuple-element.57), channel_id=1, source_target_pairs={{0,256},{256,0},{1,257},{257,1},{2,258},{258,2},{3,259},{259,3},{4... | collective-permute-start | bytes 786440 | tf_op jit(solution)/shard_map/ppermute | solution.py:313
  92.2 0.8 copy-start.1
  96.7 10.4 %copy-start.5 = (bf16[32,4096]{1,0:T(8,128)(2,1)}, bf16[32,4096]{1,0:T(8,128)(2,1)S(1)}, u32[]{:S(2)}) copy-start(bf16[32,4096]{1,0:T(8,128)(2,1)S(1)} %collective-permute-done.6.far_ref) | copy-start | bytes 786436
  96.7 21.2 %all-to-all-start.3 = ((bf16[8,16,1024]{2,1,0:T(8,128)(2,1)}), bf16[8,16,1024]{2,1,0:T(8,128)(2,1)S(1)}, u32[]{:S(2)}, u32[]{:S(2)}) async-start(bf16[8,16,1024]{2,1,0:T(8,128)(2,1)} %bitcast.12), calls=%async_computation.3 | async-start | bytes 524288 | tf_op jit(solution)/shard_map/all_to_all | solution.py:346
  117.9 0.7 copy-start.3

commit v5 on v4

--- a/solution.py
+++ b/solution.py
@@ -101,7 +101,7 @@
     high[...] = dot(near_hi, far_hi)
     for r in range(4):
         for y in range(4):
-            x = place[4] ^ r if len(outs) == 4 else r
+            x = (place[3] & 3) ^ r if len(outs) == 4 else r
             rows = pl.ds(pl.multiple_of((y * 4 + x) * 8, 8), 8)
             pair = jnp.concatenate([low[rows, :], high[rows, :]], axis=0).astype(BF)
             if len(outs) == 4:
@@ -139,7 +139,7 @@
             out_specs=out_specs,
             scratch_shapes=[pltpu.VMEM((count, step), F32)] * 2,
         ),
-        compiler_params=params(60),
+        compiler_params=params(16),
         cost_estimate=cost(4 * count * features * quarter, 7 * MB),
     )(place, tokens, weight, weight, weight_far, weight_far)
 
@@ -182,7 +182,7 @@
         out_shape=jax.ShapeDtypeStruct((8, 2 * width), BF),
         in_specs=[pl.BlockSpec(memory_space=pltpu.VMEM)],
         out_specs=pl.BlockSpec(memory_space=pltpu.VMEM),
-        compiler_params=params(60),
+        compiler_params=params(16),
         cost_estimate=cost(128 * width, MB // 2),
     )(got)
 
@@ -252,7 +252,7 @@
             pltpu.VMEM(grads.shape, BF),
             pltpu.SemaphoreType.DMA(((acts.shape[1] + grads.shape[1]) // BLOCK,)),
         ],
-        compiler_params=params(60),
+        compiler_params=params(16),
         cost_estimate=cost(1000 * MB, 5 * MB),
     )(place, got, acts, grads)
 
@@ -274,7 +274,7 @@
         ),
         in_specs=[vmem, vmem],
         out_specs=[vmem, vmem],
-        compiler_params=params(60),
+        compiler_params=params(16),
         cost_estimate=cost(rows * width, 3 * MB),
     )(keep, got)
 
@@ -297,7 +297,7 @@
         ),
         in_specs=[vmem, vmem],
         out_specs=[vmem, vmem],
-        compiler_params=params(60),
+        compiler_params=params(16),
         cost_estimate=cost(32 * 4096, 2 * MB),
     )(near, far)
 
@@ -307,7 +307,7 @@
     width = acts.shape[1]
     hidden = grad_out.shape[1]
     yh, core, row, yl, xx = (lax.axis_index(n) for n in ("yh", "core", "row", "yl", "x"))
-    place = jnp.stack([yh, core, row, yl * 4 + xx, xx]).astype(jnp.int32)
+    place = jnp.stack([yh, core, row, yl * 4 + xx]).astype(jnp.int32)
 
     def swap(value, axis):
         return lax.ppermute(value, axis, [(0, 1), (1, 0)])
@@ -321,6 +321,7 @@
     share = lax.dynamic_slice(grad_out, (row * 16, (1 - yh) * (hidden // 2)), (16, hidden // 2))
     share = swap(share, "yh")
     left_part, right_part = prepare(place, acts, grad_out, 16, 8)
+    left_part, share = barrier((left_part, share))
     left_rows = lax.all_to_all(left_part, ("yl", "x"), 0, 0, tiled=True)
     weight_far = swap(weight, "core")
 
@@ -328,16 +329,13 @@
     packed, near_tokens = barrier((pack(left_rows, right_part, share, 8), grad_out))
     got = lax.all_to_all(packed, "row", 0, 0, tiled=True)
     near = to_x_peers(product(place, near_tokens, weight, weight_far, True))
-    got, near = barrier((got, near))
+    got, near[0], near[1], near[2] = barrier((got, near[0], near[1], near[2]))
 
     keep, send = stats(place, got, acts, grad_out)
-    send, far_tokens = barrier((send, got))
-    back = swap(send, "core")
+    near_rows, far_rows = core_sum(keep, swap(send, "core"))
+    far_tokens, far_rows = barrier((got, far_rows))
+    far_rows = swap(far_rows, "yh")
     far = product(place, far_tokens, weight, weight_far, False)
-    back, far = barrier((back, far))
-    near_rows, far_rows = core_sum(keep, back)
-    far, far_rows = barrier((far, far_rows))
-    far_rows = swap(far_rows, "yh")
     far = lax.all_to_all(far, "x", 0, 0, tiled=True)
 
     chunks = x_sum(place, near, far)

time: 122 us -> 122 us (level)
  blocking collectives: 0 us -> 12 us
  Pallas kernels: 31.8 us -> 22.1 us
  starting transfers between devices: 56.5 us -> 47.6 us
  local copies, waits for them, and re-layouts: 4.65 us -> 8.53 us
  waiting for transfers between devices: 26.3 us -> 28.5 us
    all_to_all x0 -> x1, blocking collectives: none -> 12 us  [body(): left_rows = lax.all_to_all(left_part, ('yl', 'x'), 0, 0, tiled=True)]
    all_to_all x1, starting transfers between devices: 10.4 us -> 5.27 us  [body(): input_grad = y_sum(lax.all_to_all(chunks, ('yh', 'yl'), 0, 0, tiled=True))]
    all_to_all x1, waiting for transfers between devices: 4.86 us -> 0.01 us  [body(): far = lax.all_to_all(far, 'x', 0, 0, tiled=True)]
    unnamed x20 -> x26, local copies, waits for them, and re-layouts: 3.16 us -> 7.72 us
    all_to_all x1 -> x0, starting transfers between devices: 3.51 us -> none  [body(): left_rows = lax.all_to_all(left_part, ('yl', 'x'), 0, 0, tiled=True)]
    all_to_all x1, waiting for transfers between devices: 0.01 us -> 3.09 us  [body(): got = lax.all_to_all(packed, 'row', 0, 0, tiled=True)]
    pallas_call x2, Pallas kernels: 12.9 us -> 9.95 us  [product(): pl.pallas_call(product_kernel, out_shape=shape, grid_spec=pltpu.PrefetchS...]
    pallas_call x1, Pallas kernels: 2.47 us -> 0.1 us  [core_sum(): pl.pallas_call(core_sum_kernel, out_shape=(jax.ShapeDtypeStruct((rows //...]
  transfers between devices with their start and end apart: 11 -> 10, of which waited for: 6 -> 8; matrix products, arithmetic and copies ran while one was open for 1% -> 1% of each run, Pallas kernels for 16% -> 9%
where the time goes in v5:
time: 122 us; the launch traced here: 120 us
  starting transfers between devices  47.6 us (39%)
  waiting for transfers between devices  28.5 us (23%)
  Pallas kernels  22.1 us (18%)
  blocking collectives  12 us (10%)
  local copies, waits for them, and re-layouts  8.53 us (7%)
    ppermute x4, starting transfers between devices, swap(): return lax.ppermute(value, axis, [(0, 1), (1, 0)])  21.4 us
    all_to_all x1, blocking collectives, body(): left_rows = lax.all_to_all(left_part, ('yl', 'x'), 0, 0, tiled=True)  12 us
    pallas_call x2, Pallas kernels, product(): pl.pallas_call(product_kernel, out_shape=shape, grid_spec=pltpu.PrefetchS...  9.95 us
    all_to_all x1, waiting for transfers between devices, body(): input_grad = y_sum(lax.all_to_all(chunks, ('yh', 'yl'), 0, 0, tiled=True))  9.83 us
    ppermute x3, starting transfers between devices, to_x_peers(): lax.ppermute(parts[r], 'x', [(i, i ^ r) for i in range(4)])  9.13 us
    ppermute x4, waiting for transfers between devices, swap(): return lax.ppermute(value, axis, [(0, 1), (1, 0)])  8.5 us
    all_to_all x1, starting transfers between devices, body(): got = lax.all_to_all(packed, 'row', 0, 0, tiled=True)  8.11 us
    unnamed x26, local copies, waits for them, and re-layouts  7.72 us
  transfers between devices with their start and end apart: 10, of which 8 were waited for; matrix products, arithmetic and copies ran while one was open for 1% of the time, Pallas kernels for 9%

profile of v5, /device:TPU:1, one launch (start us, length us, event | category | flops | bytes accessed | tf_op | source)
XLA Modules:
  0.0 120.0 jit_solution(5425898468062573983)
XLA Ops:
  0.6 9.1 %collective-permute-start.1 = (bf16[2048,768]{1,0:T(8,128)(2,1)}, bf16[2048,768]{1,0:T(8,128)(2,1)}, u32[]{:S(2)}, u32[]{:S(2)}) collective-permute-start(bf16[2048,768]{1,0:T(8,128)(2,1)} %bitcast.6), channel_id=1, source_target_pairs={{0,128},{128,0},{1,129},{129,1},{2,130},{130,2},{3,131},{131,3},{4... | collective-permute-start | bytes 9437192 | tf_op jit(solution)/shard_map/ppermute | solution.py:313
  10.5 2.1 %collective-permute-start = (bf16[16,1536]{1,0:T(8,128)(2,1)S(1)}, bf16[16,1536]{1,0:T(8,128)(2,1)S(1)}, u32[]{:S(2)}, u32[]{:S(2)}) collective-permute-start(bf16[16,1536]{1,0:T(8,128)(2,1)S(1)} %dynamic_slice.3), channel_id=1, source_target_pairs={{0,256},{256,0},{1,257},{257,1},{2,258},{258,2},{3,259},{259,3},{4... | collective-permute-start | bytes 147464 | tf_op jit(solution)/shard_map/ppermute | solution.py:313
  13.2 2.4 %shard_map.58 = (f32[16,16,128]{2,1,0:T(8,128)}, bf16[16,1024]{1,0:T(8,128)(2,1)}) custom-call(s32[4]{0:T(128)} %pad_add_fusion.place, bf16[128,2048]{1,0:T(8,128)(2,1)} %acts_hbm.1, bf16[128,3072]{1,0:T(8,128)(2,1)} %grads_hbm.1), custom_call_target="tpu_custom_call" | custom-call | flops 167772160 | bytes 3145728 | tf_op jit(solution)/shard_map/pallas_call | solution.py:44
  15.7 4.0 %collective-permute-done.share_ref = bf16[16,1536]{1,0:T(8,128)(2,1)S(1)} collective-permute-done((bf16[16,1536]{1,0:T(8,128)(2,1)S(1)}, bf16[16,1536]{1,0:T(8,128)(2,1)S(1)}, u32[]{:S(2)}, u32[]{:S(2)}) %collective-permute-start) | collective-permute-done | bytes 49184 | tf_op jit(solution)/shard_map/ppermute | solution.py:313
  19.7 12.0 %all_to_all.20.left_ref = f32[16,16,128]{2,1,0:T(8,128)} all-to-all(f32[16,16,128]{2,1,0:T(8,128)} %get-tuple-element.31), channel_id=1, replica_groups=mesh['yh'=2,'core'=2,'row'=8,'yl'=4,'x'=4] {'yl','x'}, dimensions={0} | all-to-all | bytes 262144 | tf_op jit(solution)/shard_map/all_to_all | solution.py:325
  31.6 1.8 %shard_map.59 = bf16[8,16,2688]{2,1,0:T(8,128)(2,1)} custom-call(f32[16,16,128]{2,1,0:T(8,128)} %all_to_all.20.left_ref, bf16[16,1024]{1,0:T(8,128)(2,1)} %get-tuple-element.34.right_ref, bf16[16,1536]{1,0:T(8,128)(2,1)} %copy-done.12), custom_call_target="tpu_custom_call" | custom-call | flops 1048576 | bytes 1048576 | tf_op jit(solution)/shard_map/pallas_call | solution.py:73
  33.5 8.1 %all-to-all-start.1 = ((bf16[8,16,2688]{2,1,0:T(8,128)(2,1)}), bf16[8,16,2688]{2,1,0:T(8,128)(2,1)}, u32[]{:S(2)}, u32[]{:S(2)}) async-start(bf16[8,16,2688]{2,1,0:T(8,128)(2,1)} %shard_map.59), calls=%async_computation.1 | async-start | bytes 1376256 | tf_op jit(solution)/shard_map/all_to_all | solution.py:330
  42.7 5.0 %shard_map.60 = (bf16[64,1024]{1,0:T(8,128)(2,1)S(1)}, bf16[64,1024]{1,0:T(8,128)(2,1)S(1)}, bf16[64,1024]{1,0:T(8,128)(2,1)S(1)}, bf16[64,1024]{1,0:T(8,128)(2,1)S(1)}) custom-call(s32[4]{0:T(128)S(1)} %copy-done.8, bf16[128,3072]{1,0:T(8,128)(2,1)S(1)} %copy-done.1, bf16[2048,768]{1,0:T(8,128)(2,1)S(1)} %bitcast.7, bf16[2048,768]{1,0:T(8,128)(2,1)S(1)} %bitcast.8, ...), custom_call_target="tpu_custom_call" | custom-call | flops 805306368 | bytes 7340032 | tf_op jit(solution)/shard_map/pallas_call | solution.py:132
  48.4 2.7 %collective-permute-start.2 = (bf16[64,1024]{1,0:T(8,128)(2,1)S(1)}, bf16[64,1024]{1,0:T(8,128)(2,1)S(1)}, u32[]{:S(2)}, u32[]{:S(2)}) collective-permute-start(bf16[64,1024]{1,0:T(8,128)(2,1)S(1)} %get-tuple-element.40), channel_id=1, source_target_pairs={{0,2},{1,3},{2,0},{3,1},{4,6},{5,7},{6,4},{7,5},{8,10},{9,11},{10,... | collective-permute-start | bytes 393224 | tf_op jit(solution)/shard_map/ppermute | solution.py:317
  51.0 1.9 %collective-permute-start.3 = (bf16[64,1024]{1,0:T(8,128)(2,1)S(1)}, bf16[64,1024]{1,0:T(8,128)(2,1)}, u32[]{:S(2)}, u32[]{:S(2)}) collective-permute-start(bf16[64,1024]{1,0:T(8,128)(2,1)S(1)} %get-tuple-element.41), channel_id=1, source_target_pairs={{0,1},{1,0},{2,3},{3,2},{4,5},{5,4},{6,7},{7,6},{8,9},{9,8},{10,11... | collective-permute-start | bytes 393224 | tf_op jit(solution)/shard_map/ppermute | solution.py:317
  53.0 3.0 %collective-permute-done.2.near1_ref = bf16[64,1024]{1,0:T(8,128)(2,1)S(1)} collective-permute-done((bf16[64,1024]{1,0:T(8,128)(2,1)S(1)}, bf16[64,1024]{1,0:T(8,128)(2,1)S(1)}, u32[]{:S(2)}, u32[]{:S(2)}) %collective-permute-start.2) | collective-permute-done | bytes 131104 | tf_op jit(solution)/shard_map/ppermute | solution.py:317
  57.7 3.1 %all-to-all-done.1.got_ref.tokens_ref = bf16[8,16,2688]{2,1,0:T(8,128)(2,1)} async-done(((bf16[8,16,2688]{2,1,0:T(8,128)(2,1)}), bf16[8,16,2688]{2,1,0:T(8,128)(2,1)}, u32[]{:S(2)}, u32[]{:S(2)}) %all-to-all-start.1) | async-done | bytes 688160 | tf_op jit(solution)/shard_map/all_to_all | solution.py:330
  63.0 4.1 %shard_map.61 = (f32[64,4096]{1,0:T(8,128)S(1)}, f32[64,4096]{1,0:T(8,128)S(1)}) custom-call(s32[4]{0:T(128)S(1)} %copy-done.8, bf16[8,16,2688]{2,1,0:T(8,128)(2,1)} %all-to-all-done.1.got_ref.tokens_ref, bf16[128,2048]{1,0:T(8,128)(2,1)S(1)} %copy-done.4, bf16[128,3072]{1,0:T(8,128)(2,1)S(1)} %copy-done.2), custom_call_target="tpu_custom_call" | custom-call | flops 1048576000 | bytes 5242880 | tf_op jit(solution)/shard_map/pallas_call | solution.py:245
  67.1 4.7 %collective-permute-start.5 = (f32[64,4096]{1,0:T(8,128)S(1)}, f32[64,4096]{1,0:T(8,128)S(1)}, u32[]{:S(2)}, u32[]{:S(2)}) collective-permute-start(f32[64,4096]{1,0:T(8,128)S(1)} %get-tuple-element.48), channel_id=1, source_target_pairs={{0,128},{128,0},{1,129},{129,1},{2,130},{130,2},{3,131},{131,3},{4... | collective-permute-start | bytes 3145736 | tf_op jit(solution)/shard_map/ppermute | solution.py:313
  71.9 2.3 %collective-permute-done.5.got_ref = f32[64,4096]{1,0:T(8,128)S(1)} collective-permute-done((f32[64,4096]{1,0:T(8,128)S(1)}, f32[64,4096]{1,0:T(8,128)S(1)}, u32[]{:S(2)}, u32[]{:S(2)}) %collective-permute-start.5) | collective-permute-done | bytes 1048608 | tf_op jit(solution)/shard_map/ppermute | solution.py:313
  75.0 5.0 %shard_map.63 = bf16[4,64,1024]{2,1,0:T(8,128)(2,1)S(1)} custom-call(s32[4]{0:T(128)S(1)} %copy-done.8, bf16[8,16,2688]{2,1,0:T(8,128)(2,1)} %all-to-all-done.1.got_ref.tokens_ref, bf16[2048,768]{1,0:T(8,128)(2,1)S(1)} %bitcast.9, bf16[2048,768]{1,0:T(8,128)(2,1)S(1)} %bitcast.10, bf16[2048,768]{1,0:T(8,128)(2,1)} %collective-permute-done.1.far_lo.far_hi, ...), custom_call_target="tpu_custom_call" | custom-call | flops 805306368 | bytes 7340032 | tf_op jit(solution)/shard_map/pallas_call | solution.py:132
  80.9 3.6 %all-to-all-start.2 = ((bf16[4,64,1024]{2,1,0:T(8,128)(2,1)}), bf16[4,64,1024]{2,1,0:T(8,128)(2,1)S(1)}, u32[]{:S(2)}, u32[]{:S(2)}) async-start(bf16[4,64,1024]{2,1,0:T(8,128)(2,1)} %copy-done.3), calls=%async_computation.2 | async-start | bytes 1048576 | tf_op jit(solution)/shard_map/all_to_all | solution.py:339
  84.5 5.6 %collective-permute-start.6 = (bf16[32,4096]{1,0:T(8,128)(2,1)S(1)}, bf16[32,4096]{1,0:T(8,128)(2,1)S(1)}, u32[]{:S(2)}, u32[]{:S(2)}) collective-permute-start(bf16[32,4096]{1,0:T(8,128)(2,1)S(1)} %get-tuple-element.51), channel_id=1, source_target_pairs={{0,256},{256,0},{1,257},{257,1},{2,258},{258,2},{3,259},{259,3},{4... | collective-permute-start | bytes 786440 | tf_op jit(solution)/shard_map/ppermute | solution.py:313
  90.1 4.5 %collective-permute-start.4 = (bf16[64,1024]{1,0:T(8,128)(2,1)S(1)}, bf16[64,1024]{1,0:T(8,128)(2,1)S(1)}, u32[]{:S(2)}, u32[]{:S(2)}) collective-permute-start(bf16[64,1024]{1,0:T(8,128)(2,1)S(1)} %get-tuple-element.45), channel_id=1, source_target_pairs={{0,3},{1,2},{2,1},{3,0},{4,7},{5,6},{6,5},{7,4},{8,11},{9,10},{10,... | collective-permute-start | bytes 393224 | tf_op jit(solution)/shard_map/ppermute | solution.py:317
  94.6 2.9 %collective-permute-done.4.near3_ref = bf16[64,1024]{1,0:T(8,128)(2,1)S(1)} collective-permute-done((bf16[64,1024]{1,0:T(8,128)(2,1)S(1)}, bf16[64,1024]{1,0:T(8,128)(2,1)S(1)}, u32[]{:S(2)}, u32[]{:S(2)}) %collective-permute-start.4) | collective-permute-done | bytes 131104 | tf_op jit(solution)/shard_map/ppermute | solution.py:317
  99.1 2.2 %shard_map.64 = bf16[2,64,1024]{2,1,0:T(8,128)(2,1)} custom-call(s32[4]{0:T(128)} %pad_add_fusion.place, bf16[64,1024]{1,0:T(8,128)(2,1)} %copy-done.7, bf16[64,1024]{1,0:T(8,128)(2,1)} %copy-done.10, bf16[64,1024]{1,0:T(8,128)(2,1)} %collective-permute-done.3.near2_ref, bf16[64,1024]{1,0:T(8,128)(2,1)} %copy-done.11, bf16[4,64,1024]{2,1,0:T(8,128)(2,1)} %copy-done.9), custom_call_target="tpu_custom_call" | custom-call | flops 524288 | bytes 2097152 | tf_op jit(solution)/shard_map/pallas_call | solution.py:161
  101.2 2.2 %collective-permute-done.6.far_ref = bf16[32,4096]{1,0:T(8,128)(2,1)S(1)} collective-permute-done((bf16[32,4096]{1,0:T(8,128)(2,1)S(1)}, bf16[32,4096]{1,0:T(8,128)(2,1)S(1)}, u32[]{:S(2)}, u32[]{:S(2)}) %collective-permute-start.6) | collective-permute-done | bytes 262176 | tf_op jit(solution)/shard_map/ppermute | solution.py:313
  103.4 5.3 %all-to-all-start.3 = ((bf16[8,16,1024]{2,1,0:T(8,128)(2,1)}), bf16[8,16,1024]{2,1,0:T(8,128)(2,1)S(1)}, u32[]{:S(2)}, u32[]{:S(2)}) async-start(bf16[8,16,1024]{2,1,0:T(8,128)(2,1)} %bitcast.11), calls=%async_computation.3 | async-start | bytes 524288 | tf_op jit(solution)/shard_map/all_to_all | solution.py:344
  109.6 9.8 %all-to-all-done.3.got_ref = bf16[8,16,1024]{2,1,0:T(8,128)(2,1)S(1)} async-done(((bf16[8,16,1024]{2,1,0:T(8,128)(2,1)}), bf16[8,16,1024]{2,1,0:T(8,128)(2,1)S(1)}, u32[]{:S(2)}, u32[]{:S(2)}) %all-to-all-start.3) | async-done | bytes 262176 | tf_op jit(solution)/shard_map/all_to_all | solution.py:344
  (34 shorter events, 11.8 us)
Async XLA Ops:
  0.6 40.9 %copy-start = (bf16[1,2048,768]{2,1,0:T(8,128)(2,1)S(1)}, bf16[1,2048,768]{2,1,0:T(8,128)(2,1)}, u32[]{:S(2)}) copy-start(bf16[1,2048,768]{2,1,0:T(8,128)(2,1)} %param.5) | copy-start | bytes 9437188
  0.6 31.0 %collective-permute-start.1 = (bf16[2048,768]{1,0:T(8,128)(2,1)}, bf16[2048,768]{1,0:T(8,128)(2,1)}, u32[]{:S(2)}, u32[]{:S(2)}) collective-permute-start(bf16[2048,768]{1,0:T(8,128)(2,1)} %bitcast.6), channel_id=1, source_target_pairs={{0,128},{128,0},{1,129},{129,1},{2,130},{130,2},{3,131},{131,3},{4... | collective-permute-start | bytes 9437192 | tf_op jit(solution)/shard_map/ppermute | solution.py:313
  10.5 9.2 %collective-permute-start = (bf16[16,1536]{1,0:T(8,128)(2,1)S(1)}, bf16[16,1536]{1,0:T(8,128)(2,1)S(1)}, u32[]{:S(2)}, u32[]{:S(2)}) collective-permute-start(bf16[16,1536]{1,0:T(8,128)(2,1)S(1)} %dynamic_slice.3), channel_id=1, source_target_pairs={{0,256},{256,0},{1,257},{257,1},{2,258},{258,2},{3,259},{259,3},{4... | collective-permute-start | bytes 147464 | tf_op jit(solution)/shard_map/ppermute | solution.py:313
  13.2 28.4 %copy-start.8 = (s32[4]{0:T(128)S(1)}, s32[4]{0:T(128)}, u32[]{:S(2)}) copy-start(s32[4]{0:T(128)} %pad_add_fusion.place) | copy-start | bytes 52
  19.7 12.0 %copy-start.12 = (bf16[16,1536]{1,0:T(8,128)(2,1)}, bf16[16,1536]{1,0:T(8,128)(2,1)S(1)}, u32[]{:S(2)}) copy-start(bf16[16,1536]{1,0:T(8,128)(2,1)S(1)} %collective-permute-done.share_ref) | copy-start | bytes 147460
  33.5 27.4 %all-to-all-start.1 = ((bf16[8,16,2688]{2,1,0:T(8,128)(2,1)}), bf16[8,16,2688]{2,1,0:T(8,128)(2,1)}, u32[]{:S(2)}, u32[]{:S(2)}) async-start(bf16[8,16,2688]{2,1,0:T(8,128)(2,1)} %shard_map.59), calls=%async_computation.1 | async-start | bytes 1376256 | tf_op jit(solution)/shard_map/all_to_all | solution.py:330
  41.6 1.1 copy-start.1
  47.7 0.7 copy-start.7
  48.4 7.6 %collective-permute-start.2 = (bf16[64,1024]{1,0:T(8,128)(2,1)S(1)}, bf16[64,1024]{1,0:T(8,128)(2,1)S(1)}, u32[]{:S(2)}, u32[]{:S(2)}) collective-permute-start(bf16[64,1024]{1,0:T(8,128)(2,1)S(1)} %get-tuple-element.40), channel_id=1, source_target_pairs={{0,2},{1,3},{2,0},{3,1},{4,6},{5,7},{6,4},{7,5},{8,10},{9,11},{10,... | collective-permute-start | bytes 393224 | tf_op jit(solution)/shard_map/ppermute | solution.py:317
  51.0 6.7 %collective-permute-start.3 = (bf16[64,1024]{1,0:T(8,128)(2,1)S(1)}, bf16[64,1024]{1,0:T(8,128)(2,1)}, u32[]{:S(2)}, u32[]{:S(2)}) collective-permute-start(bf16[64,1024]{1,0:T(8,128)(2,1)S(1)} %get-tuple-element.41), channel_id=1, source_target_pairs={{0,1},{1,0},{2,3},{3,2},{4,5},{5,4},{6,7},{7,6},{8,9},{9,8},{10,11... | collective-permute-start | bytes 393224 | tf_op jit(solution)/shard_map/ppermute | solution.py:317
  56.0 0.7 copy-start.10
  60.8 1.1 copy-start.2
  62.0 1.0 copy-start.4
  67.1 7.0 %collective-permute-start.5 = (f32[64,4096]{1,0:T(8,128)S(1)}, f32[64,4096]{1,0:T(8,128)S(1)}, u32[]{:S(2)}, u32[]{:S(2)}) collective-permute-start(f32[64,4096]{1,0:T(8,128)S(1)} %get-tuple-element.48), channel_id=1, source_target_pairs={{0,128},{128,0},{1,129},{129,1},{2,130},{130,2},{3,131},{131,3},{4... | collective-permute-start | bytes 3145736 | tf_op jit(solution)/shard_map/ppermute | solution.py:313
  74.2 0.8 copy-start.5
  80.0 0.8 copy-start.3
  80.9 27.9 %copy-start.6 = (f32[32,4096]{1,0:T(8,128)S(1)}, f32[32,4096]{1,0:T(8,128)}, u32[]{:S(2)}) copy-start(f32[32,4096]{1,0:T(8,128)} %copy-done.5) | copy-start | bytes 1572868
  80.9 16.7 %all-to-all-start.2 = ((bf16[4,64,1024]{2,1,0:T(8,128)(2,1)}), bf16[4,64,1024]{2,1,0:T(8,128)(2,1)S(1)}, u32[]{:S(2)}, u32[]{:S(2)}) async-start(bf16[4,64,1024]{2,1,0:T(8,128)(2,1)} %copy-done.3), calls=%async_computation.2 | async-start | bytes 1048576 | tf_op jit(solution)/shard_map/all_to_all | solution.py:339
  84.5 19.0 %collective-permute-start.6 = (bf16[32,4096]{1,0:T(8,128)(2,1)S(1)}, bf16[32,4096]{1,0:T(8,128)(2,1)S(1)}, u32[]{:S(2)}, u32[]{:S(2)}) collective-permute-start(bf16[32,4096]{1,0:T(8,128)(2,1)S(1)} %get-tuple-element.51), channel_id=1, source_target_pairs={{0,256},{256,0},{1,257},{257,1},{2,258},{258,2},{3,259},{259,3},{4... | collective-permute-start | bytes 786440 | tf_op jit(solution)/shard_map/ppermute | solution.py:313
  90.1 7.5 %collective-permute-start.4 = (bf16[64,1024]{1,0:T(8,128)(2,1)S(1)}, bf16[64,1024]{1,0:T(8,128)(2,1)S(1)}, u32[]{:S(2)}, u32[]{:S(2)}) collective-permute-start(bf16[64,1024]{1,0:T(8,128)(2,1)S(1)} %get-tuple-element.45), channel_id=1, source_target_pairs={{0,3},{1,2},{2,1},{3,0},{4,7},{5,6},{6,5},{7,4},{8,11},{9,10},{10,... | collective-permute-start | bytes 393224 | tf_op jit(solution)/shard_map/ppermute | solution.py:317
  97.6 0.7 copy-start.11
  98.2 0.8 copy-start.9
  103.4 15.9 %all-to-all-start.3 = ((bf16[8,16,1024]{2,1,0:T(8,128)(2,1)}), bf16[8,16,1024]{2,1,0:T(8,128)(2,1)S(1)}, u32[]{:S(2)}, u32[]{:S(2)}) async-start(bf16[8,16,1024]{2,1,0:T(8,128)(2,1)} %bitcast.11), calls=%async_computation.3 | async-start | bytes 524288 | tf_op jit(solution)/shard_map/all_to_all | solution.py:344

commit v6 on v5

v6 whole, which is shorter than its diff:
```python
import functools

import jax
import jax.numpy as jnp
from jax import lax
from jax.experimental import pallas as pl
from jax.experimental.pallas import tpu as pltpu
from jax.sharding import Mesh, PartitionSpec as P

D = 16384
FF = 49152
BLOCK = 1024
TOKENS = 512
NT = (((1,), (1,)), ((), ()))
BF = jnp.bfloat16
F32 = jnp.float32
MB = 1024 * 1024


def params(mb):
    return pltpu.CompilerParams(vmem_limit_bytes=mb * MB)


def cost(flops, moved):
    return pl.CostEstimate(flops=flops, bytes_accessed=moved, transcendentals=0)


def prepare_kernel(acts_ref, grads_ref, sum_ref, send_ref):
    for i, ref in enumerate((grads_ref, acts_ref)):
        data = ref[...]
        value = lax.dot_general(data, data, NT, preferred_element_type=F32)
        sum_ref[i] = value
        send_ref[i] = value.astype(BF)


def prepare(acts, grads):
    tokens = grads.shape[0]
    vmem = pl.BlockSpec(memory_space=pltpu.VMEM)
    return pl.pallas_call(
        prepare_kernel,
        out_shape=(jax.ShapeDtypeStruct((2, tokens, tokens), F32), jax.ShapeDtypeStruct((2, tokens, tokens), BF)),
        in_specs=[vmem, vmem],
        out_specs=[vmem] * 2,
        compiler_params=params(16),
        cost_estimate=cost(2 * tokens * tokens * (grads.shape[1] + acts.shape[1]), 3 * MB),
    )(acts, grads)


def product_kernel(place, tokens_ref, near_lo, near_hi, far_lo, far_hi, *rest):
    out_ref, low, high = rest[-3:]
    quarter = near_lo.shape[1]

    def piece(core):
        lanes = pl.ds(pl.multiple_of(core * quarter, quarter), quarter)
        if len(tokens_ref.shape) == 3:
            return tokens_ref[:, :, lanes].reshape(-1, quarter)
        return tokens_ref[:, lanes]

    own, other = piece(place[1]), piece(1 - place[1])

    def dot(near, far):
        return lax.dot_general(own, near[...], NT, preferred_element_type=F32) + lax.dot_general(
            other, far[...], NT, preferred_element_type=F32
        )

    low[...] = dot(near_lo, far_lo)
    high[...] = dot(near_hi, far_hi)
    for x in range(4):
        for y in range(4):
            rows = slice((y * 4 + x) * 8, (y * 4 + x) * 8 + 8)
            pair = jnp.concatenate([low[rows, :], high[rows, :]], axis=0).astype(BF)
            out_ref[x, y * 16 : y * 16 + 16, :] = pair


def product(place, tokens, weight, weight_far, first=None):
    features, quarter = weight.shape
    half = features // 2
    step = 256
    steps = half // step
    low = pl.BlockSpec((step, quarter), lambda j, place: (j, 0))
    high = pl.BlockSpec((step, quarter), lambda j, place: (j + steps, 0))
    if tokens.ndim == 3:
        count = tokens.shape[0] * tokens.shape[1]
        token_spec = pl.BlockSpec(tokens.shape[:2] + (2 * quarter,), lambda j, place: (0, 0, 0))
    else:
        count = tokens.shape[0]
        token_spec = pl.BlockSpec((count, 2 * quarter), lambda j, place: (0, place[0]))
    in_specs = [token_spec, low, high, low, high]
    args = (place, tokens, weight, weight, weight_far, weight_far)
    part = 0
    aliases = {}
    if first is not None:
        in_specs.append(pl.BlockSpec(memory_space=pl.ANY))
        args += (first,)
        part = 1
        aliases = {6: 0}
    return pl.pallas_call(
        product_kernel,
        out_shape=jax.ShapeDtypeStruct((4, count, half), BF),
        grid_spec=pltpu.PrefetchScalarGridSpec(
            num_scalar_prefetch=1,
            grid=(steps,),
            in_specs=in_specs,
            out_specs=pl.BlockSpec((4, count // 2, step), lambda j, place: (0, part, j)),
            scratch_shapes=[pltpu.VMEM((count, step), F32)] * 2,
        ),
        input_output_aliases=aliases,
        compiler_params=params(60),
        cost_estimate=cost(4 * count * features * quarter, 7 * MB),
    )(*args)


def x_sum_kernel(place, got_ref, out_ref):
    rows = out_ref.shape[1]
    for part in range(2):
        value = got_ref[0, part * rows : part * rows + rows, :].astype(F32)
        for i in range(1, got_ref.shape[0]):
            value = value + got_ref[i, part * rows : part * rows + rows, :].astype(F32)
        out_ref[(1 - place[0]) if part else place[0]] = value.astype(BF)


def x_sum(place, got):
    _, rows, width = got.shape
    vmem = pl.BlockSpec(memory_space=pltpu.VMEM)
    return pl.pallas_call(
        x_sum_kernel,
        out_shape=jax.ShapeDtypeStruct((2, rows // 2, width), BF),
        in_specs=[pl.BlockSpec(memory_space=pltpu.SMEM), vmem],
        out_specs=vmem,
        compiler_params=params(16),
        cost_estimate=cost(8 * rows * width, 2 * MB),
    )(place, got)


def y_sum_kernel(got_ref, out_ref):
    value = got_ref[0].astype(F32)
    for i in range(1, got_ref.shape[0]):
        value = value + got_ref[i].astype(F32)
    out_ref[...] = jnp.concatenate([value[:8], value[8:]], axis=1).astype(BF)


def y_sum(got):
    width = got.shape[2]
    return pl.pallas_call(
        y_sum_kernel,
        out_shape=jax.ShapeDtypeStruct((8, 2 * width), BF),
        in_specs=[pl.BlockSpec(memory_space=pltpu.VMEM)],
        out_specs=pl.BlockSpec(memory_space=pltpu.VMEM),
        compiler_params=params(16),
        cost_estimate=cost(128 * width, MB // 2),
    )(got)


def picker(place, offset, share, stride):
    shape = (4 * share, BLOCK)
    row = lax.broadcasted_iota(jnp.int32, shape, 0)
    unit = lax.broadcasted_iota(jnp.int32, shape, 1)
    peer = row // share
    rep = (place[0] ^ (peer & 1)) * 2 + (place[1] ^ (peer >> 1))
    wanted = (rep * stride + offset) * share + (row % share)
    return jnp.where(unit == wanted, 1.0, 0.0).astype(BF)


def stats_kernel(place, left_ref, right_ref, acts_hbm, grads_hbm, keep_ref, send_ref, acts_ref, grads_ref, sems):
    hidden = grads_ref.shape[1]
    width = acts_ref.shape[1]
    copies = []
    for j in range((hidden + width) // BLOCK):
        source, target, at = (grads_hbm, grads_ref, j) if j < hidden // BLOCK else (acts_hbm, acts_ref, j - hidden // BLOCK)
        lanes = slice(at * BLOCK, (at + 1) * BLOCK)
        copies.append(pltpu.make_async_copy(source.at[:, lanes], target.at[:, lanes], sems.at[j]))
        copies[-1].start()

    def rows(pick, token_kernel, data):
        mix = jnp.dot(token_kernel, data, preferred_element_type=F32).astype(BF)
        picked = lax.dot_general(pick, data, NT, preferred_element_type=F32).astype(BF)
        return jnp.dot(picked, mix, preferred_element_type=F32) * (1.0 / TOKENS)

    right = (right_ref[...] / D).astype(BF)
    pick = picker(place, place[2], 32, 8)
    for j in range(hidden // BLOCK):
        lanes = slice(j * BLOCK, (j + 1) * BLOCK)
        copies[j].wait()
        out = rows(pick, right, grads_ref[:, lanes])
        keep_ref[:, lanes] = out[:64]
        send_ref[:, lanes] = out[64:]
    left = (left_ref[...] / FF).astype(BF)
    pick = picker(place, place[3], 16, 16)
    for j in range(width // BLOCK):
        copies[hidden // BLOCK + j].wait()
        out = rows(pick, left, acts_ref[:, j * BLOCK : (j + 1) * BLOCK])
        for dy in range(2):
            at = slice(dy * 32 + j * 16, dy * 32 + j * 16 + 16)
            keep_ref[at, hidden:] = out[dy * 16 : dy * 16 + 16]
            send_ref[at, hidden:] = out[32 + dy * 16 : 32 + dy * 16 + 16]


def stats(place, left, right, acts, grads):
    shape = jax.ShapeDtypeStruct((64, grads.shape[1] + BLOCK), F32)
    vmem = pl.BlockSpec(memory_space=pltpu.VMEM)
    hbm = pl.BlockSpec(memory_space=pltpu.HBM)
    return pl.pallas_call(
        stats_kernel,
        out_shape=(shape, shape),
        in_specs=[pl.BlockSpec(memory_space=pltpu.SMEM), vmem, vmem, hbm, hbm],
        out_specs=[vmem, vmem],
        scratch_shapes=[
            pltpu.VMEM(acts.shape, BF),
            pltpu.VMEM(grads.shape, BF),
            pltpu.SemaphoreType.DMA(((acts.shape[1] + grads.shape[1]) // BLOCK,)),
        ],
        compiler_params=params(16),
        cost_estimate=cost(1000 * MB, 5 * MB),
    )(place, left, right, acts, grads)


def core_sum_kernel(keep_ref, got_ref, near_ref, far_ref):
    half = near_ref.shape[0]
    near_ref[...] = keep_ref[:half] + got_ref[:half]
    far_ref[...] = (keep_ref[half:] + got_ref[half:]).astype(BF)


def core_sum(keep, got):
    rows, width = keep.shape
    vmem = pl.BlockSpec(memory_space=pltpu.VMEM)
    return pl.pallas_call(
        core_sum_kernel,
        out_shape=(
            jax.ShapeDtypeStruct((rows // 2, width), F32),
            jax.ShapeDtypeStruct((rows // 2, width), BF),
        ),
        in_specs=[vmem, vmem],
        out_specs=[vmem, vmem],
        compiler_params=params(16),
        cost_estimate=cost(rows * width, 3 * MB),
    )(keep, got)


def last_sum_kernel(near_ref, far_ref, left_ref, right_ref):
    hidden = right_ref.shape[1]
    right_ref[...] = near_ref[:, :hidden] + far_ref[:, :hidden].astype(F32)
    for j in range(left_ref.shape[1] // BLOCK):
        rows = slice(j * 16, j * 16 + 16)
        left_ref[:, j * BLOCK : (j + 1) * BLOCK] = near_ref[rows, hidden:] + far_ref[rows, hidden:].astype(F32)


def last_sum(near, far, hidden, width):
    vmem = pl.BlockSpec(memory_space=pltpu.VMEM)
    return pl.pallas_call(
        last_sum_kernel,
        out_shape=(
            jax.ShapeDtypeStruct((16, width), F32),
            jax.ShapeDtypeStruct((32, hidden), F32),
        ),
        in_specs=[vmem, vmem],
        out_specs=[vmem, vmem],
        compiler_params=params(16),
        cost_estimate=cost(32 * 4096, 2 * MB),
    )(near, far)


def body(acts, grad_out, weight_slab):
    weight = weight_slab[0]
    width = acts.shape[1]
    hidden = grad_out.shape[1]
    yh, core, row, yl, xx = (lax.axis_index(n) for n in ("yh", "core", "row", "yl", "x"))
    place = jnp.stack([yh, core, row, yl * 4 + xx]).astype(jnp.int32)

    def swap(value, axis):
        return lax.ppermute(value, axis, [(0, 1), (1, 0)])

    def across(value, dz, dy, dx):
        perm = [(i, i ^ (dz * 16 + dy * 4 + dx)) for i in range(128)]
        return lax.ppermute(value, ("row", "yl", "x"), perm)

    barrier = lax.optimization_barrier
    share = lax.dynamic_slice(grad_out, (row * 16, (1 - yh) * (hidden // 2)), (16, hidden // 2))
    share, acts_in = barrier((share, acts))
    share = swap(share, "yh")
    weight_far = swap(weight, "core")

    total, send = prepare(acts_in, grad_out)
    total = total + across(send, 1, 0, 1).astype(F32)
    total = total + across(total.astype(BF), 2, 0, 3).astype(F32)
    total = total + across(total.astype(BF), 7, 1, 0).astype(F32)
    left, right = total[0], total[1]
    left = left + across(left.astype(BF), 0, 2, 0).astype(F32)

    share = jnp.broadcast_to(share[None], (8,) + share.shape)
    share, near_tokens = barrier((share, grad_out))
    far_tokens = lax.all_to_all(share, "row", 0, 0, tiled=True)
    near = product(place, near_tokens, weight, weight_far)
    both = product(place, far_tokens, weight, weight_far, near)

    left, right, both = barrier((left, right, both))
    got = lax.all_to_all(both, "x", 0, 0, tiled=True)
    keep, send = stats(place, left, right, acts, grad_out)
    near_rows, far_rows = core_sum(keep, swap(send, "core"))
    got, near_rows = barrier((got, near_rows))
    far_rows = swap(far_rows, "yh")

    chunks = x_sum(place, got)
    chunks = chunks.reshape(8, -1, chunks.shape[2])
    input_grad = y_sum(lax.all_to_all(chunks, ("yh", "yl"), 0, 0, tiled=True))

    left_stats, right_stats = last_sum(near_rows, far_rows, hidden, width)
    return input_grad, left_stats, right_stats


def solution(mesh):
    split = Mesh(mesh.devices.reshape(2, 2, 8, 4, 4), ("yh", "core", "row", "yl", "x"))
    rep, col = ("yh", "core"), ("yl", "x")
    in_specs = (P(rep, "row"), P(rep, col), P(rep, "row", col))
    out_specs = (P(rep + col, "row"), P(rep + col, "row"), P(rep + ("row",), col))
    return jax.shard_map(body, mesh=split, in_specs=in_specs, out_specs=out_specs, check_vma=False)
```

time: 122 us -> 123 us (level); the launches traced: 120 us -> 123 us
  blocking collectives: 12 us -> 0 us
  waiting for transfers between devices: 28.5 us -> 37.7 us
  starting transfers between devices: 47.6 us -> 56 us
  local copies, waits for them, and re-layouts: 8.53 us -> 6.36 us
    all_to_all x1 -> x0, blocking collectives: 12 us -> none  [body(): left_rows = lax.all_to_all(left_part, ('yl', 'x'), 0, 0, tiled=True)]
    all_to_all x2, waiting for transfers between devices: 3.09 us -> 14.5 us  [the longest x1 14.3 us: body(): got = lax.all_to_all(both, 'x', 0, 0, tiled=True)]
    all_to_all x1, waiting for transfers between devices: 9.83 us -> 0.01 us  [body(): input_grad = y_sum(lax.all_to_all(chunks, ('yh', 'yl'), 0, 0, tiled=True))]
    ppermute x4, starting transfers between devices: 21.4 us -> 28.8 us  [swap(): return lax.ppermute(value, axis, [(0, 1), (1, 0)])]
    ppermute x4, waiting for transfers between devices: 8.5 us -> 15.5 us  [swap(): return lax.ppermute(value, axis, [(0, 1), (1, 0)])]
    ppermute x3 -> x4, starting transfers between devices: 9.13 us -> 14.1 us  [across(): return lax.ppermute(value, ('row', 'yl', 'x'), perm)]
    all_to_all x2, starting transfers between devices: 11.7 us -> 7.81 us  [the longest x1 4.28 us: body(): far_tokens = lax.all_to_all(share, 'row', 0, 0, tiled=True)]
    unnamed x26 -> x16, local copies, waits for them, and re-layouts: 7.72 us -> 4.77 us
  transfers between devices with their start and end apart: 10 -> 11, of which waited for: 8 -> 5; matrix products, arithmetic and copies ran while one was open for 1% -> 2% of each run, Pallas kernels for 9% -> 6%
where the time goes in v6:
time: 123 us
  starting transfers between devices  56 us (46%)
  waiting for transfers between devices  37.7 us (31%)
  Pallas kernels  20.9 us (17%)
  local copies, waits for them, and re-layouts  6.36 us (5%)
    ppermute x4, starting transfers between devices, swap(): return lax.ppermute(value, axis, [(0, 1), (1, 0)])  28.8 us
    ppermute x4, waiting for transfers between devices, swap(): return lax.ppermute(value, axis, [(0, 1), (1, 0)])  15.5 us
    all_to_all x1, waiting for transfers between devices, body(): got = lax.all_to_all(both, 'x', 0, 0, tiled=True)  14.3 us
    ppermute x4, starting transfers between devices, across(): return lax.ppermute(value, ('row', 'yl', 'x'), perm)  14.1 us
    pallas_call x2, Pallas kernels, product(): pl.pallas_call(product_kernel, out_shape=jax.ShapeDtypeStruct((4, count,...  12.9 us
    ppermute x4, waiting for transfers between devices, across(): return lax.ppermute(value, ('row', 'yl', 'x'), perm)  7.71 us
    all_to_all x1, starting transfers between devices, body(): input_grad = y_sum(lax.all_to_all(chunks, ('yh', 'yl'), 0, 0, tiled=True))  5.36 us
    unnamed x16, local copies, waits for them, and re-layouts  4.77 us
  transfers between devices with their start and end apart: 11, of which 5 were waited for; matrix products, arithmetic and copies ran while one was open for 2% of the time, Pallas kernels for 6%

profile of v6, /device:TPU:1, one launch (start us, length us, event | category | flops | bytes accessed | tf_op | source)
XLA Modules:
  0.0 122.6 jit_solution(13707523522612178785)
XLA Ops:
  0.6 8.8 %collective-permute-start.5 = (bf16[2048,768]{1,0:T(8,128)(2,1)}, bf16[2048,768]{1,0:T(8,128)(2,1)}, u32[]{:S(2)}, u32[]{:S(2)}) collective-permute-start(bf16[2048,768]{1,0:T(8,128)(2,1)} %bitcast.14), channel_id=1, source_target_pairs={{0,128},{128,0},{1,129},{129,1},{2,130},{130,2},{3,131},{131,3},{4... | collective-permute-start | bytes 9437192 | tf_op jit(solution)/shard_map/ppermute | solution.py:270
  9.4 0.8 dynamic_slice.3
  10.2 1.1 copy-done
  11.4 1.0 copy-done.4
  12.9 1.9 %collective-permute-start = (bf16[2,128,128]{2,1,0:T(8,128)(2,1)S(1)}, bf16[2,128,128]{2,1,0:T(8,128)(2,1)S(1)}, u32[]{:S(2)}, u32[]{:S(2)}) collective-permute-start(bf16[2,128,128]{2,1,0:T(8,128)(2,1)S(1)} %get-tuple-element.22), channel_id=1, source_target_pairs={{0,17},{1,16},{2,19},{3,18},{4,21},{5,20},{6,23},{7,22},{8,25},{9,... | collective-permute-start | bytes 196616 | tf_op jit(solution)/shard_map/ppermute | solution.py:274
  14.9 4.6 %collective-permute-done = bf16[2,128,128]{2,1,0:T(8,128)(2,1)S(1)} collective-permute-done((bf16[2,128,128]{2,1,0:T(8,128)(2,1)S(1)}, bf16[2,128,128]{2,1,0:T(8,128)(2,1)S(1)}, u32[]{:S(2)}, u32[]{:S(2)}) %collective-permute-start) | collective-permute-done | bytes 65568 | tf_op jit(solution)/shard_map/ppermute | solution.py:274
  19.5 2.6 %collective-permute-start.1 = (bf16[2,128,128]{2,1,0:T(8,128)(2,1)S(1)}, bf16[2,128,128]{2,1,0:T(8,128)(2,1)S(1)}, u32[]{:S(2)}, u32[]{:S(2)}) collective-permute-start(bf16[2,128,128]{2,1,0:T(8,128)(2,1)S(1)} %fusion), channel_id=1, source_target_pairs={{0,35},{1,34},{2,33},{3,32},{4,39},{5,38},{6,37},{7,36},{8,43},{9,... | collective-permute-start | bytes 196616 | tf_op jit(solution)/shard_map/ppermute | solution.py:274
  22.1 7.5 %collective-permute-start.4 = (bf16[16,1536]{1,0:T(8,128)(2,1)S(1)}, bf16[16,1536]{1,0:T(8,128)(2,1)S(1)}, u32[]{:S(2)}, u32[]{:S(2)}) collective-permute-start(bf16[16,1536]{1,0:T(8,128)(2,1)S(1)} %dynamic_slice.3), channel_id=1, source_target_pairs={{0,256},{256,0},{1,257},{257,1},{2,258},{258,2},{3,259},{259,3},{4... | collective-permute-start | bytes 147464 | tf_op jit(solution)/shard_map/ppermute | solution.py:270
  29.6 7.1 %collective-permute-start.2 = (bf16[2,128,128]{2,1,0:T(8,128)(2,1)S(1)}, bf16[2,128,128]{2,1,0:T(8,128)(2,1)S(1)}, u32[]{:S(2)}, u32[]{:S(2)}) collective-permute-start(bf16[2,128,128]{2,1,0:T(8,128)(2,1)S(1)} %fusion.2), channel_id=1, source_target_pairs={{0,116},{1,117},{2,118},{3,119},{4,112},{5,113},{6,114},{7,115},{8... | collective-permute-start | bytes 196616 | tf_op jit(solution)/shard_map/ppermute | solution.py:274
  38.1 4.3 %all-to-all-start = ((bf16[8,16,1536]{2,1,0:T(8,128)(2,1)}), bf16[8,16,1536]{2,1,0:T(8,128)(2,1)S(1)}, u32[]{:S(2)}, u32[]{:S(2)}) async-start(bf16[8,16,1536]{2,1,0:T(8,128)(2,1)} %broadcast_in_dim.2), calls=%async_computation | async-start | bytes 786432 | tf_op jit(solution)/shard_map/all_to_all | solution.py:291
  42.5 2.4 %collective-permute-start.3 = (bf16[128,128]{1,0:T(8,128)(2,1)S(1)}, bf16[128,128]{1,0:T(8,128)(2,1)S(1)}, u32[]{:S(2)}, u32[]{:S(2)}) collective-permute-start(bf16[128,128]{1,0:T(8,128)(2,1)S(1)} %fusion.1), channel_id=1, source_target_pairs={{0,8},{1,9},{2,10},{3,11},{4,12},{5,13},{6,14},{7,15},{8,0},{9,1},... | collective-permute-start | bytes 98312 | tf_op jit(solution)/shard_map/ppermute | solution.py:274
  44.9 3.1 %collective-permute-done.3 = bf16[128,128]{1,0:T(8,128)(2,1)S(1)} collective-permute-done((bf16[128,128]{1,0:T(8,128)(2,1)S(1)}, bf16[128,128]{1,0:T(8,128)(2,1)S(1)}, u32[]{:S(2)}, u32[]{:S(2)}) %collective-permute-start.3) | collective-permute-done | bytes 32800 | tf_op jit(solution)/shard_map/ppermute | solution.py:274
  48.1 6.5 %shard_map.59.rest_0_ = bf16[4,128,1024]{2,1,0:T(8,128)(2,1)} custom-call(s32[4]{0:T(128)} %pad_add_fusion.place, bf16[128,3072]{1,0:T(8,128)(2,1)} %grads_hbm.1, bf16[2048,768]{1,0:T(8,128)(2,1)} %bitcast.15, bf16[2048,768]{1,0:T(8,128)(2,1)} %bitcast.16, bf16[2048,768]{1,0:T(8,128)(2,1)} %collective-permute-done.5.far_lo.far_hi, ...), custom_call_target="tpu_custom_call" | custom-call | flops 805306368 | bytes 7340032 | tf_op jit(solution)/shard_map/pallas_call | solution.py:97
  55.5 6.5 %shard_map.60 = bf16[4,128,1024]{2,1,0:T(8,128)(2,1)} custom-call(s32[4]{0:T(128)} %pad_add_fusion.place, bf16[8,16,1536]{2,1,0:T(8,128)(2,1)} %copy-done.7, bf16[2048,768]{1,0:T(8,128)(2,1)} %bitcast.17, bf16[2048,768]{1,0:T(8,128)(2,1)} %bitcast.18, bf16[2048,768]{1,0:T(8,128)(2,1)} %collective-permute-done.5.far_lo.far_hi, ...), custom_call_target="tpu_custom_call", output_to_operand_aliasing={{}: (6, {})} | custom-call | flops 805306368 | bytes 7340032 | tf_op jit(solution)/shard_map/pallas_call | solution.py:97
  61.9 4.5 %shard_map.61 = (f32[64,4096]{1,0:T(8,128)S(1)}, f32[64,4096]{1,0:T(8,128)}) custom-call(s32[4]{0:T(128)S(1)} %copy-done.6, f32[128,128]{1,0:T(8,128)S(1)} %convert_add_fusion.3.left_ref, f32[128,128]{1,0:T(8,128)S(1)} %slice_bitcast_fusion.right_ref, bf16[128,2048]{1,0:T(8,128)(2,1)S(1)} %copy-done.5, bf16[128,3072]{1,0:T(8,128)(2,1)S(1)} %copy-done.1), custom_call_target="tpu_custom_call" | custom-call | flops 1048576000 | bytes 5242880 | tf_op jit(solution)/shard_map/pallas_call | solution.py:202
  66.5 5.3 %collective-permute-start.6 = (f32[64,4096]{1,0:T(8,128)}, f32[64,4096]{1,0:T(8,128)S(1)}, u32[]{:S(2)}, u32[]{:S(2)}) collective-permute-start(f32[64,4096]{1,0:T(8,128)} %get-tuple-element.30), channel_id=1, source_target_pairs={{0,128},{128,0},{1,129},{129,1},{2,130},{130,2},{3,131},{131,3},{4... | collective-permute-start | bytes 3145736 | tf_op jit(solution)/shard_map/ppermute | solution.py:270
  71.8 3.5 %all-to-all-start.1 = ((bf16[4,128,1024]{2,1,0:T(8,128)(2,1)}), bf16[4,128,1024]{2,1,0:T(8,128)(2,1)S(1)}, u32[]{:S(2)}, u32[]{:S(2)}) async-start(bf16[4,128,1024]{2,1,0:T(8,128)(2,1)} %shard_map.60), calls=%async_computation.1 | async-start | bytes 2097152 | tf_op jit(solution)/shard_map/all_to_all | solution.py:296
  76.2 14.3 %all-to-all-done.1.got_ref = bf16[4,128,1024]{2,1,0:T(8,128)(2,1)S(1)} async-done(((bf16[4,128,1024]{2,1,0:T(8,128)(2,1)}), bf16[4,128,1024]{2,1,0:T(8,128)(2,1)S(1)}, u32[]{:S(2)}, u32[]{:S(2)}) %all-to-all-start.1) | async-done | bytes 1048608 | tf_op jit(solution)/shard_map/all_to_all | solution.py:296
  90.5 1.4 %shard_map.63 = bf16[2,64,1024]{2,1,0:T(8,128)(2,1)} custom-call(s32[4]{0:T(128)S(1)} %copy-done.6, bf16[4,128,1024]{2,1,0:T(8,128)(2,1)S(1)} %all-to-all-done.1.got_ref), custom_call_target="tpu_custom_call" | custom-call | flops 1048576 | bytes 2097152 | tf_op jit(solution)/shard_map/pallas_call | solution.py:125
  91.9 5.4 %all-to-all-start.2 = ((bf16[8,16,1024]{2,1,0:T(8,128)(2,1)}), bf16[8,16,1024]{2,1,0:T(8,128)(2,1)S(1)}, u32[]{:S(2)}, u32[]{:S(2)}) async-start(bf16[8,16,1024]{2,1,0:T(8,128)(2,1)} %bitcast.7), calls=%async_computation.2 | async-start | bytes 524288 | tf_op jit(solution)/shard_map/all_to_all | solution.py:304
  97.2 7.3 %collective-permute-start.7 = (bf16[32,4096]{1,0:T(8,128)(2,1)S(1)}, bf16[32,4096]{1,0:T(8,128)(2,1)S(1)}, u32[]{:S(2)}, u32[]{:S(2)}) collective-permute-start(bf16[32,4096]{1,0:T(8,128)(2,1)S(1)} %get-tuple-element.34), channel_id=1, source_target_pairs={{0,256},{256,0},{1,257},{257,1},{2,258},{258,2},{3,259},{259,3},{4... | collective-permute-start | bytes 786440 | tf_op jit(solution)/shard_map/ppermute | solution.py:270
  104.5 15.5 %collective-permute-done.7.far_ref = bf16[32,4096]{1,0:T(8,128)(2,1)S(1)} collective-permute-done((bf16[32,4096]{1,0:T(8,128)(2,1)S(1)}, bf16[32,4096]{1,0:T(8,128)(2,1)S(1)}, u32[]{:S(2)}, u32[]{:S(2)}) %collective-permute-start.7) | collective-permute-done | bytes 262176 | tf_op jit(solution)/shard_map/ppermute | solution.py:270
  120.0 1.0 copy-done.3
  121.1 0.8 shard_map.65
  (31 shorter events, 4.5 us)
Async XLA Ops:
  0.6 47.4 %collective-permute-start.5 = (bf16[2048,768]{1,0:T(8,128)(2,1)}, bf16[2048,768]{1,0:T(8,128)(2,1)}, u32[]{:S(2)}, u32[]{:S(2)}) collective-permute-start(bf16[2048,768]{1,0:T(8,128)(2,1)} %bitcast.14), channel_id=1, source_target_pairs={{0,128},{128,0},{1,129},{129,1},{2,130},{130,2},{3,131},{131,3},{4... | collective-permute-start | bytes 9437192 | tf_op jit(solution)/shard_map/ppermute | solution.py:270
  10.2 1.1 copy-start
  11.4 1.0 copy-start.4
  12.9 6.5 %collective-permute-start = (bf16[2,128,128]{2,1,0:T(8,128)(2,1)S(1)}, bf16[2,128,128]{2,1,0:T(8,128)(2,1)S(1)}, u32[]{:S(2)}, u32[]{:S(2)}) collective-permute-start(bf16[2,128,128]{2,1,0:T(8,128)(2,1)S(1)} %get-tuple-element.22), channel_id=1, source_target_pairs={{0,17},{1,16},{2,19},{3,18},{4,21},{5,20},{6,23},{7,22},{8,25},{9,... | collective-permute-start | bytes 196616 | tf_op jit(solution)/shard_map/ppermute | solution.py:274
  19.5 10.1 %collective-permute-start.1 = (bf16[2,128,128]{2,1,0:T(8,128)(2,1)S(1)}, bf16[2,128,128]{2,1,0:T(8,128)(2,1)S(1)}, u32[]{:S(2)}, u32[]{:S(2)}) collective-permute-start(bf16[2,128,128]{2,1,0:T(8,128)(2,1)S(1)} %fusion), channel_id=1, source_target_pairs={{0,35},{1,34},{2,33},{3,32},{4,39},{5,38},{6,37},{7,36},{8,43},{9,... | collective-permute-start | bytes 196616 | tf_op jit(solution)/shard_map/ppermute | solution.py:274
  22.1 15.3 %collective-permute-start.4 = (bf16[16,1536]{1,0:T(8,128)(2,1)S(1)}, bf16[16,1536]{1,0:T(8,128)(2,1)S(1)}, u32[]{:S(2)}, u32[]{:S(2)}) collective-permute-start(bf16[16,1536]{1,0:T(8,128)(2,1)S(1)} %dynamic_slice.3), channel_id=1, source_target_pairs={{0,256},{256,0},{1,257},{257,1},{2,258},{258,2},{3,259},{259,3},{4... | collective-permute-start | bytes 147464 | tf_op jit(solution)/shard_map/ppermute | solution.py:270
  29.6 12.8 %collective-permute-start.2 = (bf16[2,128,128]{2,1,0:T(8,128)(2,1)S(1)}, bf16[2,128,128]{2,1,0:T(8,128)(2,1)S(1)}, u32[]{:S(2)}, u32[]{:S(2)}) collective-permute-start(bf16[2,128,128]{2,1,0:T(8,128)(2,1)S(1)} %fusion.2), channel_id=1, source_target_pairs={{0,116},{1,117},{2,118},{3,119},{4,112},{5,113},{6,114},{7,115},{8... | collective-permute-start | bytes 196616 | tf_op jit(solution)/shard_map/ppermute | solution.py:274
  38.1 16.6 %all-to-all-start = ((bf16[8,16,1536]{2,1,0:T(8,128)(2,1)}), bf16[8,16,1536]{2,1,0:T(8,128)(2,1)S(1)}, u32[]{:S(2)}, u32[]{:S(2)}) async-start(bf16[8,16,1536]{2,1,0:T(8,128)(2,1)} %broadcast_in_dim.2), calls=%async_computation | async-start | bytes 786432 | tf_op jit(solution)/shard_map/all_to_all | solution.py:291
  42.5 5.6 %collective-permute-start.3 = (bf16[128,128]{1,0:T(8,128)(2,1)S(1)}, bf16[128,128]{1,0:T(8,128)(2,1)S(1)}, u32[]{:S(2)}, u32[]{:S(2)}) collective-permute-start(bf16[128,128]{1,0:T(8,128)(2,1)S(1)} %fusion.1), channel_id=1, source_target_pairs={{0,8},{1,9},{2,10},{3,11},{4,12},{5,13},{6,14},{7,15},{8,0},{9,1},... | collective-permute-start | bytes 98312 | tf_op jit(solution)/shard_map/ppermute | solution.py:274
  54.5 7.4 %copy-start.1 = (bf16[128,3072]{1,0:T(8,128)(2,1)S(1)}, bf16[128,3072]{1,0:T(8,128)(2,1)}, u32[]{:S(2)}) copy-start(bf16[128,3072]{1,0:T(8,128)(2,1)} %grads_hbm.1) | copy-start | bytes 2359300
  54.5 7.4 %copy-start.5 = (bf16[128,2048]{1,0:T(8,128)(2,1)S(1)}, bf16[128,2048]{1,0:T(8,128)(2,1)}, u32[]{:S(2)}) copy-start(bf16[128,2048]{1,0:T(8,128)(2,1)} %acts_hbm.1) | copy-start | bytes 1572868
  54.5 7.4 %copy-start.6 = (s32[4]{0:T(128)S(1)}, s32[4]{0:T(128)}, u32[]{:S(2)}) copy-start(s32[4]{0:T(128)} %pad_add_fusion.place) | copy-start | bytes 52
  54.7 0.7 copy-start.7
  66.5 8.8 %collective-permute-start.6 = (f32[64,4096]{1,0:T(8,128)}, f32[64,4096]{1,0:T(8,128)S(1)}, u32[]{:S(2)}, u32[]{:S(2)}) collective-permute-start(f32[64,4096]{1,0:T(8,128)} %get-tuple-element.30), channel_id=1, source_target_pairs={{0,128},{128,0},{1,129},{129,1},{2,130},{130,2},{3,131},{131,3},{4... | collective-permute-start | bytes 3145736 | tf_op jit(solution)/shard_map/ppermute | solution.py:270
  71.8 18.8 %all-to-all-start.1 = ((bf16[4,128,1024]{2,1,0:T(8,128)(2,1)}), bf16[4,128,1024]{2,1,0:T(8,128)(2,1)S(1)}, u32[]{:S(2)}, u32[]{:S(2)}) async-start(bf16[4,128,1024]{2,1,0:T(8,128)(2,1)} %shard_map.60), calls=%async_computation.1 | async-start | bytes 2097152 | tf_op jit(solution)/shard_map/all_to_all | solution.py:296
  75.4 0.8 copy-start.2
  91.9 30.0 %all-to-all-start.2 = ((bf16[8,16,1024]{2,1,0:T(8,128)(2,1)}), bf16[8,16,1024]{2,1,0:T(8,128)(2,1)S(1)}, u32[]{:S(2)}, u32[]{:S(2)}) async-start(bf16[8,16,1024]{2,1,0:T(8,128)(2,1)} %bitcast.7), calls=%async_computation.2 | async-start | bytes 524288 | tf_op jit(solution)/shard_map/all_to_all | solution.py:304
  97.2 22.8 %collective-permute-start.7 = (bf16[32,4096]{1,0:T(8,128)(2,1)S(1)}, bf16[32,4096]{1,0:T(8,128)(2,1)S(1)}, u32[]{:S(2)}, u32[]{:S(2)}) collective-permute-start(bf16[32,4096]{1,0:T(8,128)(2,1)S(1)} %get-tuple-element.34), channel_id=1, source_target_pairs={{0,256},{256,0},{1,257},{257,1},{2,258},{258,2},{3,259},{259,3},{4... | collective-permute-start | bytes 786440 | tf_op jit(solution)/shard_map/ppermute | solution.py:270
  120.0 1.0 copy-start.3

commit v7 on v6

--- a/solution.py
+++ b/solution.py
@@ -281,26 +281,28 @@
 
     total, send = prepare(acts_in, grad_out)
     total = total + across(send, 1, 0, 1).astype(F32)
-    total = total + across(total.astype(BF), 2, 0, 3).astype(F32)
+    send, share = barrier((total.astype(BF), share))
+    total = total + across(send, 2, 0, 3).astype(F32)
+    near = product(place, grad_out, weight, weight_far)
     total = total + across(total.astype(BF), 7, 1, 0).astype(F32)
     left, right = total[0], total[1]
-    left = left + across(left.astype(BF), 0, 2, 0).astype(F32)
+    send, near = barrier((left.astype(BF), near))
+    left = left + across(send, 0, 2, 0).astype(F32)
 
     share = jnp.broadcast_to(share[None], (8,) + share.shape)
-    share, near_tokens = barrier((share, grad_out))
     far_tokens = lax.all_to_all(share, "row", 0, 0, tiled=True)
-    near = product(place, near_tokens, weight, weight_far)
+
+    keep, send = stats(place, left, right, acts, grad_out)
+    send, far_tokens = barrier((send, far_tokens))
     both = product(place, far_tokens, weight, weight_far, near)
-
-    left, right, both = barrier((left, right, both))
+    near_rows, far_rows = core_sum(keep, swap(send, "core"))
+    both, near_rows = barrier((both, near_rows))
+    far_rows = swap(far_rows, "yh")
     got = lax.all_to_all(both, "x", 0, 0, tiled=True)
-    keep, send = stats(place, left, right, acts, grad_out)
-    near_rows, far_rows = core_sum(keep, swap(send, "core"))
-    got, near_rows = barrier((got, near_rows))
-    far_rows = swap(far_rows, "yh")
 
     chunks = x_sum(place, got)
     chunks = chunks.reshape(8, -1, chunks.shape[2])
+    chunks, far_rows = barrier((chunks, far_rows))
     input_grad = y_sum(lax.all_to_all(chunks, ("yh", "yl"), 0, 0, tiled=True))
 
     left_stats, right_stats = last_sum(near_rows, far_rows, hidden, width)

time: 123 us -> 116 us (0.943); the launches traced: 123 us -> 114 us
  waiting for transfers between devices: 37.7 us -> 27 us
  starting transfers between devices: 56 us -> 60.8 us
  local copies, waits for them, and re-layouts: 6.36 us -> 4.79 us
    ppermute x4, waiting for transfers between devices: 15.5 us -> 4.05 us  [swap(): return lax.ppermute(value, axis, [(0, 1), (1, 0)])]
    all_to_all x1, waiting for transfers between devices: 0.01 us -> 9.73 us  [body(): input_grad = y_sum(lax.all_to_all(chunks, ('yh', 'yl'), 0, 0, tiled=True))]
    all_to_all x1, waiting for transfers between devices: 14.3 us -> 8.37 us  [body(): got = lax.all_to_all(both, 'x', 0, 0, tiled=True)]
    ppermute x4, starting transfers between devices: 14.1 us -> 19.5 us  [across(): return lax.ppermute(value, ('row', 'yl', 'x'), perm)]
    all_to_all x1, starting transfers between devices: 5.36 us -> 9.3 us  [body(): input_grad = y_sum(lax.all_to_all(chunks, ('yh', 'yl'), 0, 0, tiled=True))]
    ppermute x4, starting transfers between devices: 28.8 us -> 25 us  [swap(): return lax.ppermute(value, axis, [(0, 1), (1, 0)])]
    ppermute x4, waiting for transfers between devices: 7.71 us -> 4.82 us  [across(): return lax.ppermute(value, ('row', 'yl', 'x'), perm)]
    unnamed x16, local copies, waits for them, and re-layouts: 4.77 us -> 3.2 us
  transfers between devices with their start and end apart: 11 -> 11, of which waited for: 5 -> 5; matrix products, arithmetic and copies ran while one was open for 2% -> 2% of each run, Pallas kernels for 6% -> 17%
where the time goes in v7:
time: 116 us; the launch traced here: 114 us
  starting transfers between devices  60.8 us (52%)
  waiting for transfers between devices  27 us (23%)
  Pallas kernels  20.1 us (17%)
  local copies, waits for them, and re-layouts  4.79 us (4%)
    ppermute x4, starting transfers between devices, swap(): return lax.ppermute(value, axis, [(0, 1), (1, 0)])  25 us
    ppermute x4, starting transfers between devices, across(): return lax.ppermute(value, ('row', 'yl', 'x'), perm)  19.5 us
    pallas_call x2, Pallas kernels, product(): pl.pallas_call(product_kernel, out_shape=jax.ShapeDtypeStruct((4, count,...  13.1 us
    all_to_all x1, waiting for transfers between devices, body(): input_grad = y_sum(lax.all_to_all(chunks, ('yh', 'yl'), 0, 0, tiled=True))  9.73 us
    all_to_all x1, starting transfers between devices, body(): input_grad = y_sum(lax.all_to_all(chunks, ('yh', 'yl'), 0, 0, tiled=True))  9.3 us
    all_to_all x1, waiting for transfers between devices, body(): got = lax.all_to_all(both, 'x', 0, 0, tiled=True)  8.37 us
    ppermute x4, waiting for transfers between devices, across(): return lax.ppermute(value, ('row', 'yl', 'x'), perm)  4.82 us
    ppermute x4, waiting for transfers between devices, swap(): return lax.ppermute(value, axis, [(0, 1), (1, 0)])  4.05 us
  transfers between devices with their start and end apart: 11, of which 5 were waited for; matrix products, arithmetic and copies ran while one was open for 2% of the time, Pallas kernels for 17%

profile of v7, /device:TPU:1, one launch (start us, length us, event | category | flops | bytes accessed | tf_op | source)
XLA Modules:
  0.0 114.3 jit_solution(5366488315249984732)
XLA Ops:
  0.6 8.8 %collective-permute-start.4 = (bf16[2048,768]{1,0:T(8,128)(2,1)}, bf16[2048,768]{1,0:T(8,128)(2,1)}, u32[]{:S(2)}, u32[]{:S(2)}) collective-permute-start(bf16[2048,768]{1,0:T(8,128)(2,1)} %bitcast.14), channel_id=1, source_target_pairs={{0,128},{128,0},{1,129},{129,1},{2,130},{130,2},{3,131},{131,3},{4... | collective-permute-start | bytes 9437192 | tf_op jit(solution)/shard_map/ppermute | solution.py:270
  10.2 1.1 copy-done
  11.4 1.0 copy-done.2
  12.9 1.9 %collective-permute-start = (bf16[2,128,128]{2,1,0:T(8,128)(2,1)S(1)}, bf16[2,128,128]{2,1,0:T(8,128)(2,1)S(1)}, u32[]{:S(2)}, u32[]{:S(2)}) collective-permute-start(bf16[2,128,128]{2,1,0:T(8,128)(2,1)S(1)} %get-tuple-element.25), channel_id=1, source_target_pairs={{0,17},{1,16},{2,19},{3,18},{4,21},{5,20},{6,23},{7,22},{8,25},{9,... | collective-permute-start | bytes 196616 | tf_op jit(solution)/shard_map/ppermute | solution.py:274
  14.9 5.1 %collective-permute-start.1 = (bf16[16,1536]{1,0:T(8,128)(2,1)S(1)}, bf16[16,1536]{1,0:T(8,128)(2,1)S(1)}, u32[]{:S(2)}, u32[]{:S(2)}) collective-permute-start(bf16[16,1536]{1,0:T(8,128)(2,1)S(1)} %dynamic_slice.3), channel_id=1, source_target_pairs={{0,256},{256,0},{1,257},{257,1},{2,258},{258,2},{3,259},{259,3},{4... | collective-permute-start | bytes 147464 | tf_op jit(solution)/shard_map/ppermute | solution.py:270
  20.0 4.0 %collective-permute-done.1 = bf16[16,1536]{1,0:T(8,128)(2,1)S(1)} collective-permute-done((bf16[16,1536]{1,0:T(8,128)(2,1)S(1)}, bf16[16,1536]{1,0:T(8,128)(2,1)S(1)}, u32[]{:S(2)}, u32[]{:S(2)}) %collective-permute-start.1) | collective-permute-done | bytes 49184 | tf_op jit(solution)/shard_map/ppermute | solution.py:270
  24.0 4.8 %collective-permute-start.2 = (bf16[2,128,128]{2,1,0:T(8,128)(2,1)S(1)}, bf16[2,128,128]{2,1,0:T(8,128)(2,1)S(1)}, u32[]{:S(2)}, u32[]{:S(2)}) collective-permute-start(bf16[2,128,128]{2,1,0:T(8,128)(2,1)S(1)} %fusion), channel_id=1, source_target_pairs={{0,35},{1,34},{2,33},{3,32},{4,39},{5,38},{6,37},{7,36},{8,43},{9,... | collective-permute-start | bytes 196616 | tf_op jit(solution)/shard_map/ppermute | solution.py:274
  28.8 3.2 %collective-permute-done.2 = bf16[2,128,128]{2,1,0:T(8,128)(2,1)S(1)} collective-permute-done((bf16[2,128,128]{2,1,0:T(8,128)(2,1)S(1)}, bf16[2,128,128]{2,1,0:T(8,128)(2,1)S(1)}, u32[]{:S(2)}, u32[]{:S(2)}) %collective-permute-start.2) | collective-permute-done | bytes 65568 | tf_op jit(solution)/shard_map/ppermute | solution.py:274
  32.1 7.1 %collective-permute-start.3 = (bf16[2,128,128]{2,1,0:T(8,128)(2,1)S(1)}, bf16[2,128,128]{2,1,0:T(8,128)(2,1)S(1)}, u32[]{:S(2)}, u32[]{:S(2)}) collective-permute-start(bf16[2,128,128]{2,1,0:T(8,128)(2,1)S(1)} %fusion.2), channel_id=1, source_target_pairs={{0,116},{1,117},{2,118},{3,119},{4,112},{5,113},{6,114},{7,115},{8... | collective-permute-start | bytes 196616 | tf_op jit(solution)/shard_map/ppermute | solution.py:274
  40.7 3.5 %all-to-all-start = ((bf16[8,16,1536]{2,1,0:T(8,128)(2,1)}), bf16[8,16,1536]{2,1,0:T(8,128)(2,1)S(1)}, u32[]{:S(2)}, u32[]{:S(2)}) async-start(bf16[8,16,1536]{2,1,0:T(8,128)(2,1)} %broadcast_in_dim.2), calls=%async_computation | async-start | bytes 786432 | tf_op jit(solution)/shard_map/all_to_all | solution.py:293
  44.2 6.6 %shard_map.59.rest_0_ = bf16[4,128,1024]{2,1,0:T(8,128)(2,1)} custom-call(s32[4]{0:T(128)} %pad_add_fusion.place, bf16[128,3072]{1,0:T(8,128)(2,1)} %grads_hbm.1, bf16[2048,768]{1,0:T(8,128)(2,1)} %bitcast.15, bf16[2048,768]{1,0:T(8,128)(2,1)} %bitcast.16, bf16[2048,768]{1,0:T(8,128)(2,1)} %collective-permute-done.4.far_lo.far_hi, ...), custom_call_target="tpu_custom_call" | custom-call | flops 805306368 | bytes 7340032 | tf_op jit(solution)/shard_map/pallas_call | solution.py:97
  50.8 5.6 %collective-permute-start.5 = (bf16[128,128]{1,0:T(8,128)(2,1)S(1)}, bf16[128,128]{1,0:T(8,128)(2,1)S(1)}, u32[]{:S(2)}, u32[]{:S(2)}) collective-permute-start(bf16[128,128]{1,0:T(8,128)(2,1)S(1)} %fusion.1), channel_id=1, source_target_pairs={{0,8},{1,9},{2,10},{3,11},{4,12},{5,13},{6,14},{7,15},{8,0},{9,1},... | collective-permute-start | bytes 98312 | tf_op jit(solution)/shard_map/ppermute | solution.py:274
  56.5 1.6 %collective-permute-done.5 = bf16[128,128]{1,0:T(8,128)(2,1)S(1)} collective-permute-done((bf16[128,128]{1,0:T(8,128)(2,1)S(1)}, bf16[128,128]{1,0:T(8,128)(2,1)S(1)}, u32[]{:S(2)}, u32[]{:S(2)}) %collective-permute-start.5) | collective-permute-done | bytes 32800 | tf_op jit(solution)/shard_map/ppermute | solution.py:274
  58.1 3.5 %shard_map.60 = (f32[64,4096]{1,0:T(8,128)S(1)}, f32[64,4096]{1,0:T(8,128)S(1)}) custom-call(s32[4]{0:T(128)S(1)} %copy-done.4, f32[128,128]{1,0:T(8,128)S(1)} %convert_add_fusion.3.left_ref, f32[128,128]{1,0:T(8,128)S(1)} %slice_bitcast_fusion.right_ref, bf16[128,2048]{1,0:T(8,128)(2,1)S(1)} %copy-done.3, bf16[128,3072]{1,0:T(8,128)(2,1)S(1)} %copy-done.1), custom_call_target="tpu_custom_call" | custom-call | flops 1048576000 | bytes 5242880 | tf_op jit(solution)/shard_map/pallas_call | solution.py:202
  61.7 1.0 copy-done.6
  62.7 4.3 %collective-permute-start.6 = (f32[64,4096]{1,0:T(8,128)}, f32[64,4096]{1,0:T(8,128)S(1)}, u32[]{:S(2)}, u32[]{:S(2)}) collective-permute-start(f32[64,4096]{1,0:T(8,128)} %copy-done.6), channel_id=1, source_target_pairs={{0,128},{128,0},{1,129},{129,1},{2,130},{130,2},{3,131},{131,3},{4... | collective-permute-start | bytes 3145736 | tf_op jit(solution)/shard_map/ppermute | solution.py:270
  67.0 6.5 %shard_map.61 = bf16[4,128,1024]{2,1,0:T(8,128)(2,1)} custom-call(s32[4]{0:T(128)} %pad_add_fusion.place, bf16[8,16,1536]{2,1,0:T(8,128)(2,1)} %copy-done.7, bf16[2048,768]{1,0:T(8,128)(2,1)} %bitcast.17, bf16[2048,768]{1,0:T(8,128)(2,1)} %bitcast.18, bf16[2048,768]{1,0:T(8,128)(2,1)} %collective-permute-done.4.far_lo.far_hi, ...), custom_call_target="tpu_custom_call", output_to_operand_aliasing={{}: (6, {})} | custom-call | flops 805306368 | bytes 7340032 | tf_op jit(solution)/shard_map/pallas_call | solution.py:97
  73.6 3.5 %all-to-all-start.1 = ((bf16[4,128,1024]{2,1,0:T(8,128)(2,1)}), bf16[4,128,1024]{2,1,0:T(8,128)(2,1)S(1)}, u32[]{:S(2)}, u32[]{:S(2)}) async-start(bf16[4,128,1024]{2,1,0:T(8,128)(2,1)} %shard_map.61), calls=%async_computation.1 | async-start | bytes 2097152 | tf_op jit(solution)/shard_map/all_to_all | solution.py:301
  77.1 6.8 %collective-permute-start.7 = (bf16[32,4096]{1,0:T(8,128)(2,1)S(1)}, bf16[32,4096]{1,0:T(8,128)(2,1)S(1)}, u32[]{:S(2)}, u32[]{:S(2)}) collective-permute-start(bf16[32,4096]{1,0:T(8,128)(2,1)S(1)} %get-tuple-element.37), channel_id=1, source_target_pairs={{0,256},{256,0},{1,257},{257,1},{2,258},{258,2},{3,259},{259,3},{4... | collective-permute-start | bytes 786440 | tf_op jit(solution)/shard_map/ppermute | solution.py:270
  84.0 8.4 %all-to-all-done.1.got_ref = bf16[4,128,1024]{2,1,0:T(8,128)(2,1)S(1)} async-done(((bf16[4,128,1024]{2,1,0:T(8,128)(2,1)}), bf16[4,128,1024]{2,1,0:T(8,128)(2,1)S(1)}, u32[]{:S(2)}, u32[]{:S(2)}) %all-to-all-start.1) | async-done | bytes 1048608 | tf_op jit(solution)/shard_map/all_to_all | solution.py:301
  92.4 1.4 %shard_map.63 = bf16[2,64,1024]{2,1,0:T(8,128)(2,1)} custom-call(s32[4]{0:T(128)S(1)} %copy-done.5, bf16[4,128,1024]{2,1,0:T(8,128)(2,1)S(1)} %all-to-all-done.1.got_ref), custom_call_target="tpu_custom_call" | custom-call | flops 1048576 | bytes 2097152 | tf_op jit(solution)/shard_map/pallas_call | solution.py:125
  93.7 9.3 %all-to-all-start.2 = ((bf16[8,16,1024]{2,1,0:T(8,128)(2,1)}), bf16[8,16,1024]{2,1,0:T(8,128)(2,1)S(1)}, u32[]{:S(2)}, u32[]{:S(2)}) async-start(bf16[8,16,1024]{2,1,0:T(8,128)(2,1)} %bitcast.7), calls=%async_computation.2 | async-start | bytes 524288 | tf_op jit(solution)/shard_map/all_to_all | solution.py:306
  103.0 0.8 shard_map.65
  103.9 9.7 %all-to-all-done.2.got_ref = bf16[8,16,1024]{2,1,0:T(8,128)(2,1)S(1)} async-done(((bf16[8,16,1024]{2,1,0:T(8,128)(2,1)}), bf16[8,16,1024]{2,1,0:T(8,128)(2,1)S(1)}, u32[]{:S(2)}, u32[]{:S(2)}) %all-to-all-start.2) | async-done | bytes 262176 | tf_op jit(solution)/shard_map/all_to_all | solution.py:306
  (31 shorter events, 3.6 us)
Async XLA Ops:
  0.6 43.6 %collective-permute-start.4 = (bf16[2048,768]{1,0:T(8,128)(2,1)}, bf16[2048,768]{1,0:T(8,128)(2,1)}, u32[]{:S(2)}, u32[]{:S(2)}) collective-permute-start(bf16[2048,768]{1,0:T(8,128)(2,1)} %bitcast.14), channel_id=1, source_target_pairs={{0,128},{128,0},{1,129},{129,1},{2,130},{130,2},{3,131},{131,3},{4... | collective-permute-start | bytes 9437192 | tf_op jit(solution)/shard_map/ppermute | solution.py:270
  10.2 1.1 copy-start
  11.4 1.0 copy-start.2
  12.9 7.0 %collective-permute-start = (bf16[2,128,128]{2,1,0:T(8,128)(2,1)S(1)}, bf16[2,128,128]{2,1,0:T(8,128)(2,1)S(1)}, u32[]{:S(2)}, u32[]{:S(2)}) collective-permute-start(bf16[2,128,128]{2,1,0:T(8,128)(2,1)S(1)} %get-tuple-element.25), channel_id=1, source_target_pairs={{0,17},{1,16},{2,19},{3,18},{4,21},{5,20},{6,23},{7,22},{8,25},{9,... | collective-permute-start | bytes 196616 | tf_op jit(solution)/shard_map/ppermute | solution.py:274
  14.9 9.2 %collective-permute-start.1 = (bf16[16,1536]{1,0:T(8,128)(2,1)S(1)}, bf16[16,1536]{1,0:T(8,128)(2,1)S(1)}, u32[]{:S(2)}, u32[]{:S(2)}) collective-permute-start(bf16[16,1536]{1,0:T(8,128)(2,1)S(1)} %dynamic_slice.3), channel_id=1, source_target_pairs={{0,256},{256,0},{1,257},{257,1},{2,258},{258,2},{3,259},{259,3},{4... | collective-permute-start | bytes 147464 | tf_op jit(solution)/shard_map/ppermute | solution.py:270
  24.0 8.0 %collective-permute-start.2 = (bf16[2,128,128]{2,1,0:T(8,128)(2,1)S(1)}, bf16[2,128,128]{2,1,0:T(8,128)(2,1)S(1)}, u32[]{:S(2)}, u32[]{:S(2)}) collective-permute-start(bf16[2,128,128]{2,1,0:T(8,128)(2,1)S(1)} %fusion), channel_id=1, source_target_pairs={{0,35},{1,34},{2,33},{3,32},{4,39},{5,38},{6,37},{7,36},{8,43},{9,... | collective-permute-start | bytes 196616 | tf_op jit(solution)/shard_map/ppermute | solution.py:274
  32.1 12.1 %collective-permute-start.3 = (bf16[2,128,128]{2,1,0:T(8,128)(2,1)S(1)}, bf16[2,128,128]{2,1,0:T(8,128)(2,1)S(1)}, u32[]{:S(2)}, u32[]{:S(2)}) collective-permute-start(bf16[2,128,128]{2,1,0:T(8,128)(2,1)S(1)} %fusion.2), channel_id=1, source_target_pairs={{0,116},{1,117},{2,118},{3,119},{4,112},{5,113},{6,114},{7,115},{8... | collective-permute-start | bytes 196616 | tf_op jit(solution)/shard_map/ppermute | solution.py:274
  40.7 22.0 %all-to-all-start = ((bf16[8,16,1536]{2,1,0:T(8,128)(2,1)}), bf16[8,16,1536]{2,1,0:T(8,128)(2,1)S(1)}, u32[]{:S(2)}, u32[]{:S(2)}) async-start(bf16[8,16,1536]{2,1,0:T(8,128)(2,1)} %broadcast_in_dim.2), calls=%async_computation | async-start | bytes 786432 | tf_op jit(solution)/shard_map/all_to_all | solution.py:293
  44.2 13.9 %copy-start.1 = (bf16[128,3072]{1,0:T(8,128)(2,1)S(1)}, bf16[128,3072]{1,0:T(8,128)(2,1)}, u32[]{:S(2)}) copy-start(bf16[128,3072]{1,0:T(8,128)(2,1)} %grads_hbm.1) | copy-start | bytes 2359300
  44.2 13.9 %copy-start.3 = (bf16[128,2048]{1,0:T(8,128)(2,1)S(1)}, bf16[128,2048]{1,0:T(8,128)(2,1)}, u32[]{:S(2)}) copy-start(bf16[128,2048]{1,0:T(8,128)(2,1)} %acts_hbm.1) | copy-start | bytes 1572868
  44.2 13.9 %copy-start.4 = (s32[4]{0:T(128)S(1)}, s32[4]{0:T(128)}, u32[]{:S(2)}) copy-start(s32[4]{0:T(128)} %pad_add_fusion.place) | copy-start | bytes 52
  50.8 7.2 %collective-permute-start.5 = (bf16[128,128]{1,0:T(8,128)(2,1)S(1)}, bf16[128,128]{1,0:T(8,128)(2,1)S(1)}, u32[]{:S(2)}, u32[]{:S(2)}) collective-permute-start(bf16[128,128]{1,0:T(8,128)(2,1)S(1)} %fusion.1), channel_id=1, source_target_pairs={{0,8},{1,9},{2,10},{3,11},{4,12},{5,13},{6,14},{7,15},{8,0},{9,1},... | collective-permute-start | bytes 98312 | tf_op jit(solution)/shard_map/ppermute | solution.py:274
  61.6 1.0 copy-start.6
  62.7 4.3 %copy-start.7 = (bf16[8,16,1536]{2,1,0:T(8,128)(2,1)}, bf16[8,16,1536]{2,1,0:T(8,128)(2,1)S(1)}, u32[]{:S(2)}) copy-start(bf16[8,16,1536]{2,1,0:T(8,128)(2,1)S(1)} %all-to-all-done.tokens_ref) | copy-start | bytes 1179652
  62.7 10.8 %collective-permute-start.6 = (f32[64,4096]{1,0:T(8,128)}, f32[64,4096]{1,0:T(8,128)S(1)}, u32[]{:S(2)}, u32[]{:S(2)}) collective-permute-start(f32[64,4096]{1,0:T(8,128)} %copy-done.6), channel_id=1, source_target_pairs={{0,128},{128,0},{1,129},{129,1},{2,130},{130,2},{3,131},{131,3},{4... | collective-permute-start | bytes 3145736 | tf_op jit(solution)/shard_map/ppermute | solution.py:270
  73.5 18.9 %copy-start.5 = (s32[4]{0:T(128)S(1)}, s32[4]{0:T(128)}, u32[]{:S(2)}) copy-start(s32[4]{0:T(128)} %pad_add_fusion.place) | copy-start | bytes 52
  73.6 18.8 %all-to-all-start.1 = ((bf16[4,128,1024]{2,1,0:T(8,128)(2,1)}), bf16[4,128,1024]{2,1,0:T(8,128)(2,1)S(1)}, u32[]{:S(2)}, u32[]{:S(2)}) async-start(bf16[4,128,1024]{2,1,0:T(8,128)(2,1)} %shard_map.61), calls=%async_computation.1 | async-start | bytes 2097152 | tf_op jit(solution)/shard_map/all_to_all | solution.py:301
  77.1 16.6 %collective-permute-start.7 = (bf16[32,4096]{1,0:T(8,128)(2,1)S(1)}, bf16[32,4096]{1,0:T(8,128)(2,1)S(1)}, u32[]{:S(2)}, u32[]{:S(2)}) collective-permute-start(bf16[32,4096]{1,0:T(8,128)(2,1)S(1)} %get-tuple-element.37), channel_id=1, source_target_pairs={{0,256},{256,0},{1,257},{257,1},{2,258},{258,2},{3,259},{259,3},{4... | collective-permute-start | bytes 786440 | tf_op jit(solution)/shard_map/ppermute | solution.py:270
  93.7 19.9 %all-to-all-start.2 = ((bf16[8,16,1024]{2,1,0:T(8,128)(2,1)}), bf16[8,16,1024]{2,1,0:T(8,128)(2,1)S(1)}, u32[]{:S(2)}, u32[]{:S(2)}) async-start(bf16[8,16,1024]{2,1,0:T(8,128)(2,1)} %bitcast.7), calls=%async_computation.2 | async-start | bytes 524288 | tf_op jit(solution)/shard_map/all_to_all | solution.py:306

commit v8 on v6

--- a/solution.py
+++ b/solution.py
@@ -46,68 +46,58 @@
     )(acts, grads)
 
 
-def product_kernel(place, tokens_ref, near_lo, near_hi, far_lo, far_hi, *rest):
-    out_ref, low, high = rest[-3:]
-    quarter = near_lo.shape[1]
+def product_kernel(place, near_ref, far_ref, own_lo, own_hi, other_lo, other_hi, out_ref, low, high):
+    quarter = own_lo.shape[1]
+    half = near_ref.shape[0]
 
     def piece(core):
         lanes = pl.ds(pl.multiple_of(core * quarter, quarter), quarter)
-        if len(tokens_ref.shape) == 3:
-            return tokens_ref[:, :, lanes].reshape(-1, quarter)
-        return tokens_ref[:, lanes]
+        return jnp.concatenate([near_ref[:, lanes], far_ref[:, :, lanes].reshape(half, quarter)], axis=0)
 
     own, other = piece(place[1]), piece(1 - place[1])
 
-    def dot(near, far):
-        return lax.dot_general(own, near[...], NT, preferred_element_type=F32) + lax.dot_general(
-            other, far[...], NT, preferred_element_type=F32
+    def dot(first, second):
+        return lax.dot_general(own, first[...], NT, preferred_element_type=F32) + lax.dot_general(
+            other, second[...], NT, preferred_element_type=F32
         )
 
-    low[...] = dot(near_lo, far_lo)
-    high[...] = dot(near_hi, far_hi)
+    low[...] = dot(own_lo, other_lo)
+    high[...] = dot(own_hi, other_hi)
     for x in range(4):
-        for y in range(4):
+        for y in range(8):
             rows = slice((y * 4 + x) * 8, (y * 4 + x) * 8 + 8)
             pair = jnp.concatenate([low[rows, :], high[rows, :]], axis=0).astype(BF)
             out_ref[x, y * 16 : y * 16 + 16, :] = pair
 
 
-def product(place, tokens, weight, weight_far, first=None):
+def product(place, near, far, weight, weight_far):
     features, quarter = weight.shape
     half = features // 2
     step = 256
     steps = half // step
     low = pl.BlockSpec((step, quarter), lambda j, place: (j, 0))
     high = pl.BlockSpec((step, quarter), lambda j, place: (j + steps, 0))
-    if tokens.ndim == 3:
-        count = tokens.shape[0] * tokens.shape[1]
-        token_spec = pl.BlockSpec(tokens.shape[:2] + (2 * quarter,), lambda j, place: (0, 0, 0))
-    else:
-        count = tokens.shape[0]
-        token_spec = pl.BlockSpec((count, 2 * quarter), lambda j, place: (0, place[0]))
-    in_specs = [token_spec, low, high, low, high]
-    args = (place, tokens, weight, weight, weight_far, weight_far)
-    part = 0
-    aliases = {}
-    if first is not None:
-        in_specs.append(pl.BlockSpec(memory_space=pl.ANY))
-        args += (first,)
-        part = 1
-        aliases = {6: 0}
+    count = near.shape[0]
     return pl.pallas_call(
         product_kernel,
         out_shape=jax.ShapeDtypeStruct((4, count, half), BF),
         grid_spec=pltpu.PrefetchScalarGridSpec(
             num_scalar_prefetch=1,
             grid=(steps,),
-            in_specs=in_specs,
-            out_specs=pl.BlockSpec((4, count // 2, step), lambda j, place: (0, part, j)),
-            scratch_shapes=[pltpu.VMEM((count, step), F32)] * 2,
+            in_specs=[
+                pl.BlockSpec((count, 2 * quarter), lambda j, place: (0, place[0])),
+                pl.BlockSpec(far.shape, lambda j, place: (0, 0, 0)),
+                low,
+                high,
+                low,
+                high,
+            ],
+            out_specs=pl.BlockSpec((4, count, step), lambda j, place: (0, 0, j)),
+            scratch_shapes=[pltpu.VMEM((2 * count, step), F32)] * 2,
         ),
-        input_output_aliases=aliases,
         compiler_params=params(60),
-        cost_estimate=cost(4 * count * features * quarter, 7 * MB),
-    )(*args)
+        cost_estimate=cost(8 * count * features * quarter, 8 * MB),
+    )(place, near, far, weight, weight, weight_far, weight_far)
 
 
 def x_sum_kernel(place, got_ref, out_ref):
@@ -161,7 +151,7 @@
     return jnp.where(unit == wanted, 1.0, 0.0).astype(BF)
 
 
-def stats_kernel(place, left_ref, right_ref, acts_hbm, grads_hbm, keep_ref, send_ref, acts_ref, grads_ref, sems):
+def stats_kernel(place, total_ref, pair_ref, left2_ref, left3_ref, acts_hbm, grads_hbm, keep_ref, send_ref, acts_ref, grads_ref, sems):
     hidden = grads_ref.shape[1]
     width = acts_ref.shape[1]
     copies = []
@@ -176,7 +166,8 @@
         picked = lax.dot_general(pick, data, NT, preferred_element_type=F32).astype(BF)
         return jnp.dot(picked, mix, preferred_element_type=F32) * (1.0 / TOKENS)
 
-    right = (right_ref[...] / D).astype(BF)
+    right = total_ref[1] + pair_ref[1].astype(F32)
+    right = (right / D).astype(BF)
     pick = picker(place, place[2], 32, 8)
     for j in range(hidden // BLOCK):
         lanes = slice(j * BLOCK, (j + 1) * BLOCK)
@@ -184,7 +175,8 @@
         out = rows(pick, right, grads_ref[:, lanes])
         keep_ref[:, lanes] = out[:64]
         send_ref[:, lanes] = out[64:]
-    left = (left_ref[...] / FF).astype(BF)
+    left = total_ref[0] + pair_ref[0].astype(F32) + left2_ref[...].astype(F32) + left3_ref[...].astype(F32)
+    left = (left / FF).astype(BF)
     pick = picker(place, place[3], 16, 16)
     for j in range(width // BLOCK):
         copies[hidden // BLOCK + j].wait()
@@ -195,14 +187,14 @@
             send_ref[at, hidden:] = out[32 + dy * 16 : 32 + dy * 16 + 16]
 
 
-def stats(place, left, right, acts, grads):
+def stats(place, total, pair, left2, left3, acts, grads):
     shape = jax.ShapeDtypeStruct((64, grads.shape[1] + BLOCK), F32)
     vmem = pl.BlockSpec(memory_space=pltpu.VMEM)
     hbm = pl.BlockSpec(memory_space=pltpu.HBM)
     return pl.pallas_call(
         stats_kernel,
         out_shape=(shape, shape),
-        in_specs=[pl.BlockSpec(memory_space=pltpu.SMEM), vmem, vmem, hbm, hbm],
+        in_specs=[pl.BlockSpec(memory_space=pltpu.SMEM)] + [vmem] * 4 + [hbm, hbm],
         out_specs=[vmem, vmem],
         scratch_shapes=[
             pltpu.VMEM(acts.shape, BF),
@@ -211,7 +203,7 @@
         ],
         compiler_params=params(16),
         cost_estimate=cost(1000 * MB, 5 * MB),
-    )(place, left, right, acts, grads)
+    )(place, total, pair, left2, left3, acts, grads)
 
 
 def core_sum_kernel(keep_ref, got_ref, near_ref, far_ref):
@@ -280,22 +272,23 @@
     weight_far = swap(weight, "core")
 
     total, send = prepare(acts_in, grad_out)
-    total = total + across(send, 1, 0, 1).astype(F32)
-    total = total + across(total.astype(BF), 2, 0, 3).astype(F32)
-    total = total + across(total.astype(BF), 7, 1, 0).astype(F32)
-    left, right = total[0], total[1]
-    left = left + across(left.astype(BF), 0, 2, 0).astype(F32)
-
     share = jnp.broadcast_to(share[None], (8,) + share.shape)
-    share, near_tokens = barrier((share, grad_out))
+    send, share = barrier((send, share))
     far_tokens = lax.all_to_all(share, "row", 0, 0, tiled=True)
-    near = product(place, near_tokens, weight, weight_far)
-    both = product(place, far_tokens, weight, weight_far, near)
-
-    left, right, both = barrier((left, right, both))
+    parts = [across(send, r, 0, r).astype(F32) for r in (1, 2, 3)]
+    total = total + parts[0] + parts[1] + parts[2]
+    send = total.astype(BF)
+    pair = across(send, 7, 1, 0)
+    left2 = across(send[0], 0, 2, 0)
+
+    both = product(place, grad_out, far_tokens, weight, weight_far)
+    both, last = barrier((both, send[0]))
+    left3 = across(last, 0, 3, 0)
     got = lax.all_to_all(both, "x", 0, 0, tiled=True)
-    keep, send = stats(place, left, right, acts, grad_out)
-    near_rows, far_rows = core_sum(keep, swap(send, "core"))
+
+    keep, send = stats(place, total, pair, left2, left3, acts, grad_out)
+    back, got = barrier((swap(send, "core"), got))
+    near_rows, far_rows = core_sum(keep, back)
     got, near_rows = barrier((got, near_rows))
     far_rows = swap(far_rows, "yh")
 

time: 123 us -> 127 us (1.033)
  blocking collectives: 0 us -> 17.4 us
  waiting for transfers between devices: 37.7 us -> 29.7 us
  Pallas kernels: 20.9 us -> 13.6 us
  starting transfers between devices: 56 us -> 59.8 us
  local copies, waits for them, and re-layouts: 6.36 us -> 4.5 us
    all_to_all x0 -> x1, blocking collectives: none -> 17.4 us  [body(): got = lax.all_to_all(both, 'x', 0, 0, tiled=True)]
    all_to_all x1 -> x0, waiting for transfers between devices: 14.3 us -> none  [body(): got = lax.all_to_all(both, 'x', 0, 0, tiled=True)]
    ppermute x4 -> x6, starting transfers between devices: 14.1 us -> 24.2 us  [across(): return lax.ppermute(value, ('row', 'yl', 'x'), perm)]
    pallas_call x2 -> x1, Pallas kernels: 12.9 us -> 6.56 us  [product(): pl.pallas_call(product_kernel, out_shape=jax.ShapeDtypeStruct((4, count,...]
    ppermute x4, waiting for transfers between devices: 15.5 us -> 19.9 us  [swap(): return lax.ppermute(value, axis, [(0, 1), (1, 0)])]
    ppermute x4, starting transfers between devices: 28.8 us -> 24.8 us  [swap(): return lax.ppermute(value, axis, [(0, 1), (1, 0)])]
    all_to_all x1 -> x0, starting transfers between devices: 3.53 us -> none  [body(): got = lax.all_to_all(both, 'x', 0, 0, tiled=True)]
    ppermute x4 -> x6, waiting for transfers between devices: 7.71 us -> 9.81 us  [across(): return lax.ppermute(value, ('row', 'yl', 'x'), perm)]
  transfers between devices with their start and end apart: 11 -> 12, of which waited for: 5 -> 5; matrix products, arithmetic and copies ran while one was open for 2% -> 2% of each run, Pallas kernels for 6% -> 6%
where the time goes in v8:
time: 127 us; the launch traced here: 126 us
  starting transfers between devices  59.8 us (47%)
  waiting for transfers between devices  29.7 us (23%)
  blocking collectives  17.4 us (14%)
  Pallas kernels  13.6 us (11%)
  local copies, waits for them, and re-layouts  4.5 us (4%)
    ppermute x4, starting transfers between devices, swap(): return lax.ppermute(value, axis, [(0, 1), (1, 0)])  24.8 us
    ppermute x6, starting transfers between devices, across(): return lax.ppermute(value, ('row', 'yl', 'x'), perm)  24.2 us
    ppermute x4, waiting for transfers between devices, swap(): return lax.ppermute(value, axis, [(0, 1), (1, 0)])  19.9 us
    all_to_all x1, blocking collectives, body(): got = lax.all_to_all(both, 'x', 0, 0, tiled=True)  17.4 us
    ppermute x6, waiting for transfers between devices, across(): return lax.ppermute(value, ('row', 'yl', 'x'), perm)  9.81 us
    pallas_call x1, Pallas kernels, product(): pl.pallas_call(product_kernel, out_shape=jax.ShapeDtypeStruct((4, count,...  6.56 us
    all_to_all x1, starting transfers between devices, body(): far_tokens = lax.all_to_all(share, 'row', 0, 0, tiled=True)  5.66 us
    all_to_all x1, starting transfers between devices, body(): input_grad = y_sum(lax.all_to_all(chunks, ('yh', 'yl'), 0, 0, tiled=True))  5.18 us
  transfers between devices with their start and end apart: 12, of which 5 were waited for; matrix products, arithmetic and copies ran while one was open for 2% of the time, Pallas kernels for 6%

profile of v8, /device:TPU:1, one launch (start us, length us, event | category | flops | bytes accessed | tf_op | source)
XLA Modules:
  0.0 126.4 jit_solution(15492672690922200980)
XLA Ops:
  0.6 8.8 %collective-permute-start.6 = (bf16[2048,768]{1,0:T(8,128)(2,1)}, bf16[2048,768]{1,0:T(8,128)(2,1)}, u32[]{:S(2)}, u32[]{:S(2)}) collective-permute-start(bf16[2048,768]{1,0:T(8,128)(2,1)} %bitcast.8), channel_id=1, source_target_pairs={{0,128},{128,0},{1,129},{129,1},{2,130},{130,2},{3,131},{131,3},{4... | collective-permute-start | bytes 9437192 | tf_op jit(solution)/shard_map/ppermute | solution.py:262
  9.4 0.8 dynamic_slice.3
  10.2 2.1 %collective-permute-start = (bf16[16,1536]{1,0:T(8,128)(2,1)S(1)}, bf16[16,1536]{1,0:T(8,128)(2,1)S(1)}, u32[]{:S(2)}, u32[]{:S(2)}) collective-permute-start(bf16[16,1536]{1,0:T(8,128)(2,1)S(1)} %dynamic_slice.3), channel_id=1, source_target_pairs={{0,256},{256,0},{1,257},{257,1},{2,258},{258,2},{3,259},{259,3},{4... | collective-permute-start | bytes 147464 | tf_op jit(solution)/shard_map/ppermute | solution.py:262
  12.3 1.1 copy-done
  13.5 1.0 copy-done.2
  15.0 4.4 %collective-permute-done = bf16[16,1536]{1,0:T(8,128)(2,1)S(1)} collective-permute-done((bf16[16,1536]{1,0:T(8,128)(2,1)S(1)}, bf16[16,1536]{1,0:T(8,128)(2,1)S(1)}, u32[]{:S(2)}, u32[]{:S(2)}) %collective-permute-start) | collective-permute-done | bytes 49184 | tf_op jit(solution)/shard_map/ppermute | solution.py:262
  20.2 5.7 %all-to-all-start = ((bf16[8,16,1536]{2,1,0:T(8,128)(2,1)}), bf16[8,16,1536]{2,1,0:T(8,128)(2,1)S(1)}, u32[]{:S(2)}, u32[]{:S(2)}) async-start(bf16[8,16,1536]{2,1,0:T(8,128)(2,1)} %broadcast_in_dim.2), calls=%async_computation | async-start | bytes 786432 | tf_op jit(solution)/shard_map/all_to_all | solution.py:277
  25.8 4.3 %collective-permute-start.1 = (bf16[2,128,128]{2,1,0:T(8,128)(2,1)S(1)}, bf16[2,128,128]{2,1,0:T(8,128)(2,1)S(1)}, u32[]{:S(2)}, u32[]{:S(2)}) collective-permute-start(bf16[2,128,128]{2,1,0:T(8,128)(2,1)S(1)} %get-tuple-element.25), channel_id=1, source_target_pairs={{0,17},{1,16},{2,19},{3,18},{4,21},{5,20},{6,23},{7,22},{8,25},{9,... | collective-permute-start | bytes 196616 | tf_op jit(solution)/shard_map/ppermute | solution.py:266
  30.1 6.2 %collective-permute-start.2 = (bf16[2,128,128]{2,1,0:T(8,128)(2,1)S(1)}, bf16[2,128,128]{2,1,0:T(8,128)(2,1)S(1)}, u32[]{:S(2)}, u32[]{:S(2)}) collective-permute-start(bf16[2,128,128]{2,1,0:T(8,128)(2,1)S(1)} %get-tuple-element.25), channel_id=1, source_target_pairs={{0,34},{1,35},{2,32},{3,33},{4,38},{5,39},{6,36},{7,37},{8,42},{9,... | collective-permute-start | bytes 196616 | tf_op jit(solution)/shard_map/ppermute | solution.py:266
  36.3 1.9 %collective-permute-start.3 = (bf16[2,128,128]{2,1,0:T(8,128)(2,1)S(1)}, bf16[2,128,128]{2,1,0:T(8,128)(2,1)S(1)}, u32[]{:S(2)}, u32[]{:S(2)}) collective-permute-start(bf16[2,128,128]{2,1,0:T(8,128)(2,1)S(1)} %get-tuple-element.25), channel_id=1, source_target_pairs={{0,51},{1,50},{2,49},{3,48},{4,55},{5,54},{6,53},{7,52},{8,59},{9,... | collective-permute-start | bytes 196616 | tf_op jit(solution)/shard_map/ppermute | solution.py:266
  39.6 5.8 %collective-permute-done.3 = bf16[2,128,128]{2,1,0:T(8,128)(2,1)S(1)} collective-permute-done((bf16[2,128,128]{2,1,0:T(8,128)(2,1)S(1)}, bf16[2,128,128]{2,1,0:T(8,128)(2,1)S(1)}, u32[]{:S(2)}, u32[]{:S(2)}) %collective-permute-start.3) | collective-permute-done | bytes 65568 | tf_op jit(solution)/shard_map/ppermute | solution.py:266
  45.4 4.2 %collective-permute-start.4 = (bf16[2,128,128]{2,1,0:T(8,128)(2,1)S(1)}, bf16[2,128,128]{2,1,0:T(8,128)(2,1)S(1)}, u32[]{:S(2)}, u32[]{:S(2)}) collective-permute-start(bf16[2,128,128]{2,1,0:T(8,128)(2,1)S(1)} %get-tuple-element.39), channel_id=1, source_target_pairs={{0,116},{1,117},{2,118},{3,119},{4,112},{5,113},{6,114},{7,115},{8... | collective-permute-start | bytes 196616 | tf_op jit(solution)/shard_map/ppermute | solution.py:266
  49.7 4.3 %collective-permute-start.5 = (bf16[128,128]{1,0:T(8,128)(2,1)S(1)}, bf16[128,128]{1,0:T(8,128)(2,1)S(1)}, u32[]{:S(2)}, u32[]{:S(2)}) collective-permute-start(bf16[128,128]{1,0:T(8,128)(2,1)S(1)} %slice_bitcast_fusion), channel_id=1, source_target_pairs={{0,8},{1,9},{2,10},{3,11},{4,12},{5,13},{6,14},{7,15},{8,0},{9,1},... | collective-permute-start | bytes 98312 | tf_op jit(solution)/shard_map/ppermute | solution.py:266
  54.7 6.6 %shard_map.59 = bf16[4,128,1024]{2,1,0:T(8,128)(2,1)} custom-call(s32[4]{0:T(128)} %pad_add_fusion.place, bf16[128,3072]{1,0:T(8,128)(2,1)} %grads_hbm.1, bf16[8,16,1536]{2,1,0:T(8,128)(2,1)} %copy-done.6, bf16[2048,768]{1,0:T(8,128)(2,1)} %bitcast.9, bf16[2048,768]{1,0:T(8,128)(2,1)} %bitcast.10, ...), custom_call_target="tpu_custom_call" | custom-call | flops 1610612736 | bytes 8388608 | tf_op jit(solution)/shard_map/pallas_call | solution.py:81
  61.3 3.3 %collective-permute-start.7 = (bf16[128,128]{1,0:T(8,128)(2,1)S(1)}, bf16[128,128]{1,0:T(8,128)(2,1)S(1)}, u32[]{:S(2)}, u32[]{:S(2)}) collective-permute-start(bf16[128,128]{1,0:T(8,128)(2,1)S(1)} %slice_bitcast_fusion), channel_id=1, source_target_pairs={{0,12},{1,13},{2,14},{3,15},{4,8},{5,9},{6,10},{7,11},{8,4},{9,5},... | collective-permute-start | bytes 98312 | tf_op jit(solution)/shard_map/ppermute | solution.py:266
  64.7 3.2 %collective-permute-done.7.left3_ref = bf16[128,128]{1,0:T(8,128)(2,1)S(1)} collective-permute-done((bf16[128,128]{1,0:T(8,128)(2,1)S(1)}, bf16[128,128]{1,0:T(8,128)(2,1)S(1)}, u32[]{:S(2)}, u32[]{:S(2)}) %collective-permute-start.7) | collective-permute-done | bytes 32800 | tf_op jit(solution)/shard_map/ppermute | solution.py:266
  67.9 3.6 %shard_map.60 = (f32[64,4096]{1,0:T(8,128)S(1)}, f32[64,4096]{1,0:T(8,128)S(1)}) custom-call(s32[4]{0:T(128)S(1)} %copy-done.4, f32[2,128,128]{2,1,0:T(8,128)S(1)} %get-tuple-element.40.total_ref, bf16[2,128,128]{2,1,0:T(8,128)(2,1)S(1)} %collective-permute-done.4.pair_ref, bf16[128,128]{1,0:T(8,128)(2,1)S(1)} %collective-permute-done.5.left2_ref, ...), custom_call_target="tpu_custom_call" | custom-call | flops 1048576000 | bytes 5242880 | tf_op jit(solution)/shard_map/pallas_call | solution.py:194
  71.5 6.7 %collective-permute-start.8 = (f32[64,4096]{1,0:T(8,128)S(1)}, f32[64,4096]{1,0:T(8,128)S(1)}, u32[]{:S(2)}, u32[]{:S(2)}) collective-permute-start(f32[64,4096]{1,0:T(8,128)S(1)} %get-tuple-element.28), channel_id=1, source_target_pairs={{0,128},{128,0},{1,129},{129,1},{2,130},{130,2},{3,131},{131,3},{4... | collective-permute-start | bytes 3145736 | tf_op jit(solution)/shard_map/ppermute | solution.py:262
  78.1 17.4 %all_to_all.15.got_ref = bf16[4,128,1024]{2,1,0:T(8,128)(2,1)S(1)} all-to-all(bf16[4,128,1024]{2,1,0:T(8,128)(2,1)S(1)} %copy-done.5), channel_id=1, replica_groups=mesh['yh'=2,'core'=2,'row'=8,'yl'=4,'x'=4] {'x'}, dimensions={0} | all-to-all | bytes 2097152 | tf_op jit(solution)/shard_map/all_to_all | solution.py:287
  95.6 1.4 %shard_map.62 = bf16[2,64,1024]{2,1,0:T(8,128)(2,1)} custom-call(s32[4]{0:T(128)S(1)} %copy-done.4, bf16[4,128,1024]{2,1,0:T(8,128)(2,1)S(1)} %all_to_all.15.got_ref), custom_call_target="tpu_custom_call" | custom-call | flops 1048576 | bytes 2097152 | tf_op jit(solution)/shard_map/pallas_call | solution.py:115
  97.0 5.2 %all-to-all-start.2 = ((bf16[8,16,1024]{2,1,0:T(8,128)(2,1)}), bf16[8,16,1024]{2,1,0:T(8,128)(2,1)S(1)}, u32[]{:S(2)}, u32[]{:S(2)}) async-start(bf16[8,16,1024]{2,1,0:T(8,128)(2,1)} %bitcast.6), calls=%async_computation.2 | async-start | bytes 524288 | tf_op jit(solution)/shard_map/all_to_all | solution.py:297
  102.2 7.3 %collective-permute-start.9 = (bf16[32,4096]{1,0:T(8,128)(2,1)S(1)}, bf16[32,4096]{1,0:T(8,128)(2,1)S(1)}, u32[]{:S(2)}, u32[]{:S(2)}) collective-permute-start(bf16[32,4096]{1,0:T(8,128)(2,1)S(1)} %get-tuple-element.36), channel_id=1, source_target_pairs={{0,256},{256,0},{1,257},{257,1},{2,258},{258,2},{3,259},{259,3},{4... | collective-permute-start | bytes 786440 | tf_op jit(solution)/shard_map/ppermute | solution.py:262
  109.5 15.5 %collective-permute-done.9.far_ref = bf16[32,4096]{1,0:T(8,128)(2,1)S(1)} collective-permute-done((bf16[32,4096]{1,0:T(8,128)(2,1)S(1)}, bf16[32,4096]{1,0:T(8,128)(2,1)S(1)}, u32[]{:S(2)}, u32[]{:S(2)}) %collective-permute-start.9) | collective-permute-done | bytes 262176 | tf_op jit(solution)/shard_map/ppermute | solution.py:262
  124.9 0.8 shard_map.64
  (27 shorter events, 4.2 us)
Async XLA Ops:
  0.6 53.4 %collective-permute-start.6 = (bf16[2048,768]{1,0:T(8,128)(2,1)}, bf16[2048,768]{1,0:T(8,128)(2,1)}, u32[]{:S(2)}, u32[]{:S(2)}) collective-permute-start(bf16[2048,768]{1,0:T(8,128)(2,1)} %bitcast.8), channel_id=1, source_target_pairs={{0,128},{128,0},{1,129},{129,1},{2,130},{130,2},{3,131},{131,3},{4... | collective-permute-start | bytes 9437192 | tf_op jit(solution)/shard_map/ppermute | solution.py:262
  10.2 9.2 %collective-permute-start = (bf16[16,1536]{1,0:T(8,128)(2,1)S(1)}, bf16[16,1536]{1,0:T(8,128)(2,1)S(1)}, u32[]{:S(2)}, u32[]{:S(2)}) collective-permute-start(bf16[16,1536]{1,0:T(8,128)(2,1)S(1)} %dynamic_slice.3), channel_id=1, source_target_pairs={{0,256},{256,0},{1,257},{257,1},{2,258},{258,2},{3,259},{259,3},{4... | collective-permute-start | bytes 147464 | tf_op jit(solution)/shard_map/ppermute | solution.py:262
  12.3 1.1 copy-start
  13.5 1.0 copy-start.2
  20.2 33.8 %all-to-all-start = ((bf16[8,16,1536]{2,1,0:T(8,128)(2,1)}), bf16[8,16,1536]{2,1,0:T(8,128)(2,1)S(1)}, u32[]{:S(2)}, u32[]{:S(2)}) async-start(bf16[8,16,1536]{2,1,0:T(8,128)(2,1)} %broadcast_in_dim.2), calls=%async_computation | async-start | bytes 786432 | tf_op jit(solution)/shard_map/all_to_all | solution.py:277
  25.8 13.0 %collective-permute-start.1 = (bf16[2,128,128]{2,1,0:T(8,128)(2,1)S(1)}, bf16[2,128,128]{2,1,0:T(8,128)(2,1)S(1)}, u32[]{:S(2)}, u32[]{:S(2)}) collective-permute-start(bf16[2,128,128]{2,1,0:T(8,128)(2,1)S(1)} %get-tuple-element.25), channel_id=1, source_target_pairs={{0,17},{1,16},{2,19},{3,18},{4,21},{5,20},{6,23},{7,22},{8,25},{9,... | collective-permute-start | bytes 196616 | tf_op jit(solution)/shard_map/ppermute | solution.py:266
  30.1 9.5 %collective-permute-start.2 = (bf16[2,128,128]{2,1,0:T(8,128)(2,1)S(1)}, bf16[2,128,128]{2,1,0:T(8,128)(2,1)S(1)}, u32[]{:S(2)}, u32[]{:S(2)}) collective-permute-start(bf16[2,128,128]{2,1,0:T(8,128)(2,1)S(1)} %get-tuple-element.25), channel_id=1, source_target_pairs={{0,34},{1,35},{2,32},{3,33},{4,38},{5,39},{6,36},{7,37},{8,42},{9,... | collective-permute-start | bytes 196616 | tf_op jit(solution)/shard_map/ppermute | solution.py:266
  36.3 9.1 %collective-permute-start.3 = (bf16[2,128,128]{2,1,0:T(8,128)(2,1)S(1)}, bf16[2,128,128]{2,1,0:T(8,128)(2,1)S(1)}, u32[]{:S(2)}, u32[]{:S(2)}) collective-permute-start(bf16[2,128,128]{2,1,0:T(8,128)(2,1)S(1)} %get-tuple-element.25), channel_id=1, source_target_pairs={{0,51},{1,50},{2,49},{3,48},{4,55},{5,54},{6,53},{7,52},{8,59},{9,... | collective-permute-start | bytes 196616 | tf_op jit(solution)/shard_map/ppermute | solution.py:266
  45.4 19.2 %collective-permute-start.4 = (bf16[2,128,128]{2,1,0:T(8,128)(2,1)S(1)}, bf16[2,128,128]{2,1,0:T(8,128)(2,1)S(1)}, u32[]{:S(2)}, u32[]{:S(2)}) collective-permute-start(bf16[2,128,128]{2,1,0:T(8,128)(2,1)S(1)} %get-tuple-element.39), channel_id=1, source_target_pairs={{0,116},{1,117},{2,118},{3,119},{4,112},{5,113},{6,114},{7,115},{8... | collective-permute-start | bytes 196616 | tf_op jit(solution)/shard_map/ppermute | solution.py:266
  49.7 18.2 %copy-start.1 = (bf16[128,3072]{1,0:T(8,128)(2,1)S(1)}, bf16[128,3072]{1,0:T(8,128)(2,1)}, u32[]{:S(2)}) copy-start(bf16[128,3072]{1,0:T(8,128)(2,1)} %grads_hbm.1) | copy-start | bytes 2359300
  49.7 18.2 %copy-start.3 = (bf16[128,2048]{1,0:T(8,128)(2,1)S(1)}, bf16[128,2048]{1,0:T(8,128)(2,1)}, u32[]{:S(2)}) copy-start(bf16[128,2048]{1,0:T(8,128)(2,1)} %acts_hbm.1) | copy-start | bytes 1572868
  49.7 18.2 %copy-start.4 = (s32[4]{0:T(128)S(1)}, s32[4]{0:T(128)}, u32[]{:S(2)}) copy-start(s32[4]{0:T(128)} %pad_add_fusion.place) | copy-start | bytes 52
  49.7 14.9 %collective-permute-start.5 = (bf16[128,128]{1,0:T(8,128)(2,1)S(1)}, bf16[128,128]{1,0:T(8,128)(2,1)S(1)}, u32[]{:S(2)}, u32[]{:S(2)}) collective-permute-start(bf16[128,128]{1,0:T(8,128)(2,1)S(1)} %slice_bitcast_fusion), channel_id=1, source_target_pairs={{0,8},{1,9},{2,10},{3,11},{4,12},{5,13},{6,14},{7,15},{8,0},{9,1},... | collective-permute-start | bytes 98312 | tf_op jit(solution)/shard_map/ppermute | solution.py:266
  54.0 0.7 copy-start.6
  61.3 16.8 %copy-start.5 = (bf16[4,128,1024]{2,1,0:T(8,128)(2,1)S(1)}, bf16[4,128,1024]{2,1,0:T(8,128)(2,1)}, u32[]{:S(2)}) copy-start(bf16[4,128,1024]{2,1,0:T(8,128)(2,1)} %shard_map.59) | copy-start | bytes 3145732
  61.3 6.6 %collective-permute-start.7 = (bf16[128,128]{1,0:T(8,128)(2,1)S(1)}, bf16[128,128]{1,0:T(8,128)(2,1)S(1)}, u32[]{:S(2)}, u32[]{:S(2)}) collective-permute-start(bf16[128,128]{1,0:T(8,128)(2,1)S(1)} %slice_bitcast_fusion), channel_id=1, source_target_pairs={{0,12},{1,13},{2,14},{3,15},{4,8},{5,9},{6,10},{7,11},{8,4},{9,5},... | collective-permute-start | bytes 98312 | tf_op jit(solution)/shard_map/ppermute | solution.py:266
  71.5 24.1 %collective-permute-start.8 = (f32[64,4096]{1,0:T(8,128)S(1)}, f32[64,4096]{1,0:T(8,128)S(1)}, u32[]{:S(2)}, u32[]{:S(2)}) collective-permute-start(f32[64,4096]{1,0:T(8,128)S(1)} %get-tuple-element.28), channel_id=1, source_target_pairs={{0,128},{128,0},{1,129},{129,1},{2,130},{130,2},{3,131},{131,3},{4... | collective-permute-start | bytes 3145736 | tf_op jit(solution)/shard_map/ppermute | solution.py:262
  97.0 28.7 %all-to-all-start.2 = ((bf16[8,16,1024]{2,1,0:T(8,128)(2,1)}), bf16[8,16,1024]{2,1,0:T(8,128)(2,1)S(1)}, u32[]{:S(2)}, u32[]{:S(2)}) async-start(bf16[8,16,1024]{2,1,0:T(8,128)(2,1)} %bitcast.6), calls=%async_computation.2 | async-start | bytes 524288 | tf_op jit(solution)/shard_map/all_to_all | solution.py:297
  102.2 22.7 %collective-permute-start.9 = (bf16[32,4096]{1,0:T(8,128)(2,1)S(1)}, bf16[32,4096]{1,0:T(8,128)(2,1)S(1)}, u32[]{:S(2)}, u32[]{:S(2)}) collective-permute-start(bf16[32,4096]{1,0:T(8,128)(2,1)S(1)} %get-tuple-element.36), channel_id=1, source_target_pairs={{0,256},{256,0},{1,257},{257,1},{2,258},{258,2},{3,259},{259,3},{4... | collective-permute-start | bytes 786440 | tf_op jit(solution)/shard_map/ppermute | solution.py:262

commit v9 on v8

--- a/solution.py
+++ b/solution.py
@@ -21,8 +21,8 @@
     return pltpu.CompilerParams(vmem_limit_bytes=mb * MB)
 
 
-def cost(flops, moved):
-    return pl.CostEstimate(flops=flops, bytes_accessed=moved, transcendentals=0)
+def cost():
+    return pl.CostEstimate(flops=1, bytes_accessed=1, transcendentals=0)
 
 
 def prepare_kernel(acts_ref, grads_ref, sum_ref, send_ref):
@@ -42,7 +42,7 @@
         in_specs=[vmem, vmem],
         out_specs=[vmem] * 2,
         compiler_params=params(16),
-        cost_estimate=cost(2 * tokens * tokens * (grads.shape[1] + acts.shape[1]), 3 * MB),
+        cost_estimate=cost(),
     )(acts, grads)
 
 
@@ -96,7 +96,7 @@
             scratch_shapes=[pltpu.VMEM((2 * count, step), F32)] * 2,
         ),
         compiler_params=params(60),
-        cost_estimate=cost(8 * count * features * quarter, 8 * MB),
+        cost_estimate=cost(),
     )(place, near, far, weight, weight, weight_far, weight_far)
 
 
@@ -118,7 +118,7 @@
         in_specs=[pl.BlockSpec(memory_space=pltpu.SMEM), vmem],
         out_specs=vmem,
         compiler_params=params(16),
-        cost_estimate=cost(8 * rows * width, 2 * MB),
+        cost_estimate=cost(),
     )(place, got)
 
 
@@ -137,7 +137,7 @@
         in_specs=[pl.BlockSpec(memory_space=pltpu.VMEM)],
         out_specs=pl.BlockSpec(memory_space=pltpu.VMEM),
         compiler_params=params(16),
-        cost_estimate=cost(128 * width, MB // 2),
+        cost_estimate=cost(),
     )(got)
 
 
@@ -151,7 +151,7 @@
     return jnp.where(unit == wanted, 1.0, 0.0).astype(BF)
 
 
-def stats_kernel(place, total_ref, pair_ref, left2_ref, left3_ref, acts_hbm, grads_hbm, keep_ref, send_ref, acts_ref, grads_ref, sems):
+def stats_kernel(place, left_ref, right_ref, acts_hbm, grads_hbm, keep_ref, send_ref, acts_ref, grads_ref, sems):
     hidden = grads_ref.shape[1]
     width = acts_ref.shape[1]
     copies = []
@@ -166,8 +166,7 @@
         picked = lax.dot_general(pick, data, NT, preferred_element_type=F32).astype(BF)
         return jnp.dot(picked, mix, preferred_element_type=F32) * (1.0 / TOKENS)
 
-    right = total_ref[1] + pair_ref[1].astype(F32)
-    right = (right / D).astype(BF)
+    right = (right_ref[...] / D).astype(BF)
     pick = picker(place, place[2], 32, 8)
     for j in range(hidden // BLOCK):
         lanes = slice(j * BLOCK, (j + 1) * BLOCK)
@@ -175,8 +174,7 @@
         out = rows(pick, right, grads_ref[:, lanes])
         keep_ref[:, lanes] = out[:64]
         send_ref[:, lanes] = out[64:]
-    left = total_ref[0] + pair_ref[0].astype(F32) + left2_ref[...].astype(F32) + left3_ref[...].astype(F32)
-    left = (left / FF).astype(BF)
+    left = (left_ref[...] / FF).astype(BF)
     pick = picker(place, place[3], 16, 16)
     for j in range(width // BLOCK):
         copies[hidden // BLOCK + j].wait()
@@ -187,14 +185,14 @@
             send_ref[at, hidden:] = out[32 + dy * 16 : 32 + dy * 16 + 16]
 
 
-def stats(place, total, pair, left2, left3, acts, grads):
+def stats(place, left, right, acts, grads):
     shape = jax.ShapeDtypeStruct((64, grads.shape[1] + BLOCK), F32)
     vmem = pl.BlockSpec(memory_space=pltpu.VMEM)
     hbm = pl.BlockSpec(memory_space=pltpu.HBM)
     return pl.pallas_call(
         stats_kernel,
         out_shape=(shape, shape),
-        in_specs=[pl.BlockSpec(memory_space=pltpu.SMEM)] + [vmem] * 4 + [hbm, hbm],
+        in_specs=[pl.BlockSpec(memory_space=pltpu.SMEM), vmem, vmem, hbm, hbm],
         out_specs=[vmem, vmem],
         scratch_shapes=[
             pltpu.VMEM(acts.shape, BF),
@@ -202,8 +200,8 @@
             pltpu.SemaphoreType.DMA(((acts.shape[1] + grads.shape[1]) // BLOCK,)),
         ],
         compiler_params=params(16),
-        cost_estimate=cost(1000 * MB, 5 * MB),
-    )(place, total, pair, left2, left3, acts, grads)
+        cost_estimate=cost(),
+    )(place, left, right, acts, grads)
 
 
 def core_sum_kernel(keep_ref, got_ref, near_ref, far_ref):
@@ -224,7 +222,7 @@
         in_specs=[vmem, vmem],
         out_specs=[vmem, vmem],
         compiler_params=params(16),
-        cost_estimate=cost(rows * width, 3 * MB),
+        cost_estimate=cost(),
     )(keep, got)
 
 
@@ -247,7 +245,7 @@
         in_specs=[vmem, vmem],
         out_specs=[vmem, vmem],
         compiler_params=params(16),
-        cost_estimate=cost(32 * 4096, 2 * MB),
+        cost_estimate=cost(),
     )(near, far)
 
 
@@ -272,28 +270,28 @@
     weight_far = swap(weight, "core")
 
     total, send = prepare(acts_in, grad_out)
+    total = total + across(send, 1, 0, 1).astype(F32)
+    send, share = barrier((total.astype(BF), share))
+    total = total + across(send, 2, 0, 3).astype(F32)
+    total = total + across(total.astype(BF), 7, 1, 0).astype(F32)
+    left, right = total[0], total[1]
     share = jnp.broadcast_to(share[None], (8,) + share.shape)
-    send, share = barrier((send, share))
+    send, share = barrier((left.astype(BF), share))
     far_tokens = lax.all_to_all(share, "row", 0, 0, tiled=True)
-    parts = [across(send, r, 0, r).astype(F32) for r in (1, 2, 3)]
-    total = total + parts[0] + parts[1] + parts[2]
-    send = total.astype(BF)
-    pair = across(send, 7, 1, 0)
-    left2 = across(send[0], 0, 2, 0)
-
+    left = left + across(send, 0, 2, 0).astype(F32)
+
+    keep, send = stats(place, left, right, acts, grad_out)
+    far_tokens, send = barrier((far_tokens, send))
     both = product(place, grad_out, far_tokens, weight, weight_far)
-    both, last = barrier((both, send[0]))
-    left3 = across(last, 0, 3, 0)
+    both, send = barrier((both, send))
     got = lax.all_to_all(both, "x", 0, 0, tiled=True)
-
-    keep, send = stats(place, total, pair, left2, left3, acts, grad_out)
-    back, got = barrier((swap(send, "core"), got))
-    near_rows, far_rows = core_sum(keep, back)
+    near_rows, far_rows = core_sum(keep, swap(send, "core"))
     got, near_rows = barrier((got, near_rows))
     far_rows = swap(far_rows, "yh")
 
     chunks = x_sum(place, got)
     chunks = chunks.reshape(8, -1, chunks.shape[2])
+    chunks, far_rows = barrier((chunks, far_rows))
     input_grad = y_sum(lax.all_to_all(chunks, ("yh", "yl"), 0, 0, tiled=True))
 
     left_stats, right_stats = last_sum(near_rows, far_rows, hidden, width)

time: 127 us -> 118 us (0.929)
  blocking collectives: 17.4 us -> 0 us
  starting transfers between devices: 59.8 us -> 64.6 us
  local copies, waits for them, and re-layouts: 4.5 us -> 6.34 us
  Pallas kernels: 13.6 us -> 15.3 us
    all_to_all x1 -> x0, blocking collectives: 17.4 us -> none  [body(): got = lax.all_to_all(both, 'x', 0, 0, tiled=True)]
    ppermute x4, waiting for transfers between devices: 19.9 us -> 9.38 us  [swap(): return lax.ppermute(value, axis, [(0, 1), (1, 0)])]
    all_to_all x1, waiting for transfers between devices: 0.01 us -> 8.28 us  [body(): input_grad = y_sum(lax.all_to_all(chunks, ('yh', 'yl'), 0, 0, tiled=True))]
    all_to_all x0 -> x1, waiting for transfers between devices: none -> 5.55 us  [body(): got = lax.all_to_all(both, 'x', 0, 0, tiled=True)]
    ppermute x6 -> x4, starting transfers between devices: 24.2 us -> 19.8 us  [across(): return lax.ppermute(value, ('row', 'yl', 'x'), perm)]
    ppermute x6 -> x4, waiting for transfers between devices: 9.81 us -> 6.17 us  [across(): return lax.ppermute(value, ('row', 'yl', 'x'), perm)]
    all_to_all x0 -> x1, starting transfers between devices: none -> 3.53 us  [body(): got = lax.all_to_all(both, 'x', 0, 0, tiled=True)]
    ppermute x4, starting transfers between devices: 24.8 us -> 28 us  [swap(): return lax.ppermute(value, axis, [(0, 1), (1, 0)])]
  transfers between devices with their start and end apart: 12 -> 11, of which waited for: 5 -> 7; matrix products, arithmetic and copies ran while one was open for 2% -> 2% of each run, Pallas kernels for 6% -> 7%
where the time goes in v9:
time: 118 us; the launch traced here: 117 us
  starting transfers between devices  64.6 us (55%)
  waiting for transfers between devices  29.4 us (25%)
  Pallas kernels  15.3 us (13%)
  local copies, waits for them, and re-layouts  6.34 us (5%)
    ppermute x4, starting transfers between devices, swap(): return lax.ppermute(value, axis, [(0, 1), (1, 0)])  28 us
    ppermute x4, starting transfers between devices, across(): return lax.ppermute(value, ('row', 'yl', 'x'), perm)  19.8 us
    ppermute x4, waiting for transfers between devices, swap(): return lax.ppermute(value, axis, [(0, 1), (1, 0)])  9.38 us
    all_to_all x1, waiting for transfers between devices, body(): input_grad = y_sum(lax.all_to_all(chunks, ('yh', 'yl'), 0, 0, tiled=True))  8.28 us
    all_to_all x1, starting transfers between devices, body(): far_tokens = lax.all_to_all(share, 'row', 0, 0, tiled=True)  6.66 us
    all_to_all x1, starting transfers between devices, body(): input_grad = y_sum(lax.all_to_all(chunks, ('yh', 'yl'), 0, 0, tiled=True))  6.59 us
    pallas_call x1, Pallas kernels, product(): pl.pallas_call(product_kernel, out_shape=jax.ShapeDtypeStruct((4, count,...  6.56 us
    ppermute x4, waiting for transfers between devices, across(): return lax.ppermute(value, ('row', 'yl', 'x'), perm)  6.17 us
  transfers between devices with their start and end apart: 11, of which 7 were waited for; matrix products, arithmetic and copies ran while one was open for 2% of the time, Pallas kernels for 7%

profile of v9, /device:TPU:1, one launch (start us, length us, event | category | flops | bytes accessed | tf_op | source)
XLA Modules:
  0.0 116.7 jit_solution(7830196998555437437)
XLA Ops:
  0.6 8.8 %collective-permute-start.5 = (bf16[2048,768]{1,0:T(8,128)(2,1)}, bf16[2048,768]{1,0:T(8,128)(2,1)}, u32[]{:S(2)}, u32[]{:S(2)}) collective-permute-start(bf16[2048,768]{1,0:T(8,128)(2,1)} %bitcast.14), channel_id=1, source_target_pairs={{0,128},{128,0},{1,129},{129,1},{2,130},{130,2},{3,131},{131,3},{4... | collective-permute-start | bytes 9437192 | tf_op jit(solution)/shard_map/ppermute | solution.py:260
  10.2 1.1 copy-done
  11.4 1.0 copy-done.2
  12.9 1.9 %collective-permute-start = (bf16[2,128,128]{2,1,0:T(8,128)(2,1)S(1)}, bf16[2,128,128]{2,1,0:T(8,128)(2,1)S(1)}, u32[]{:S(2)}, u32[]{:S(2)}) collective-permute-start(bf16[2,128,128]{2,1,0:T(8,128)(2,1)S(1)} %get-tuple-element.27), channel_id=1, source_target_pairs={{0,17},{1,16},{2,19},{3,18},{4,21},{5,20},{6,23},{7,22},{8,25},{9,... | collective-permute-start | bytes 196616 | tf_op jit(solution)/shard_map/ppermute | solution.py:264
  14.9 5.1 %collective-permute-start.1 = (bf16[16,1536]{1,0:T(8,128)(2,1)S(1)}, bf16[16,1536]{1,0:T(8,128)(2,1)S(1)}, u32[]{:S(2)}, u32[]{:S(2)}) collective-permute-start(bf16[16,1536]{1,0:T(8,128)(2,1)S(1)} %dynamic_slice.3), channel_id=1, source_target_pairs={{0,256},{256,0},{1,257},{257,1},{2,258},{258,2},{3,259},{259,3},{4... | collective-permute-start | bytes 147464 | tf_op jit(solution)/shard_map/ppermute | solution.py:260
  20.0 4.0 %collective-permute-done.1 = bf16[16,1536]{1,0:T(8,128)(2,1)S(1)} collective-permute-done((bf16[16,1536]{1,0:T(8,128)(2,1)S(1)}, bf16[16,1536]{1,0:T(8,128)(2,1)S(1)}, u32[]{:S(2)}, u32[]{:S(2)}) %collective-permute-start.1) | collective-permute-done | bytes 49184 | tf_op jit(solution)/shard_map/ppermute | solution.py:260
  24.0 4.8 %collective-permute-start.2 = (bf16[2,128,128]{2,1,0:T(8,128)(2,1)S(1)}, bf16[2,128,128]{2,1,0:T(8,128)(2,1)S(1)}, u32[]{:S(2)}, u32[]{:S(2)}) collective-permute-start(bf16[2,128,128]{2,1,0:T(8,128)(2,1)S(1)} %fusion), channel_id=1, source_target_pairs={{0,35},{1,34},{2,33},{3,32},{4,39},{5,38},{6,37},{7,36},{8,43},{9,... | collective-permute-start | bytes 196616 | tf_op jit(solution)/shard_map/ppermute | solution.py:264
  28.8 3.2 %collective-permute-done.2 = bf16[2,128,128]{2,1,0:T(8,128)(2,1)S(1)} collective-permute-done((bf16[2,128,128]{2,1,0:T(8,128)(2,1)S(1)}, bf16[2,128,128]{2,1,0:T(8,128)(2,1)S(1)}, u32[]{:S(2)}, u32[]{:S(2)}) %collective-permute-start.2) | collective-permute-done | bytes 65568 | tf_op jit(solution)/shard_map/ppermute | solution.py:264
  32.1 7.2 %collective-permute-start.3 = (bf16[2,128,128]{2,1,0:T(8,128)(2,1)S(1)}, bf16[2,128,128]{2,1,0:T(8,128)(2,1)S(1)}, u32[]{:S(2)}, u32[]{:S(2)}) collective-permute-start(bf16[2,128,128]{2,1,0:T(8,128)(2,1)S(1)} %fusion.2), channel_id=1, source_target_pairs={{0,116},{1,117},{2,118},{3,119},{4,112},{5,113},{6,114},{7,115},{8... | collective-permute-start | bytes 196616 | tf_op jit(solution)/shard_map/ppermute | solution.py:264
  39.2 1.6 %collective-permute-done.3 = bf16[2,128,128]{2,1,0:T(8,128)(2,1)S(1)} collective-permute-done((bf16[2,128,128]{2,1,0:T(8,128)(2,1)S(1)}, bf16[2,128,128]{2,1,0:T(8,128)(2,1)S(1)}, u32[]{:S(2)}, u32[]{:S(2)}) %collective-permute-start.3) | collective-permute-done | bytes 65568 | tf_op jit(solution)/shard_map/ppermute | solution.py:264
  41.7 6.7 %all-to-all-start = ((bf16[8,16,1536]{2,1,0:T(8,128)(2,1)}), bf16[8,16,1536]{2,1,0:T(8,128)(2,1)S(1)}, u32[]{:S(2)}, u32[]{:S(2)}) async-start(bf16[8,16,1536]{2,1,0:T(8,128)(2,1)} %broadcast_in_dim.2), calls=%async_computation | async-start | bytes 786432 | tf_op jit(solution)/shard_map/all_to_all | solution.py:280
  48.5 6.0 %collective-permute-start.4 = (bf16[128,128]{1,0:T(8,128)(2,1)S(1)}, bf16[128,128]{1,0:T(8,128)(2,1)S(1)}, u32[]{:S(2)}, u32[]{:S(2)}) collective-permute-start(bf16[128,128]{1,0:T(8,128)(2,1)S(1)} %fusion.1), channel_id=1, source_target_pairs={{0,8},{1,9},{2,10},{3,11},{4,12},{5,13},{6,14},{7,15},{8,0},{9,1},... | collective-permute-start | bytes 98312 | tf_op jit(solution)/shard_map/ppermute | solution.py:264
  54.5 1.3 %collective-permute-done.4 = bf16[128,128]{1,0:T(8,128)(2,1)S(1)} collective-permute-done((bf16[128,128]{1,0:T(8,128)(2,1)S(1)}, bf16[128,128]{1,0:T(8,128)(2,1)S(1)}, u32[]{:S(2)}, u32[]{:S(2)}) %collective-permute-start.4) | collective-permute-done | bytes 32800 | tf_op jit(solution)/shard_map/ppermute | solution.py:264
  55.8 4.5 %shard_map.59 = (f32[64,4096]{1,0:T(8,128)S(1)}, f32[64,4096]{1,0:T(8,128)}) custom-call(s32[4]{0:T(128)S(1)} %pad_add_fusion.place, f32[128,128]{1,0:T(8,128)S(1)} %convert_add_fusion.3.left_ref, f32[128,128]{1,0:T(8,128)S(1)} %slice_bitcast_fusion.right_ref, bf16[128,2048]{1,0:T(8,128)(2,1)S(1)} %copy-done.3, bf16[128,3072]{1,0:T(8,128)(2,1)S(1)} %copy-done.1), custom_call_target="tpu_custom_call" | custom-call | flops 1 | bytes 1 | tf_op jit(solution)/shard_map/pallas_call | solution.py:192
  61.1 6.6 %shard_map.60 = bf16[4,128,1024]{2,1,0:T(8,128)(2,1)} custom-call(s32[4]{0:T(128)} %copy-done.6, bf16[128,3072]{1,0:T(8,128)(2,1)} %near_ref.1, bf16[8,16,1536]{2,1,0:T(8,128)(2,1)} %copy-done.8, bf16[2048,768]{1,0:T(8,128)(2,1)} %bitcast.15, bf16[2048,768]{1,0:T(8,128)(2,1)} %bitcast.16, bf16[2048,768]{1,0:T(8,128)(2,1)} %collective-permute-done.5.other_lo.other_hi, ...), custom_call_target="tpu_custom_call" | custom-call | flops 1 | bytes 1 | tf_op jit(solution)/shard_map/pallas_call | solution.py:81
  67.6 6.2 %collective-permute-start.6 = (f32[64,4096]{1,0:T(8,128)}, f32[64,4096]{1,0:T(8,128)S(1)}, u32[]{:S(2)}, u32[]{:S(2)}) collective-permute-start(f32[64,4096]{1,0:T(8,128)} %get-tuple-element.38), channel_id=1, source_target_pairs={{0,128},{128,0},{1,129},{129,1},{2,130},{130,2},{3,131},{131,3},{4... | collective-permute-start | bytes 3145736 | tf_op jit(solution)/shard_map/ppermute | solution.py:260
  73.8 3.5 %all-to-all-start.1 = ((bf16[4,128,1024]{2,1,0:T(8,128)(2,1)}), bf16[4,128,1024]{2,1,0:T(8,128)(2,1)S(1)}, u32[]{:S(2)}, u32[]{:S(2)}) async-start(bf16[4,128,1024]{2,1,0:T(8,128)(2,1)} %shard_map.60), calls=%async_computation.1 | async-start | bytes 2097152 | tf_op jit(solution)/shard_map/all_to_all | solution.py:287
  79.0 8.0 %collective-permute-start.7 = (bf16[32,4096]{1,0:T(8,128)(2,1)}, bf16[32,4096]{1,0:T(8,128)(2,1)S(1)}, u32[]{:S(2)}, u32[]{:S(2)}) collective-permute-start(bf16[32,4096]{1,0:T(8,128)(2,1)} %get-tuple-element.41), channel_id=1, source_target_pairs={{0,256},{256,0},{1,257},{257,1},{2,258},{258,2},{3,259},{259,3},{4... | collective-permute-start | bytes 786440 | tf_op jit(solution)/shard_map/ppermute | solution.py:260
  87.0 5.6 %all-to-all-done.1.got_ref = bf16[4,128,1024]{2,1,0:T(8,128)(2,1)S(1)} async-done(((bf16[4,128,1024]{2,1,0:T(8,128)(2,1)}), bf16[4,128,1024]{2,1,0:T(8,128)(2,1)S(1)}, u32[]{:S(2)}, u32[]{:S(2)}) %all-to-all-start.1) | async-done | bytes 1048608 | tf_op jit(solution)/shard_map/all_to_all | solution.py:287
  92.6 1.4 %shard_map.62 = bf16[2,64,1024]{2,1,0:T(8,128)(2,1)} custom-call(s32[4]{0:T(128)S(1)} %copy-done.7, bf16[4,128,1024]{2,1,0:T(8,128)(2,1)S(1)} %all-to-all-done.1.got_ref), custom_call_target="tpu_custom_call" | custom-call | flops 1 | bytes 1 | tf_op jit(solution)/shard_map/pallas_call | solution.py:115
  93.9 5.3 %collective-permute-done.7.far_ref = bf16[32,4096]{1,0:T(8,128)(2,1)S(1)} collective-permute-done((bf16[32,4096]{1,0:T(8,128)(2,1)}, bf16[32,4096]{1,0:T(8,128)(2,1)S(1)}, u32[]{:S(2)}, u32[]{:S(2)}) %collective-permute-start.7) | collective-permute-done | bytes 262176 | tf_op jit(solution)/shard_map/ppermute | solution.py:260
  99.3 6.6 %all-to-all-start.2 = ((bf16[8,16,1024]{2,1,0:T(8,128)(2,1)}), bf16[8,16,1024]{2,1,0:T(8,128)(2,1)S(1)}, u32[]{:S(2)}, u32[]{:S(2)}) async-start(bf16[8,16,1024]{2,1,0:T(8,128)(2,1)} %bitcast.7), calls=%async_computation.2 | async-start | bytes 524288 | tf_op jit(solution)/shard_map/all_to_all | solution.py:295
  105.9 1.0 copy-done.5
  107.7 8.3 %all-to-all-done.2.got_ref = bf16[8,16,1024]{2,1,0:T(8,128)(2,1)S(1)} async-done(((bf16[8,16,1024]{2,1,0:T(8,128)(2,1)}), bf16[8,16,1024]{2,1,0:T(8,128)(2,1)S(1)}, u32[]{:S(2)}, u32[]{:S(2)}) %all-to-all-start.2) | async-done | bytes 262176 | tf_op jit(solution)/shard_map/all_to_all | solution.py:295
  (32 shorter events, 6.2 us)
Async XLA Ops:
  0.6 59.7 %collective-permute-start.5 = (bf16[2048,768]{1,0:T(8,128)(2,1)}, bf16[2048,768]{1,0:T(8,128)(2,1)}, u32[]{:S(2)}, u32[]{:S(2)}) collective-permute-start(bf16[2048,768]{1,0:T(8,128)(2,1)} %bitcast.14), channel_id=1, source_target_pairs={{0,128},{128,0},{1,129},{129,1},{2,130},{130,2},{3,131},{131,3},{4... | collective-permute-start | bytes 9437192 | tf_op jit(solution)/shard_map/ppermute | solution.py:260
  10.2 1.1 copy-start
  11.4 1.0 copy-start.2
  12.4 43.3 %copy-start.1 = (bf16[128,3072]{1,0:T(8,128)(2,1)S(1)}, bf16[128,3072]{1,0:T(8,128)(2,1)}, u32[]{:S(2)}) copy-start(bf16[128,3072]{1,0:T(8,128)(2,1)} %near_ref.1) | copy-start | bytes 2359300
  12.4 43.3 %copy-start.3 = (bf16[128,2048]{1,0:T(8,128)(2,1)S(1)}, bf16[128,2048]{1,0:T(8,128)(2,1)}, u32[]{:S(2)}) copy-start(bf16[128,2048]{1,0:T(8,128)(2,1)} %acts_hbm.1) | copy-start | bytes 1572868
  12.9 7.0 %collective-permute-start = (bf16[2,128,128]{2,1,0:T(8,128)(2,1)S(1)}, bf16[2,128,128]{2,1,0:T(8,128)(2,1)S(1)}, u32[]{:S(2)}, u32[]{:S(2)}) collective-permute-start(bf16[2,128,128]{2,1,0:T(8,128)(2,1)S(1)} %get-tuple-element.27), channel_id=1, source_target_pairs={{0,17},{1,16},{2,19},{3,18},{4,21},{5,20},{6,23},{7,22},{8,25},{9,... | collective-permute-start | bytes 196616 | tf_op jit(solution)/shard_map/ppermute | solution.py:264
  14.9 9.2 %collective-permute-start.1 = (bf16[16,1536]{1,0:T(8,128)(2,1)S(1)}, bf16[16,1536]{1,0:T(8,128)(2,1)S(1)}, u32[]{:S(2)}, u32[]{:S(2)}) collective-permute-start(bf16[16,1536]{1,0:T(8,128)(2,1)S(1)} %dynamic_slice.3), channel_id=1, source_target_pairs={{0,256},{256,0},{1,257},{257,1},{2,258},{258,2},{3,259},{259,3},{4... | collective-permute-start | bytes 147464 | tf_op jit(solution)/shard_map/ppermute | solution.py:260
  24.0 8.0 %collective-permute-start.2 = (bf16[2,128,128]{2,1,0:T(8,128)(2,1)S(1)}, bf16[2,128,128]{2,1,0:T(8,128)(2,1)S(1)}, u32[]{:S(2)}, u32[]{:S(2)}) collective-permute-start(bf16[2,128,128]{2,1,0:T(8,128)(2,1)S(1)} %fusion), channel_id=1, source_target_pairs={{0,35},{1,34},{2,33},{3,32},{4,39},{5,38},{6,37},{7,36},{8,43},{9,... | collective-permute-start | bytes 196616 | tf_op jit(solution)/shard_map/ppermute | solution.py:264
  32.1 8.8 %collective-permute-start.3 = (bf16[2,128,128]{2,1,0:T(8,128)(2,1)S(1)}, bf16[2,128,128]{2,1,0:T(8,128)(2,1)S(1)}, u32[]{:S(2)}, u32[]{:S(2)}) collective-permute-start(bf16[2,128,128]{2,1,0:T(8,128)(2,1)S(1)} %fusion.2), channel_id=1, source_target_pairs={{0,116},{1,117},{2,118},{3,119},{4,112},{5,113},{6,114},{7,115},{8... | collective-permute-start | bytes 196616 | tf_op jit(solution)/shard_map/ppermute | solution.py:264
  41.7 18.6 %all-to-all-start = ((bf16[8,16,1536]{2,1,0:T(8,128)(2,1)}), bf16[8,16,1536]{2,1,0:T(8,128)(2,1)S(1)}, u32[]{:S(2)}, u32[]{:S(2)}) async-start(bf16[8,16,1536]{2,1,0:T(8,128)(2,1)} %broadcast_in_dim.2), calls=%async_computation | async-start | bytes 786432 | tf_op jit(solution)/shard_map/all_to_all | solution.py:280
  48.5 11.9 %copy-start.6 = (s32[4]{0:T(128)}, s32[4]{0:T(128)S(1)}, u32[]{:S(2)}) copy-start(s32[4]{0:T(128)S(1)} %pad_add_fusion.place) | copy-start | bytes 52
  48.5 7.3 %collective-permute-start.4 = (bf16[128,128]{1,0:T(8,128)(2,1)S(1)}, bf16[128,128]{1,0:T(8,128)(2,1)S(1)}, u32[]{:S(2)}, u32[]{:S(2)}) collective-permute-start(bf16[128,128]{1,0:T(8,128)(2,1)S(1)} %fusion.1), channel_id=1, source_target_pairs={{0,8},{1,9},{2,10},{3,11},{4,12},{5,13},{6,14},{7,15},{8,0},{9,1},... | collective-permute-start | bytes 98312 | tf_op jit(solution)/shard_map/ppermute | solution.py:264
  60.3 0.7 copy-start.8
  67.6 24.9 %copy-start.7 = (s32[4]{0:T(128)S(1)}, s32[4]{0:T(128)}, u32[]{:S(2)}) copy-start(s32[4]{0:T(128)} %copy-done.6) | copy-start | bytes 52
  67.6 9.7 %collective-permute-start.6 = (f32[64,4096]{1,0:T(8,128)}, f32[64,4096]{1,0:T(8,128)S(1)}, u32[]{:S(2)}, u32[]{:S(2)}) collective-permute-start(f32[64,4096]{1,0:T(8,128)} %get-tuple-element.38), channel_id=1, source_target_pairs={{0,128},{128,0},{1,129},{129,1},{2,130},{130,2},{3,131},{131,3},{4... | collective-permute-start | bytes 3145736 | tf_op jit(solution)/shard_map/ppermute | solution.py:260
  73.8 18.8 %all-to-all-start.1 = ((bf16[4,128,1024]{2,1,0:T(8,128)(2,1)}), bf16[4,128,1024]{2,1,0:T(8,128)(2,1)S(1)}, u32[]{:S(2)}, u32[]{:S(2)}) async-start(bf16[4,128,1024]{2,1,0:T(8,128)(2,1)} %shard_map.60), calls=%async_computation.1 | async-start | bytes 2097152 | tf_op jit(solution)/shard_map/all_to_all | solution.py:287
  78.2 0.8 copy-start.4
  79.0 20.2 %collective-permute-start.7 = (bf16[32,4096]{1,0:T(8,128)(2,1)}, bf16[32,4096]{1,0:T(8,128)(2,1)S(1)}, u32[]{:S(2)}, u32[]{:S(2)}) collective-permute-start(bf16[32,4096]{1,0:T(8,128)(2,1)} %get-tuple-element.41), channel_id=1, source_target_pairs={{0,256},{256,0},{1,257},{257,1},{2,258},{258,2},{3,259},{259,3},{4... | collective-permute-start | bytes 786440 | tf_op jit(solution)/shard_map/ppermute | solution.py:260
  99.3 16.7 %all-to-all-start.2 = ((bf16[8,16,1024]{2,1,0:T(8,128)(2,1)}), bf16[8,16,1024]{2,1,0:T(8,128)(2,1)S(1)}, u32[]{:S(2)}, u32[]{:S(2)}) async-start(bf16[8,16,1024]{2,1,0:T(8,128)(2,1)} %bitcast.7), calls=%async_computation.2 | async-start | bytes 524288 | tf_op jit(solution)/shard_map/all_to_all | solution.py:295
  105.9 1.0 copy-start.5

commit v10 on v9

--- a/solution.py
+++ b/solution.py
@@ -271,8 +271,7 @@
 
     total, send = prepare(acts_in, grad_out)
     total = total + across(send, 1, 0, 1).astype(F32)
-    send, share = barrier((total.astype(BF), share))
-    total = total + across(send, 2, 0, 3).astype(F32)
+    total = total + across(total.astype(BF), 2, 0, 3).astype(F32)
     total = total + across(total.astype(BF), 7, 1, 0).astype(F32)
     left, right = total[0], total[1]
     share = jnp.broadcast_to(share[None], (8,) + share.shape)

time: 118 us -> 117 us (level)
  starting transfers between devices: 64.6 us -> 62.2 us
    ppermute x4, waiting for transfers between devices: 9.38 us -> 2.87 us  [swap(): return lax.ppermute(value, axis, [(0, 1), (1, 0)])]
    ppermute x4, waiting for transfers between devices: 6.17 us -> 11.6 us  [across(): return lax.ppermute(value, ('row', 'yl', 'x'), perm)]
    all_to_all x1, starting transfers between devices: 6.59 us -> 10.3 us  [body(): input_grad = y_sum(lax.all_to_all(chunks, ('yh', 'yl'), 0, 0, tiled=True))]
    all_to_all x1, starting transfers between devices: 6.66 us -> 3.45 us  [body(): far_tokens = lax.all_to_all(share, 'row', 0, 0, tiled=True)]
    ppermute x4, starting transfers between devices: 19.8 us -> 17.2 us  [across(): return lax.ppermute(value, ('row', 'yl', 'x'), perm)]
  transfers between devices with their start and end apart: 11 -> 11, of which waited for: 7 -> 8; matrix products, arithmetic and copies ran while one was open for 2% -> 2% of each run, Pallas kernels for 7% -> 7%
where the time goes in v10:
time: 117 us; the launch traced here: 115 us
  starting transfers between devices  62.2 us (53%)
  waiting for transfers between devices  30.4 us (26%)
  Pallas kernels  15.3 us (13%)
  local copies, waits for them, and re-layouts  6.35 us (5%)
    ppermute x4, starting transfers between devices, swap(): return lax.ppermute(value, axis, [(0, 1), (1, 0)])  27.6 us
    ppermute x4, starting transfers between devices, across(): return lax.ppermute(value, ('row', 'yl', 'x'), perm)  17.2 us
    ppermute x4, waiting for transfers between devices, across(): return lax.ppermute(value, ('row', 'yl', 'x'), perm)  11.6 us
    all_to_all x1, starting transfers between devices, body(): input_grad = y_sum(lax.all_to_all(chunks, ('yh', 'yl'), 0, 0, tiled=True))  10.3 us
    all_to_all x1, waiting for transfers between devices, body(): input_grad = y_sum(lax.all_to_all(chunks, ('yh', 'yl'), 0, 0, tiled=True))  8.22 us
    all_to_all x1, waiting for transfers between devices, body(): got = lax.all_to_all(both, 'x', 0, 0, tiled=True)  6.69 us
    pallas_call x1, Pallas kernels, product(): pl.pallas_call(product_kernel, out_shape=jax.ShapeDtypeStruct((4, count,...  6.56 us
    unnamed x18, local copies, waits for them, and re-layouts  4.76 us
  transfers between devices with their start and end apart: 11, of which 8 were waited for; matrix products, arithmetic and copies ran while one was open for 2% of the time, Pallas kernels for 7%

profile of v10, /device:TPU:1, one launch (start us, length us, event | category | flops | bytes accessed | tf_op | source)
XLA Modules:
  0.0 115.3 jit_solution(16207764935232779979)
XLA Ops:
  0.6 8.8 %collective-permute-start.5 = (bf16[2048,768]{1,0:T(8,128)(2,1)}, bf16[2048,768]{1,0:T(8,128)(2,1)}, u32[]{:S(2)}, u32[]{:S(2)}) collective-permute-start(bf16[2048,768]{1,0:T(8,128)(2,1)} %bitcast.14), channel_id=1, source_target_pairs={{0,128},{128,0},{1,129},{129,1},{2,130},{130,2},{3,131},{131,3},{4... | collective-permute-start | bytes 9437192 | tf_op jit(solution)/shard_map/ppermute | solution.py:260
  10.2 1.1 copy-done
  11.4 1.0 copy-done.2
  12.9 1.9 %collective-permute-start = (bf16[2,128,128]{2,1,0:T(8,128)(2,1)S(1)}, bf16[2,128,128]{2,1,0:T(8,128)(2,1)S(1)}, u32[]{:S(2)}, u32[]{:S(2)}) collective-permute-start(bf16[2,128,128]{2,1,0:T(8,128)(2,1)S(1)} %get-tuple-element.25), channel_id=1, source_target_pairs={{0,17},{1,16},{2,19},{3,18},{4,21},{5,20},{6,23},{7,22},{8,25},{9,... | collective-permute-start | bytes 196616 | tf_op jit(solution)/shard_map/ppermute | solution.py:264
  14.9 4.6 %collective-permute-done = bf16[2,128,128]{2,1,0:T(8,128)(2,1)S(1)} collective-permute-done((bf16[2,128,128]{2,1,0:T(8,128)(2,1)S(1)}, bf16[2,128,128]{2,1,0:T(8,128)(2,1)S(1)}, u32[]{:S(2)}, u32[]{:S(2)}) %collective-permute-start) | collective-permute-done | bytes 65568 | tf_op jit(solution)/shard_map/ppermute | solution.py:264
  19.5 2.6 %collective-permute-start.1 = (bf16[2,128,128]{2,1,0:T(8,128)(2,1)S(1)}, bf16[2,128,128]{2,1,0:T(8,128)(2,1)S(1)}, u32[]{:S(2)}, u32[]{:S(2)}) collective-permute-start(bf16[2,128,128]{2,1,0:T(8,128)(2,1)S(1)} %fusion), channel_id=1, source_target_pairs={{0,35},{1,34},{2,33},{3,32},{4,39},{5,38},{6,37},{7,36},{8,43},{9,... | collective-permute-start | bytes 196616 | tf_op jit(solution)/shard_map/ppermute | solution.py:264
  22.1 5.4 %collective-permute-done.1 = bf16[2,128,128]{2,1,0:T(8,128)(2,1)S(1)} collective-permute-done((bf16[2,128,128]{2,1,0:T(8,128)(2,1)S(1)}, bf16[2,128,128]{2,1,0:T(8,128)(2,1)S(1)}, u32[]{:S(2)}, u32[]{:S(2)}) %collective-permute-start.1) | collective-permute-done | bytes 65568 | tf_op jit(solution)/shard_map/ppermute | solution.py:264
  27.5 8.1 %collective-permute-start.2 = (bf16[2,128,128]{2,1,0:T(8,128)(2,1)S(1)}, bf16[2,128,128]{2,1,0:T(8,128)(2,1)S(1)}, u32[]{:S(2)}, u32[]{:S(2)}) collective-permute-start(bf16[2,128,128]{2,1,0:T(8,128)(2,1)S(1)} %fusion.2), channel_id=1, source_target_pairs={{0,116},{1,117},{2,118},{3,119},{4,112},{5,113},{6,114},{7,115},{8... | collective-permute-start | bytes 196616 | tf_op jit(solution)/shard_map/ppermute | solution.py:264
  35.6 6.6 %collective-permute-start.3 = (bf16[16,1536]{1,0:T(8,128)(2,1)S(1)}, bf16[16,1536]{1,0:T(8,128)(2,1)S(1)}, u32[]{:S(2)}, u32[]{:S(2)}) collective-permute-start(bf16[16,1536]{1,0:T(8,128)(2,1)S(1)} %dynamic_slice.3), channel_id=1, source_target_pairs={{0,256},{256,0},{1,257},{257,1},{2,258},{258,2},{3,259},{259,3},{4... | collective-permute-start | bytes 147464 | tf_op jit(solution)/shard_map/ppermute | solution.py:260
  42.3 2.1 %collective-permute-done.3 = bf16[16,1536]{1,0:T(8,128)(2,1)S(1)} collective-permute-done((bf16[16,1536]{1,0:T(8,128)(2,1)S(1)}, bf16[16,1536]{1,0:T(8,128)(2,1)S(1)}, u32[]{:S(2)}, u32[]{:S(2)}) %collective-permute-start.3) | collective-permute-done | bytes 49184 | tf_op jit(solution)/shard_map/ppermute | solution.py:260
  45.2 3.5 %all-to-all-start = ((bf16[8,16,1536]{2,1,0:T(8,128)(2,1)}), bf16[8,16,1536]{2,1,0:T(8,128)(2,1)S(1)}, u32[]{:S(2)}, u32[]{:S(2)}) async-start(bf16[8,16,1536]{2,1,0:T(8,128)(2,1)} %broadcast_in_dim.2), calls=%async_computation | async-start | bytes 786432 | tf_op jit(solution)/shard_map/all_to_all | solution.py:279
  48.7 4.5 %collective-permute-start.4 = (bf16[128,128]{1,0:T(8,128)(2,1)S(1)}, bf16[128,128]{1,0:T(8,128)(2,1)S(1)}, u32[]{:S(2)}, u32[]{:S(2)}) collective-permute-start(bf16[128,128]{1,0:T(8,128)(2,1)S(1)} %fusion.1), channel_id=1, source_target_pairs={{0,8},{1,9},{2,10},{3,11},{4,12},{5,13},{6,14},{7,15},{8,0},{9,1},... | collective-permute-start | bytes 98312 | tf_op jit(solution)/shard_map/ppermute | solution.py:264
  53.2 1.6 %collective-permute-done.4 = bf16[128,128]{1,0:T(8,128)(2,1)S(1)} collective-permute-done((bf16[128,128]{1,0:T(8,128)(2,1)S(1)}, bf16[128,128]{1,0:T(8,128)(2,1)S(1)}, u32[]{:S(2)}, u32[]{:S(2)}) %collective-permute-start.4) | collective-permute-done | bytes 32800 | tf_op jit(solution)/shard_map/ppermute | solution.py:264
  54.9 4.5 %shard_map.59 = (f32[64,4096]{1,0:T(8,128)S(1)}, f32[64,4096]{1,0:T(8,128)}) custom-call(s32[4]{0:T(128)S(1)} %pad_add_fusion.place, f32[128,128]{1,0:T(8,128)S(1)} %convert_add_fusion.3.left_ref, f32[128,128]{1,0:T(8,128)S(1)} %slice_bitcast_fusion.right_ref, bf16[128,2048]{1,0:T(8,128)(2,1)S(1)} %copy-done.3, bf16[128,3072]{1,0:T(8,128)(2,1)S(1)} %copy-done.1), custom_call_target="tpu_custom_call" | custom-call | flops 1 | bytes 1 | tf_op jit(solution)/shard_map/pallas_call | solution.py:192
  59.4 1.1 all-to-all-done.far_ref
  61.2 6.6 %shard_map.60 = bf16[4,128,1024]{2,1,0:T(8,128)(2,1)} custom-call(s32[4]{0:T(128)} %copy-done.6, bf16[128,3072]{1,0:T(8,128)(2,1)} %near_ref.1, bf16[8,16,1536]{2,1,0:T(8,128)(2,1)} %copy-done.8, bf16[2048,768]{1,0:T(8,128)(2,1)} %bitcast.15, bf16[2048,768]{1,0:T(8,128)(2,1)} %bitcast.16, bf16[2048,768]{1,0:T(8,128)(2,1)} %collective-permute-done.5.other_lo.other_hi, ...), custom_call_target="tpu_custom_call" | custom-call | flops 1 | bytes 1 | tf_op jit(solution)/shard_map/pallas_call | solution.py:81
  67.8 5.7 %collective-permute-start.6 = (f32[64,4096]{1,0:T(8,128)}, f32[64,4096]{1,0:T(8,128)S(1)}, u32[]{:S(2)}, u32[]{:S(2)}) collective-permute-start(f32[64,4096]{1,0:T(8,128)} %get-tuple-element.34), channel_id=1, source_target_pairs={{0,128},{128,0},{1,129},{129,1},{2,130},{130,2},{3,131},{131,3},{4... | collective-permute-start | bytes 3145736 | tf_op jit(solution)/shard_map/ppermute | solution.py:260
  73.5 3.8 %all-to-all-start.1 = ((bf16[4,128,1024]{2,1,0:T(8,128)(2,1)}), bf16[4,128,1024]{2,1,0:T(8,128)(2,1)S(1)}, u32[]{:S(2)}, u32[]{:S(2)}) async-start(bf16[4,128,1024]{2,1,0:T(8,128)(2,1)} %shard_map.60), calls=%async_computation.1 | async-start | bytes 2097152 | tf_op jit(solution)/shard_map/all_to_all | solution.py:286
  79.0 6.6 %collective-permute-start.7 = (bf16[32,4096]{1,0:T(8,128)(2,1)}, bf16[32,4096]{1,0:T(8,128)(2,1)S(1)}, u32[]{:S(2)}, u32[]{:S(2)}) collective-permute-start(bf16[32,4096]{1,0:T(8,128)(2,1)} %get-tuple-element.37), channel_id=1, source_target_pairs={{0,256},{256,0},{1,257},{257,1},{2,258},{258,2},{3,259},{259,3},{4... | collective-permute-start | bytes 786440 | tf_op jit(solution)/shard_map/ppermute | solution.py:260
  85.5 6.7 %all-to-all-done.1.got_ref = bf16[4,128,1024]{2,1,0:T(8,128)(2,1)S(1)} async-done(((bf16[4,128,1024]{2,1,0:T(8,128)(2,1)}), bf16[4,128,1024]{2,1,0:T(8,128)(2,1)S(1)}, u32[]{:S(2)}, u32[]{:S(2)}) %all-to-all-start.1) | async-done | bytes 1048608 | tf_op jit(solution)/shard_map/all_to_all | solution.py:286
  92.2 1.4 %shard_map.62 = bf16[2,64,1024]{2,1,0:T(8,128)(2,1)} custom-call(s32[4]{0:T(128)S(1)} %copy-done.7, bf16[4,128,1024]{2,1,0:T(8,128)(2,1)S(1)} %all-to-all-done.1.got_ref), custom_call_target="tpu_custom_call" | custom-call | flops 1 | bytes 1 | tf_op jit(solution)/shard_map/pallas_call | solution.py:115
  94.3 10.3 %all-to-all-start.2 = ((bf16[8,16,1024]{2,1,0:T(8,128)(2,1)}), bf16[8,16,1024]{2,1,0:T(8,128)(2,1)S(1)}, u32[]{:S(2)}, u32[]{:S(2)}) async-start(bf16[8,16,1024]{2,1,0:T(8,128)(2,1)} %bitcast.7), calls=%async_computation.2 | async-start | bytes 524288 | tf_op jit(solution)/shard_map/all_to_all | solution.py:294
  104.6 1.0 copy-done.5
  106.4 8.2 %all-to-all-done.2.got_ref = bf16[8,16,1024]{2,1,0:T(8,128)(2,1)S(1)} async-done(((bf16[8,16,1024]{2,1,0:T(8,128)(2,1)}), bf16[8,16,1024]{2,1,0:T(8,128)(2,1)S(1)}, u32[]{:S(2)}, u32[]{:S(2)}) %all-to-all-start.2) | async-done | bytes 262176 | tf_op jit(solution)/shard_map/all_to_all | solution.py:294
  (32 shorter events, 6.9 us)
Async XLA Ops:
  0.6 59.9 %collective-permute-start.5 = (bf16[2048,768]{1,0:T(8,128)(2,1)}, bf16[2048,768]{1,0:T(8,128)(2,1)}, u32[]{:S(2)}, u32[]{:S(2)}) collective-permute-start(bf16[2048,768]{1,0:T(8,128)(2,1)} %bitcast.14), channel_id=1, source_target_pairs={{0,128},{128,0},{1,129},{129,1},{2,130},{130,2},{3,131},{131,3},{4... | collective-permute-start | bytes 9437192 | tf_op jit(solution)/shard_map/ppermute | solution.py:260
  10.2 1.1 copy-start
  11.4 1.0 copy-start.2
  12.4 42.4 %copy-start.1 = (bf16[128,3072]{1,0:T(8,128)(2,1)S(1)}, bf16[128,3072]{1,0:T(8,128)(2,1)}, u32[]{:S(2)}) copy-start(bf16[128,3072]{1,0:T(8,128)(2,1)} %near_ref.1) | copy-start | bytes 2359300
  12.4 42.4 %copy-start.3 = (bf16[128,2048]{1,0:T(8,128)(2,1)S(1)}, bf16[128,2048]{1,0:T(8,128)(2,1)}, u32[]{:S(2)}) copy-start(bf16[128,2048]{1,0:T(8,128)(2,1)} %acts_hbm.1) | copy-start | bytes 1572868
  12.9 6.5 %collective-permute-start = (bf16[2,128,128]{2,1,0:T(8,128)(2,1)S(1)}, bf16[2,128,128]{2,1,0:T(8,128)(2,1)S(1)}, u32[]{:S(2)}, u32[]{:S(2)}) collective-permute-start(bf16[2,128,128]{2,1,0:T(8,128)(2,1)S(1)} %get-tuple-element.25), channel_id=1, source_target_pairs={{0,17},{1,16},{2,19},{3,18},{4,21},{5,20},{6,23},{7,22},{8,25},{9,... | collective-permute-start | bytes 196616 | tf_op jit(solution)/shard_map/ppermute | solution.py:264
  19.5 8.0 %collective-permute-start.1 = (bf16[2,128,128]{2,1,0:T(8,128)(2,1)S(1)}, bf16[2,128,128]{2,1,0:T(8,128)(2,1)S(1)}, u32[]{:S(2)}, u32[]{:S(2)}) collective-permute-start(bf16[2,128,128]{2,1,0:T(8,128)(2,1)S(1)} %fusion), channel_id=1, source_target_pairs={{0,35},{1,34},{2,33},{3,32},{4,39},{5,38},{6,37},{7,36},{8,43},{9,... | collective-permute-start | bytes 196616 | tf_op jit(solution)/shard_map/ppermute | solution.py:264
  27.5 14.7 %collective-permute-start.2 = (bf16[2,128,128]{2,1,0:T(8,128)(2,1)S(1)}, bf16[2,128,128]{2,1,0:T(8,128)(2,1)S(1)}, u32[]{:S(2)}, u32[]{:S(2)}) collective-permute-start(bf16[2,128,128]{2,1,0:T(8,128)(2,1)S(1)} %fusion.2), channel_id=1, source_target_pairs={{0,116},{1,117},{2,118},{3,119},{4,112},{5,113},{6,114},{7,115},{8... | collective-permute-start | bytes 196616 | tf_op jit(solution)/shard_map/ppermute | solution.py:264
  35.6 8.8 %collective-permute-start.3 = (bf16[16,1536]{1,0:T(8,128)(2,1)S(1)}, bf16[16,1536]{1,0:T(8,128)(2,1)S(1)}, u32[]{:S(2)}, u32[]{:S(2)}) collective-permute-start(bf16[16,1536]{1,0:T(8,128)(2,1)S(1)} %dynamic_slice.3), channel_id=1, source_target_pairs={{0,256},{256,0},{1,257},{257,1},{2,258},{258,2},{3,259},{259,3},{4... | collective-permute-start | bytes 147464 | tf_op jit(solution)/shard_map/ppermute | solution.py:260
  45.2 15.3 %all-to-all-start = ((bf16[8,16,1536]{2,1,0:T(8,128)(2,1)}), bf16[8,16,1536]{2,1,0:T(8,128)(2,1)S(1)}, u32[]{:S(2)}, u32[]{:S(2)}) async-start(bf16[8,16,1536]{2,1,0:T(8,128)(2,1)} %broadcast_in_dim.2), calls=%async_computation | async-start | bytes 786432 | tf_op jit(solution)/shard_map/all_to_all | solution.py:279
  48.7 11.8 %copy-start.6 = (s32[4]{0:T(128)}, s32[4]{0:T(128)S(1)}, u32[]{:S(2)}) copy-start(s32[4]{0:T(128)S(1)} %pad_add_fusion.place) | copy-start | bytes 52
  48.7 6.1 %collective-permute-start.4 = (bf16[128,128]{1,0:T(8,128)(2,1)S(1)}, bf16[128,128]{1,0:T(8,128)(2,1)S(1)}, u32[]{:S(2)}, u32[]{:S(2)}) collective-permute-start(bf16[128,128]{1,0:T(8,128)(2,1)S(1)} %fusion.1), channel_id=1, source_target_pairs={{0,8},{1,9},{2,10},{3,11},{4,12},{5,13},{6,14},{7,15},{8,0},{9,1},... | collective-permute-start | bytes 98312 | tf_op jit(solution)/shard_map/ppermute | solution.py:264
  60.5 0.7 copy-start.8
  67.8 24.4 %copy-start.7 = (s32[4]{0:T(128)S(1)}, s32[4]{0:T(128)}, u32[]{:S(2)}) copy-start(s32[4]{0:T(128)} %copy-done.6) | copy-start | bytes 52
  67.8 9.5 %collective-permute-start.6 = (f32[64,4096]{1,0:T(8,128)}, f32[64,4096]{1,0:T(8,128)S(1)}, u32[]{:S(2)}, u32[]{:S(2)}) collective-permute-start(f32[64,4096]{1,0:T(8,128)} %get-tuple-element.34), channel_id=1, source_target_pairs={{0,128},{128,0},{1,129},{129,1},{2,130},{130,2},{3,131},{131,3},{4... | collective-permute-start | bytes 3145736 | tf_op jit(solution)/shard_map/ppermute | solution.py:260
  73.5 18.7 %all-to-all-start.1 = ((bf16[4,128,1024]{2,1,0:T(8,128)(2,1)}), bf16[4,128,1024]{2,1,0:T(8,128)(2,1)S(1)}, u32[]{:S(2)}, u32[]{:S(2)}) async-start(bf16[4,128,1024]{2,1,0:T(8,128)(2,1)} %shard_map.60), calls=%async_computation.1 | async-start | bytes 2097152 | tf_op jit(solution)/shard_map/all_to_all | solution.py:286
  78.2 0.8 copy-start.4
  79.0 15.4 %collective-permute-start.7 = (bf16[32,4096]{1,0:T(8,128)(2,1)}, bf16[32,4096]{1,0:T(8,128)(2,1)S(1)}, u32[]{:S(2)}, u32[]{:S(2)}) collective-permute-start(bf16[32,4096]{1,0:T(8,128)(2,1)} %get-tuple-element.37), channel_id=1, source_target_pairs={{0,256},{256,0},{1,257},{257,1},{2,258},{258,2},{3,259},{259,3},{4... | collective-permute-start | bytes 786440 | tf_op jit(solution)/shard_map/ppermute | solution.py:260
  94.3 20.3 %all-to-all-start.2 = ((bf16[8,16,1024]{2,1,0:T(8,128)(2,1)}), bf16[8,16,1024]{2,1,0:T(8,128)(2,1)S(1)}, u32[]{:S(2)}, u32[]{:S(2)}) async-start(bf16[8,16,1024]{2,1,0:T(8,128)(2,1)} %bitcast.7), calls=%async_computation.2 | async-start | bytes 524288 | tf_op jit(solution)/shard_map/all_to_all | solution.py:294
  104.6 1.0 copy-start.5

commit v11 on v10

--- a/solution.py
+++ b/solution.py
@@ -151,7 +151,7 @@
     return jnp.where(unit == wanted, 1.0, 0.0).astype(BF)
 
 
-def stats_kernel(place, left_ref, right_ref, acts_hbm, grads_hbm, keep_ref, send_ref, acts_ref, grads_ref, sems):
+def stats_kernel(place, total_ref, pair_ref, left2_ref, left3_ref, acts_hbm, grads_hbm, keep_ref, send_ref, acts_ref, grads_ref, sems):
     hidden = grads_ref.shape[1]
     width = acts_ref.shape[1]
     copies = []
@@ -166,7 +166,8 @@
         picked = lax.dot_general(pick, data, NT, preferred_element_type=F32).astype(BF)
         return jnp.dot(picked, mix, preferred_element_type=F32) * (1.0 / TOKENS)
 
-    right = (right_ref[...] / D).astype(BF)
+    right = total_ref[1] + pair_ref[1].astype(F32)
+    right = (right / D).astype(BF)
     pick = picker(place, place[2], 32, 8)
     for j in range(hidden // BLOCK):
         lanes = slice(j * BLOCK, (j + 1) * BLOCK)
@@ -174,7 +175,8 @@
         out = rows(pick, right, grads_ref[:, lanes])
         keep_ref[:, lanes] = out[:64]
         send_ref[:, lanes] = out[64:]
-    left = (left_ref[...] / FF).astype(BF)
+    left = total_ref[0] + pair_ref[0].astype(F32) + left2_ref[...].astype(F32) + left3_ref[...].astype(F32)
+    left = (left / FF).astype(BF)
     pick = picker(place, place[3], 16, 16)
     for j in range(width // BLOCK):
         copies[hidden // BLOCK + j].wait()
@@ -185,14 +187,14 @@
             send_ref[at, hidden:] = out[32 + dy * 16 : 32 + dy * 16 + 16]
 
 
-def stats(place, left, right, acts, grads):
+def stats(place, total, pair, left2, left3, acts, grads):
     shape = jax.ShapeDtypeStruct((64, grads.shape[1] + BLOCK), F32)
     vmem = pl.BlockSpec(memory_space=pltpu.VMEM)
     hbm = pl.BlockSpec(memory_space=pltpu.HBM)
     return pl.pallas_call(
         stats_kernel,
         out_shape=(shape, shape),
-        in_specs=[pl.BlockSpec(memory_space=pltpu.SMEM), vmem, vmem, hbm, hbm],
+        in_specs=[pl.BlockSpec(memory_space=pltpu.SMEM)] + [vmem] * 4 + [hbm, hbm],
         out_specs=[vmem, vmem],
         scratch_shapes=[
             pltpu.VMEM(acts.shape, BF),
@@ -201,7 +203,7 @@
         ],
         compiler_params=params(16),
         cost_estimate=cost(),
-    )(place, left, right, acts, grads)
+    )(place, total, pair, left2, left3, acts, grads)
 
 
 def core_sum_kernel(keep_ref, got_ref, near_ref, far_ref):
@@ -272,21 +274,19 @@
     total, send = prepare(acts_in, grad_out)
     total = total + across(send, 1, 0, 1).astype(F32)
     total = total + across(total.astype(BF), 2, 0, 3).astype(F32)
-    total = total + across(total.astype(BF), 7, 1, 0).astype(F32)
-    left, right = total[0], total[1]
+    send = total.astype(BF)
+    pair = across(send, 7, 1, 0)
+    left2, left3 = across(send[0], 0, 2, 0), across(send[0], 0, 3, 0)
+
     share = jnp.broadcast_to(share[None], (8,) + share.shape)
-    send, share = barrier((left.astype(BF), share))
     far_tokens = lax.all_to_all(share, "row", 0, 0, tiled=True)
-    left = left + across(send, 0, 2, 0).astype(F32)
-
-    keep, send = stats(place, left, right, acts, grad_out)
-    far_tokens, send = barrier((far_tokens, send))
-    both = product(place, grad_out, far_tokens, weight, weight_far)
-    both, send = barrier((both, send))
+
+    keep, send = stats(place, total, pair, left2, left3, acts, grad_out)
+    near_rows, far_rows = core_sum(keep, swap(send, "core"))
+    near_rows, near_tokens, far_tokens = barrier((near_rows, grad_out, far_tokens))
+    far_rows = swap(far_rows, "yh")
+    both = product(place, near_tokens, far_tokens, weight, weight_far)
     got = lax.all_to_all(both, "x", 0, 0, tiled=True)
-    near_rows, far_rows = core_sum(keep, swap(send, "core"))
-    got, near_rows = barrier((got, near_rows))
-    far_rows = swap(far_rows, "yh")
 
     chunks = x_sum(place, got)
     chunks = chunks.reshape(8, -1, chunks.shape[2])

time: 117 us -> 132 us (1.13)
  the two profiles are of different devices: /device:TPU:1 before, /device:TPU:2 now
where the time goes in v11:
time: 132 us; the launch traced here: 131 us
  starting transfers between devices  67.6 us (51%)
  waiting for transfers between devices  40.4 us (31%)
  Pallas kernels  14.5 us (11%)
  local copies, waits for them, and re-layouts  7.33 us (6%)
    ppermute x5, starting transfers between devices, across(): return lax.ppermute(value, ('row', 'yl', 'x'), perm)  29.4 us
    ppermute x4, starting transfers between devices, swap(): return lax.ppermute(value, axis, [(0, 1), (1, 0)])  17.5 us
    all_to_all x1, waiting for transfers between devices, body(): far_tokens = lax.all_to_all(share, 'row', 0, 0, tiled=True)  14.4 us
    all_to_all x1, waiting for transfers between devices, body(): input_grad = y_sum(lax.all_to_all(chunks, ('yh', 'yl'), 0, 0, tiled=True))  9.65 us
    all_to_all x1, starting transfers between devices, body(): input_grad = y_sum(lax.all_to_all(chunks, ('yh', 'yl'), 0, 0, tiled=True))  8.49 us
    ppermute x5, waiting for transfers between devices, across(): return lax.ppermute(value, ('row', 'yl', 'x'), perm)  7.74 us
    pallas_call x1, Pallas kernels, product(): pl.pallas_call(product_kernel, out_shape=jax.ShapeDtypeStruct((4, count,...  6.56 us
    all_to_all x1, starting transfers between devices, body(): far_tokens = lax.all_to_all(share, 'row', 0, 0, tiled=True)  6.45 us
  transfers between devices with their start and end apart: 12, of which 7 were waited for; matrix products, arithmetic and copies ran while one was open for 1% of the time, Pallas kernels for 6%

profile of v11, /device:TPU:2, one launch (start us, length us, event | category | flops | bytes accessed | tf_op | source)
XLA Modules:
  0.0 130.7 jit_solution(4582146891191507255)
XLA Ops:
  0.6 1.9 %collective-permute-start.7 = (bf16[2048,768]{1,0:T(8,128)(2,1)}, bf16[2048,768]{1,0:T(8,128)(2,1)}, u32[]{:S(2)}, u32[]{:S(2)}) collective-permute-start(bf16[2048,768]{1,0:T(8,128)(2,1)} %bitcast.8), channel_id=1, source_target_pairs={{0,128},{128,0},{1,129},{129,1},{2,130},{130,2},{3,131},{131,3},{4... | collective-permute-start | bytes 9437192 | tf_op jit(solution)/shard_map/ppermute | solution.py:262
  3.4 1.1 copy-done
  6.1 4.3 %collective-permute-start = (bf16[2,128,128]{2,1,0:T(8,128)(2,1)S(1)}, bf16[2,128,128]{2,1,0:T(8,128)(2,1)S(1)}, u32[]{:S(2)}, u32[]{:S(2)}) collective-permute-start(bf16[2,128,128]{2,1,0:T(8,128)(2,1)S(1)} %get-tuple-element.20), channel_id=1, source_target_pairs={{0,17},{1,16},{2,19},{3,18},{4,21},{5,20},{6,23},{7,22},{8,25},{9,... | collective-permute-start | bytes 196616 | tf_op jit(solution)/shard_map/ppermute | solution.py:266
  10.3 3.0 %collective-permute-done = bf16[2,128,128]{2,1,0:T(8,128)(2,1)S(1)} collective-permute-done((bf16[2,128,128]{2,1,0:T(8,128)(2,1)S(1)}, bf16[2,128,128]{2,1,0:T(8,128)(2,1)S(1)}, u32[]{:S(2)}, u32[]{:S(2)}) %collective-permute-start) | collective-permute-done | bytes 65568 | tf_op jit(solution)/shard_map/ppermute | solution.py:266
  13.4 7.4 %collective-permute-start.1 = (bf16[2,128,128]{2,1,0:T(8,128)(2,1)S(1)}, bf16[2,128,128]{2,1,0:T(8,128)(2,1)S(1)}, u32[]{:S(2)}, u32[]{:S(2)}) collective-permute-start(bf16[2,128,128]{2,1,0:T(8,128)(2,1)S(1)} %fusion), channel_id=1, source_target_pairs={{0,35},{1,34},{2,33},{3,32},{4,39},{5,38},{6,37},{7,36},{8,43},{9,... | collective-permute-start | bytes 196616 | tf_op jit(solution)/shard_map/ppermute | solution.py:266
  20.8 2.2 %collective-permute-done.1 = bf16[2,128,128]{2,1,0:T(8,128)(2,1)S(1)} collective-permute-done((bf16[2,128,128]{2,1,0:T(8,128)(2,1)S(1)}, bf16[2,128,128]{2,1,0:T(8,128)(2,1)S(1)}, u32[]{:S(2)}, u32[]{:S(2)}) %collective-permute-start.1) | collective-permute-done | bytes 65568 | tf_op jit(solution)/shard_map/ppermute | solution.py:266
  23.0 6.2 %collective-permute-start.4 = (bf16[128,128]{1,0:T(8,128)(2,1)S(1)}, bf16[128,128]{1,0:T(8,128)(2,1)S(1)}, u32[]{:S(2)}, u32[]{:S(2)}) collective-permute-start(bf16[128,128]{1,0:T(8,128)(2,1)S(1)} %slice_bitcast_fusion), channel_id=1, source_target_pairs={{0,12},{1,13},{2,14},{3,15},{4,8},{5,9},{6,10},{7,11},{8,4},{9,5},... | collective-permute-start | bytes 98312 | tf_op jit(solution)/shard_map/ppermute | solution.py:266
  29.3 1.9 %collective-permute-start.3 = (bf16[128,128]{1,0:T(8,128)(2,1)S(1)}, bf16[128,128]{1,0:T(8,128)(2,1)S(1)}, u32[]{:S(2)}, u32[]{:S(2)}) collective-permute-start(bf16[128,128]{1,0:T(8,128)(2,1)S(1)} %slice_bitcast_fusion), channel_id=1, source_target_pairs={{0,8},{1,9},{2,10},{3,11},{4,12},{5,13},{6,14},{7,15},{8,0},{9,1},... | collective-permute-start | bytes 98312 | tf_op jit(solution)/shard_map/ppermute | solution.py:266
  31.2 9.6 %collective-permute-start.2 = (bf16[2,128,128]{2,1,0:T(8,128)(2,1)S(1)}, bf16[2,128,128]{2,1,0:T(8,128)(2,1)S(1)}, u32[]{:S(2)}, u32[]{:S(2)}) collective-permute-start(bf16[2,128,128]{2,1,0:T(8,128)(2,1)S(1)} %get-tuple-element.33), channel_id=1, source_target_pairs={{0,116},{1,117},{2,118},{3,119},{4,112},{5,113},{6,114},{7,115},{8... | collective-permute-start | bytes 196616 | tf_op jit(solution)/shard_map/ppermute | solution.py:266
  40.9 2.5 %collective-permute-done.2.pair_ref = bf16[2,128,128]{2,1,0:T(8,128)(2,1)S(1)} collective-permute-done((bf16[2,128,128]{2,1,0:T(8,128)(2,1)S(1)}, bf16[2,128,128]{2,1,0:T(8,128)(2,1)S(1)}, u32[]{:S(2)}, u32[]{:S(2)}) %collective-permute-start.2) | collective-permute-done | bytes 65568 | tf_op jit(solution)/shard_map/ppermute | solution.py:266
  43.4 1.1 copy-done.1
  45.6 4.5 %shard_map.59 = (f32[64,4096]{1,0:T(8,128)S(1)}, f32[64,4096]{1,0:T(8,128)}) custom-call(s32[4]{0:T(128)S(1)} %pad_add_fusion.place, f32[2,128,128]{2,1,0:T(8,128)S(1)} %get-tuple-element.34.total_ref, bf16[2,128,128]{2,1,0:T(8,128)(2,1)S(1)} %collective-permute-done.2.pair_ref, bf16[128,128]{1,0:T(8,128)(2,1)S(1)} %collective-permute-done.3.left2_ref, ...), custom_call_target="tpu_custom_call" | custom-call | flops 1 | bytes 1 | tf_op jit(solution)/shard_map/pallas_call | solution.py:194
  50.1 1.9 %collective-permute-start.5 = (f32[64,4096]{1,0:T(8,128)}, f32[64,4096]{1,0:T(8,128)S(1)}, u32[]{:S(2)}, u32[]{:S(2)}) collective-permute-start(f32[64,4096]{1,0:T(8,128)} %get-tuple-element.22), channel_id=1, source_target_pairs={{0,128},{128,0},{1,129},{129,1},{2,130},{130,2},{3,131},{131,3},{4... | collective-permute-start | bytes 3145736 | tf_op jit(solution)/shard_map/ppermute | solution.py:262
  52.0 7.4 %collective-permute-start.6 = (bf16[16,1536]{1,0:T(8,128)(2,1)S(1)}, bf16[16,1536]{1,0:T(8,128)(2,1)S(1)}, u32[]{:S(2)}, u32[]{:S(2)}) collective-permute-start(bf16[16,1536]{1,0:T(8,128)(2,1)S(1)} %dynamic_slice.3), channel_id=1, source_target_pairs={{0,256},{256,0},{1,257},{257,1},{2,258},{258,2},{3,259},{259,3},{4... | collective-permute-start | bytes 147464 | tf_op jit(solution)/shard_map/ppermute | solution.py:262
  59.4 2.6 %collective-permute-done.6 = bf16[16,1536]{1,0:T(8,128)(2,1)S(1)} collective-permute-done((bf16[16,1536]{1,0:T(8,128)(2,1)S(1)}, bf16[16,1536]{1,0:T(8,128)(2,1)S(1)}, u32[]{:S(2)}, u32[]{:S(2)}) %collective-permute-start.6) | collective-permute-done | bytes 49184 | tf_op jit(solution)/shard_map/ppermute | solution.py:262
  62.8 6.5 %all-to-all-start = ((bf16[8,16,1536]{2,1,0:T(8,128)(2,1)}), bf16[8,16,1536]{2,1,0:T(8,128)(2,1)S(1)}, u32[]{:S(2)}, u32[]{:S(2)}) async-start(bf16[8,16,1536]{2,1,0:T(8,128)(2,1)} %broadcast_in_dim.2), calls=%async_computation | async-start | bytes 786432 | tf_op jit(solution)/shard_map/all_to_all | solution.py:282
  69.4 14.4 %all-to-all-done.far_ref = bf16[8,16,1536]{2,1,0:T(8,128)(2,1)S(1)} async-done(((bf16[8,16,1536]{2,1,0:T(8,128)(2,1)}), bf16[8,16,1536]{2,1,0:T(8,128)(2,1)S(1)}, u32[]{:S(2)}, u32[]{:S(2)}) %all-to-all-start) | async-done | bytes 393248 | tf_op jit(solution)/shard_map/all_to_all | solution.py:282
  84.5 6.6 %shard_map.61 = bf16[4,128,1024]{2,1,0:T(8,128)(2,1)} custom-call(s32[4]{0:T(128)} %copy-done.4, bf16[128,3072]{1,0:T(8,128)(2,1)} %near_ref, bf16[8,16,1536]{2,1,0:T(8,128)(2,1)} %copy-done.6, bf16[2048,768]{1,0:T(8,128)(2,1)} %bitcast.9, bf16[2048,768]{1,0:T(8,128)(2,1)} %bitcast.10, bf16[2048,768]{1,0:T(8,128)(2,1)} %collective-permute-done.7.other_lo.other_hi, ...), custom_call_target="tpu_custom_call" | custom-call | flops 1 | bytes 1 | tf_op jit(solution)/shard_map/pallas_call | solution.py:81
  91.1 5.8 %all-to-all-start.1 = ((bf16[4,128,1024]{2,1,0:T(8,128)(2,1)}), bf16[4,128,1024]{2,1,0:T(8,128)(2,1)S(1)}, u32[]{:S(2)}, u32[]{:S(2)}) async-start(bf16[4,128,1024]{2,1,0:T(8,128)(2,1)} %shard_map.61), calls=%async_computation.1 | async-start | bytes 2097152 | tf_op jit(solution)/shard_map/all_to_all | solution.py:289
  96.8 6.2 %collective-permute-start.8 = (bf16[32,4096]{1,0:T(8,128)(2,1)S(1)}, bf16[32,4096]{1,0:T(8,128)(2,1)S(1)}, u32[]{:S(2)}, u32[]{:S(2)}) collective-permute-start(bf16[32,4096]{1,0:T(8,128)(2,1)S(1)} %get-tuple-element.27), channel_id=1, source_target_pairs={{0,256},{256,0},{1,257},{257,1},{2,258},{258,2},{3,259},{259,3},{4... | collective-permute-start | bytes 786440 | tf_op jit(solution)/shard_map/ppermute | solution.py:262
  103.1 6.0 %all-to-all-done.1.got_ref = bf16[4,128,1024]{2,1,0:T(8,128)(2,1)S(1)} async-done(((bf16[4,128,1024]{2,1,0:T(8,128)(2,1)}), bf16[4,128,1024]{2,1,0:T(8,128)(2,1)S(1)}, u32[]{:S(2)}, u32[]{:S(2)}) %all-to-all-start.1) | async-done | bytes 1048608 | tf_op jit(solution)/shard_map/all_to_all | solution.py:289
  109.7 1.4 %shard_map.62 = bf16[2,64,1024]{2,1,0:T(8,128)(2,1)} custom-call(s32[4]{0:T(128)S(1)} %copy-done.5, bf16[4,128,1024]{2,1,0:T(8,128)(2,1)S(1)} %all-to-all-done.1.got_ref), custom_call_target="tpu_custom_call" | custom-call | flops 1 | bytes 1 | tf_op jit(solution)/shard_map/pallas_call | solution.py:115
  111.1 8.5 %all-to-all-start.2 = ((bf16[8,16,1024]{2,1,0:T(8,128)(2,1)}), bf16[8,16,1024]{2,1,0:T(8,128)(2,1)S(1)}, u32[]{:S(2)}, u32[]{:S(2)}) async-start(bf16[8,16,1024]{2,1,0:T(8,128)(2,1)} %bitcast.6), calls=%async_computation.2 | async-start | bytes 524288 | tf_op jit(solution)/shard_map/all_to_all | solution.py:294
  120.4 9.7 %all-to-all-done.2.got_ref = bf16[8,16,1024]{2,1,0:T(8,128)(2,1)S(1)} async-done(((bf16[8,16,1024]{2,1,0:T(8,128)(2,1)}), bf16[8,16,1024]{2,1,0:T(8,128)(2,1)S(1)}, u32[]{:S(2)}, u32[]{:S(2)}) %all-to-all-start.2) | async-done | bytes 262176 | tf_op jit(solution)/shard_map/all_to_all | solution.py:294
  (27 shorter events, 7.3 us)
Async XLA Ops:
  0.6 83.1 %collective-permute-start.7 = (bf16[2048,768]{1,0:T(8,128)(2,1)}, bf16[2048,768]{1,0:T(8,128)(2,1)}, u32[]{:S(2)}, u32[]{:S(2)}) collective-permute-start(bf16[2048,768]{1,0:T(8,128)(2,1)} %bitcast.8), channel_id=1, source_target_pairs={{0,128},{128,0},{1,129},{129,1},{2,130},{130,2},{3,131},{131,3},{4... | collective-permute-start | bytes 9437192 | tf_op jit(solution)/shard_map/ppermute | solution.py:262
  3.4 1.1 copy-start
  4.5 1.0 copy-start.2
  6.1 7.3 %collective-permute-start = (bf16[2,128,128]{2,1,0:T(8,128)(2,1)S(1)}, bf16[2,128,128]{2,1,0:T(8,128)(2,1)S(1)}, u32[]{:S(2)}, u32[]{:S(2)}) collective-permute-start(bf16[2,128,128]{2,1,0:T(8,128)(2,1)S(1)} %get-tuple-element.20), channel_id=1, source_target_pairs={{0,17},{1,16},{2,19},{3,18},{4,21},{5,20},{6,23},{7,22},{8,25},{9,... | collective-permute-start | bytes 196616 | tf_op jit(solution)/shard_map/ppermute | solution.py:266
  13.4 9.6 %collective-permute-start.1 = (bf16[2,128,128]{2,1,0:T(8,128)(2,1)S(1)}, bf16[2,128,128]{2,1,0:T(8,128)(2,1)S(1)}, u32[]{:S(2)}, u32[]{:S(2)}) collective-permute-start(bf16[2,128,128]{2,1,0:T(8,128)(2,1)S(1)} %fusion), channel_id=1, source_target_pairs={{0,35},{1,34},{2,33},{3,32},{4,39},{5,38},{6,37},{7,36},{8,43},{9,... | collective-permute-start | bytes 196616 | tf_op jit(solution)/shard_map/ppermute | solution.py:266
  23.0 17.9 %collective-permute-start.4 = (bf16[128,128]{1,0:T(8,128)(2,1)S(1)}, bf16[128,128]{1,0:T(8,128)(2,1)S(1)}, u32[]{:S(2)}, u32[]{:S(2)}) collective-permute-start(bf16[128,128]{1,0:T(8,128)(2,1)S(1)} %slice_bitcast_fusion), channel_id=1, source_target_pairs={{0,12},{1,13},{2,14},{3,15},{4,8},{5,9},{6,10},{7,11},{8,4},{9,5},... | collective-permute-start | bytes 98312 | tf_op jit(solution)/shard_map/ppermute | solution.py:266
  29.3 11.6 %collective-permute-start.3 = (bf16[128,128]{1,0:T(8,128)(2,1)S(1)}, bf16[128,128]{1,0:T(8,128)(2,1)S(1)}, u32[]{:S(2)}, u32[]{:S(2)}) collective-permute-start(bf16[128,128]{1,0:T(8,128)(2,1)S(1)} %slice_bitcast_fusion), channel_id=1, source_target_pairs={{0,8},{1,9},{2,10},{3,11},{4,12},{5,13},{6,14},{7,15},{8,0},{9,1},... | collective-permute-start | bytes 98312 | tf_op jit(solution)/shard_map/ppermute | solution.py:266
  31.2 12.2 %collective-permute-start.2 = (bf16[2,128,128]{2,1,0:T(8,128)(2,1)S(1)}, bf16[2,128,128]{2,1,0:T(8,128)(2,1)S(1)}, u32[]{:S(2)}, u32[]{:S(2)}) collective-permute-start(bf16[2,128,128]{2,1,0:T(8,128)(2,1)S(1)} %get-tuple-element.33), channel_id=1, source_target_pairs={{0,116},{1,117},{2,118},{3,119},{4,112},{5,113},{6,114},{7,115},{8... | collective-permute-start | bytes 196616 | tf_op jit(solution)/shard_map/ppermute | solution.py:266
  40.9 42.9 %copy-start.4 = (s32[4]{0:T(128)}, s32[4]{0:T(128)S(1)}, u32[]{:S(2)}) copy-start(s32[4]{0:T(128)S(1)} %pad_add_fusion.place) | copy-start | bytes 52
  43.4 1.1 copy-start.1
  44.5 1.0 copy-start.3
  50.1 19.1 %collective-permute-start.5 = (f32[64,4096]{1,0:T(8,128)}, f32[64,4096]{1,0:T(8,128)S(1)}, u32[]{:S(2)}, u32[]{:S(2)}) collective-permute-start(f32[64,4096]{1,0:T(8,128)} %get-tuple-element.22), channel_id=1, source_target_pairs={{0,128},{128,0},{1,129},{129,1},{2,130},{130,2},{3,131},{131,3},{4... | collective-permute-start | bytes 3145736 | tf_op jit(solution)/shard_map/ppermute | solution.py:262
  52.0 10.0 %collective-permute-start.6 = (bf16[16,1536]{1,0:T(8,128)(2,1)S(1)}, bf16[16,1536]{1,0:T(8,128)(2,1)S(1)}, u32[]{:S(2)}, u32[]{:S(2)}) collective-permute-start(bf16[16,1536]{1,0:T(8,128)(2,1)S(1)} %dynamic_slice.3), channel_id=1, source_target_pairs={{0,256},{256,0},{1,257},{257,1},{2,258},{258,2},{3,259},{259,3},{4... | collective-permute-start | bytes 147464 | tf_op jit(solution)/shard_map/ppermute | solution.py:262
  62.8 21.0 %all-to-all-start = ((bf16[8,16,1536]{2,1,0:T(8,128)(2,1)}), bf16[8,16,1536]{2,1,0:T(8,128)(2,1)S(1)}, u32[]{:S(2)}, u32[]{:S(2)}) async-start(bf16[8,16,1536]{2,1,0:T(8,128)(2,1)} %broadcast_in_dim.2), calls=%async_computation | async-start | bytes 786432 | tf_op jit(solution)/shard_map/all_to_all | solution.py:282
  83.8 0.7 copy-start.6
  91.1 18.0 %all-to-all-start.1 = ((bf16[4,128,1024]{2,1,0:T(8,128)(2,1)}), bf16[4,128,1024]{2,1,0:T(8,128)(2,1)S(1)}, u32[]{:S(2)}, u32[]{:S(2)}) async-start(bf16[4,128,1024]{2,1,0:T(8,128)(2,1)} %shard_map.61), calls=%async_computation.1 | async-start | bytes 2097152 | tf_op jit(solution)/shard_map/all_to_all | solution.py:289
  96.8 14.2 %collective-permute-start.8 = (bf16[32,4096]{1,0:T(8,128)(2,1)S(1)}, bf16[32,4096]{1,0:T(8,128)(2,1)S(1)}, u32[]{:S(2)}, u32[]{:S(2)}) collective-permute-start(bf16[32,4096]{1,0:T(8,128)(2,1)S(1)} %get-tuple-element.27), channel_id=1, source_target_pairs={{0,256},{256,0},{1,257},{257,1},{2,258},{258,2},{3,259},{259,3},{4... | collective-permute-start | bytes 786440 | tf_op jit(solution)/shard_map/ppermute | solution.py:262
  109.1 0.7 copy-start.5
  111.1 19.0 %all-to-all-start.2 = ((bf16[8,16,1024]{2,1,0:T(8,128)(2,1)}), bf16[8,16,1024]{2,1,0:T(8,128)(2,1)S(1)}, u32[]{:S(2)}, u32[]{:S(2)}) async-start(bf16[8,16,1024]{2,1,0:T(8,128)(2,1)} %bitcast.6), calls=%async_computation.2 | async-start | bytes 524288 | tf_op jit(solution)/shard_map/all_to_all | solution.py:294

commit v12 on v11

--- a/solution.py
+++ b/solution.py
@@ -274,14 +274,15 @@
     total, send = prepare(acts_in, grad_out)
     total = total + across(send, 1, 0, 1).astype(F32)
     total = total + across(total.astype(BF), 2, 0, 3).astype(F32)
-    send = total.astype(BF)
+    share = jnp.broadcast_to(share[None], (8,) + share.shape)
+    send, share = barrier((total.astype(BF), share))
     pair = across(send, 7, 1, 0)
     left2, left3 = across(send[0], 0, 2, 0), across(send[0], 0, 3, 0)
 
-    share = jnp.broadcast_to(share[None], (8,) + share.shape)
     far_tokens = lax.all_to_all(share, "row", 0, 0, tiled=True)
 
     keep, send = stats(place, total, pair, left2, left3, acts, grad_out)
+    send, far_tokens = barrier((send, far_tokens))
     near_rows, far_rows = core_sum(keep, swap(send, "core"))
     near_rows, near_tokens, far_tokens = barrier((near_rows, grad_out, far_tokens))
     far_rows = swap(far_rows, "yh")

time: 132 us -> 117 us (0.89)
  the two profiles are of different devices: /device:TPU:2 before, /device:TPU:66 now
where the time goes in v12:
time: 117 us; the launch traced here: 116 us
  starting transfers between devices  66 us (56%)
  waiting for transfers between devices  30.1 us (26%)
  Pallas kernels  13.6 us (12%)
  local copies, waits for them, and re-layouts  5.38 us (5%)
    ppermute x5, starting transfers between devices, across(): return lax.ppermute(value, ('row', 'yl', 'x'), perm)  24.7 us
    ppermute x4, starting transfers between devices, swap(): return lax.ppermute(value, axis, [(0, 1), (1, 0)])  18.1 us
    all_to_all x1, waiting for transfers between devices, body(): input_grad = y_sum(lax.all_to_all(chunks, ('yh', 'yl'), 0, 0, tiled=True))  10.4 us
    all_to_all x1, starting transfers between devices, body(): input_grad = y_sum(lax.all_to_all(chunks, ('yh', 'yl'), 0, 0, tiled=True))  9.76 us
    all_to_all x1, starting transfers between devices, body(): far_tokens = lax.all_to_all(share, 'row', 0, 0, tiled=True)  8.14 us
    all_to_all x1, waiting for transfers between devices, body(): got = lax.all_to_all(both, 'x', 0, 0, tiled=True)  7.65 us
    ppermute x5, waiting for transfers between devices, across(): return lax.ppermute(value, ('row', 'yl', 'x'), perm)  6.99 us
    pallas_call x1, Pallas kernels, product(): pl.pallas_call(product_kernel, out_shape=jax.ShapeDtypeStruct((4, count,...  6.57 us
  transfers between devices with their start and end apart: 12, of which 6 were waited for; matrix products, arithmetic and copies ran while one was open for 1% of the time, Pallas kernels for 5%

profile of v12, /device:TPU:66, one launch (start us, length us, event | category | flops | bytes accessed | tf_op | source)
XLA Modules:
  0.0 115.9 jit_solution(1340773604114873157)
XLA Ops:
  0.6 1.9 %collective-permute-start.7 = (bf16[2048,768]{1,0:T(8,128)(2,1)}, bf16[2048,768]{1,0:T(8,128)(2,1)}, u32[]{:S(2)}, u32[]{:S(2)}) collective-permute-start(bf16[2048,768]{1,0:T(8,128)(2,1)} %bitcast.8), channel_id=1, source_target_pairs={{0,128},{128,0},{1,129},{129,1},{2,130},{130,2},{3,131},{131,3},{4... | collective-permute-start | bytes 9437192 | tf_op jit(solution)/shard_map/ppermute | solution.py:262
  3.4 1.1 copy-done
  4.5 1.0 copy-done.2
  6.1 6.9 %collective-permute-start = (bf16[2,128,128]{2,1,0:T(8,128)(2,1)S(1)}, bf16[2,128,128]{2,1,0:T(8,128)(2,1)S(1)}, u32[]{:S(2)}, u32[]{:S(2)}) collective-permute-start(bf16[2,128,128]{2,1,0:T(8,128)(2,1)S(1)} %get-tuple-element.24), channel_id=1, source_target_pairs={{0,17},{1,16},{2,19},{3,18},{4,21},{5,20},{6,23},{7,22},{8,25},{9,... | collective-permute-start | bytes 196616 | tf_op jit(solution)/shard_map/ppermute | solution.py:266
  13.0 2.7 %collective-permute-done = bf16[2,128,128]{2,1,0:T(8,128)(2,1)S(1)} collective-permute-done((bf16[2,128,128]{2,1,0:T(8,128)(2,1)S(1)}, bf16[2,128,128]{2,1,0:T(8,128)(2,1)S(1)}, u32[]{:S(2)}, u32[]{:S(2)}) %collective-permute-start) | collective-permute-done | bytes 65568 | tf_op jit(solution)/shard_map/ppermute | solution.py:266
  15.7 4.7 %collective-permute-start.1 = (bf16[2,128,128]{2,1,0:T(8,128)(2,1)S(1)}, bf16[2,128,128]{2,1,0:T(8,128)(2,1)S(1)}, u32[]{:S(2)}, u32[]{:S(2)}) collective-permute-start(bf16[2,128,128]{2,1,0:T(8,128)(2,1)S(1)} %fusion), channel_id=1, source_target_pairs={{0,35},{1,34},{2,33},{3,32},{4,39},{5,38},{6,37},{7,36},{8,43},{9,... | collective-permute-start | bytes 196616 | tf_op jit(solution)/shard_map/ppermute | solution.py:266
  20.4 7.7 %collective-permute-start.2 = (bf16[16,1536]{1,0:T(8,128)(2,1)S(1)}, bf16[16,1536]{1,0:T(8,128)(2,1)S(1)}, u32[]{:S(2)}, u32[]{:S(2)}) collective-permute-start(bf16[16,1536]{1,0:T(8,128)(2,1)S(1)} %dynamic_slice.3), channel_id=1, source_target_pairs={{0,256},{256,0},{1,257},{257,1},{2,258},{258,2},{3,259},{259,3},{4... | collective-permute-start | bytes 147464 | tf_op jit(solution)/shard_map/ppermute | solution.py:262
  28.2 2.1 %collective-permute-done.2 = bf16[16,1536]{1,0:T(8,128)(2,1)S(1)} collective-permute-done((bf16[16,1536]{1,0:T(8,128)(2,1)S(1)}, bf16[16,1536]{1,0:T(8,128)(2,1)S(1)}, u32[]{:S(2)}, u32[]{:S(2)}) %collective-permute-start.2) | collective-permute-done | bytes 49184 | tf_op jit(solution)/shard_map/ppermute | solution.py:262
  31.1 8.1 %all-to-all-start = ((bf16[8,16,1536]{2,1,0:T(8,128)(2,1)}), bf16[8,16,1536]{2,1,0:T(8,128)(2,1)S(1)}, u32[]{:S(2)}, u32[]{:S(2)}) async-start(bf16[8,16,1536]{2,1,0:T(8,128)(2,1)} %broadcast_in_dim.2), calls=%async_computation | async-start | bytes 786432 | tf_op jit(solution)/shard_map/all_to_all | solution.py:282
  39.2 5.5 %collective-permute-start.5 = (bf16[128,128]{1,0:T(8,128)(2,1)S(1)}, bf16[128,128]{1,0:T(8,128)(2,1)S(1)}, u32[]{:S(2)}, u32[]{:S(2)}) collective-permute-start(bf16[128,128]{1,0:T(8,128)(2,1)S(1)} %slice_bitcast_fusion), channel_id=1, source_target_pairs={{0,12},{1,13},{2,14},{3,15},{4,8},{5,9},{6,10},{7,11},{8,4},{9,5},... | collective-permute-start | bytes 98312 | tf_op jit(solution)/shard_map/ppermute | solution.py:266
  44.7 1.9 %collective-permute-start.4 = (bf16[128,128]{1,0:T(8,128)(2,1)S(1)}, bf16[128,128]{1,0:T(8,128)(2,1)S(1)}, u32[]{:S(2)}, u32[]{:S(2)}) collective-permute-start(bf16[128,128]{1,0:T(8,128)(2,1)S(1)} %slice_bitcast_fusion), channel_id=1, source_target_pairs={{0,8},{1,9},{2,10},{3,11},{4,12},{5,13},{6,14},{7,15},{8,0},{9,1},... | collective-permute-start | bytes 98312 | tf_op jit(solution)/shard_map/ppermute | solution.py:266
  46.6 5.7 %collective-permute-start.3 = (bf16[2,128,128]{2,1,0:T(8,128)(2,1)S(1)}, bf16[2,128,128]{2,1,0:T(8,128)(2,1)S(1)}, u32[]{:S(2)}, u32[]{:S(2)}) collective-permute-start(bf16[2,128,128]{2,1,0:T(8,128)(2,1)S(1)} %get-tuple-element.26), channel_id=1, source_target_pairs={{0,116},{1,117},{2,118},{3,119},{4,112},{5,113},{6,114},{7,115},{8... | collective-permute-start | bytes 196616 | tf_op jit(solution)/shard_map/ppermute | solution.py:266
  52.5 4.2 %collective-permute-done.3.pair_ref = bf16[2,128,128]{2,1,0:T(8,128)(2,1)S(1)} collective-permute-done((bf16[2,128,128]{2,1,0:T(8,128)(2,1)S(1)}, bf16[2,128,128]{2,1,0:T(8,128)(2,1)S(1)}, u32[]{:S(2)}, u32[]{:S(2)}) %collective-permute-start.3) | collective-permute-done | bytes 65568 | tf_op jit(solution)/shard_map/ppermute | solution.py:266
  56.7 3.6 %shard_map.59 = (f32[64,4096]{1,0:T(8,128)S(1)}, f32[64,4096]{1,0:T(8,128)S(1)}) custom-call(s32[4]{0:T(128)S(1)} %pad_add_fusion.place, f32[2,128,128]{2,1,0:T(8,128)S(1)} %get-tuple-element.42.total_ref, bf16[2,128,128]{2,1,0:T(8,128)(2,1)S(1)} %collective-permute-done.3.pair_ref, bf16[128,128]{1,0:T(8,128)(2,1)S(1)} %collective-permute-done.4.left2_ref, ...), custom_call_target="tpu_custom_call" | custom-call | flops 1 | bytes 1 | tf_op jit(solution)/shard_map/pallas_call | solution.py:194
  60.3 0.9 copy-done.6
  61.2 1.9 %collective-permute-start.6 = (f32[64,4096]{1,0:T(8,128)}, f32[64,4096]{1,0:T(8,128)S(1)}, u32[]{:S(2)}, u32[]{:S(2)}) collective-permute-start(f32[64,4096]{1,0:T(8,128)} %copy-done.6), channel_id=1, source_target_pairs={{0,128},{128,0},{1,129},{129,1},{2,130},{130,2},{3,131},{131,3},{4... | collective-permute-start | bytes 3145736 | tf_op jit(solution)/shard_map/ppermute | solution.py:262
  63.2 2.8 %collective-permute-done.6.got_ref = f32[64,4096]{1,0:T(8,128)S(1)} collective-permute-done((f32[64,4096]{1,0:T(8,128)}, f32[64,4096]{1,0:T(8,128)S(1)}, u32[]{:S(2)}, u32[]{:S(2)}) %collective-permute-start.6) | collective-permute-done | bytes 1048608 | tf_op jit(solution)/shard_map/ppermute | solution.py:262
  66.1 6.6 %shard_map.61 = bf16[4,128,1024]{2,1,0:T(8,128)(2,1)} custom-call(s32[4]{0:T(128)} %copy-done.4, bf16[128,3072]{1,0:T(8,128)(2,1)} %near_ref, bf16[8,16,1536]{2,1,0:T(8,128)(2,1)} %copy-done.7, bf16[2048,768]{1,0:T(8,128)(2,1)} %bitcast.9, bf16[2048,768]{1,0:T(8,128)(2,1)} %bitcast.10, bf16[2048,768]{1,0:T(8,128)(2,1)} %collective-permute-done.7.other_lo.other_hi, ...), custom_call_target="tpu_custom_call" | custom-call | flops 1 | bytes 1 | tf_op jit(solution)/shard_map/pallas_call | solution.py:81
  72.7 5.3 %all-to-all-start.1 = ((bf16[4,128,1024]{2,1,0:T(8,128)(2,1)}), bf16[4,128,1024]{2,1,0:T(8,128)(2,1)S(1)}, u32[]{:S(2)}, u32[]{:S(2)}) async-start(bf16[4,128,1024]{2,1,0:T(8,128)(2,1)} %shard_map.61), calls=%async_computation.1 | async-start | bytes 2097152 | tf_op jit(solution)/shard_map/all_to_all | solution.py:290
  78.0 6.6 %collective-permute-start.8 = (bf16[32,4096]{1,0:T(8,128)(2,1)S(1)}, bf16[32,4096]{1,0:T(8,128)(2,1)S(1)}, u32[]{:S(2)}, u32[]{:S(2)}) collective-permute-start(bf16[32,4096]{1,0:T(8,128)(2,1)S(1)} %get-tuple-element.35), channel_id=1, source_target_pairs={{0,256},{256,0},{1,257},{257,1},{2,258},{258,2},{3,259},{259,3},{4... | collective-permute-start | bytes 786440 | tf_op jit(solution)/shard_map/ppermute | solution.py:262
  84.6 7.7 %all-to-all-done.1.got_ref = bf16[4,128,1024]{2,1,0:T(8,128)(2,1)S(1)} async-done(((bf16[4,128,1024]{2,1,0:T(8,128)(2,1)}), bf16[4,128,1024]{2,1,0:T(8,128)(2,1)S(1)}, u32[]{:S(2)}, u32[]{:S(2)}) %all-to-all-start.1) | async-done | bytes 1048608 | tf_op jit(solution)/shard_map/all_to_all | solution.py:290
  92.9 1.4 %shard_map.62 = bf16[2,64,1024]{2,1,0:T(8,128)(2,1)} custom-call(s32[4]{0:T(128)S(1)} %copy-done.5, bf16[4,128,1024]{2,1,0:T(8,128)(2,1)S(1)} %all-to-all-done.1.got_ref), custom_call_target="tpu_custom_call" | custom-call | flops 1 | bytes 1 | tf_op jit(solution)/shard_map/pallas_call | solution.py:115
  94.2 9.8 %all-to-all-start.2 = ((bf16[8,16,1024]{2,1,0:T(8,128)(2,1)}), bf16[8,16,1024]{2,1,0:T(8,128)(2,1)S(1)}, u32[]{:S(2)}, u32[]{:S(2)}) async-start(bf16[8,16,1024]{2,1,0:T(8,128)(2,1)} %bitcast.6), calls=%async_computation.2 | async-start | bytes 524288 | tf_op jit(solution)/shard_map/all_to_all | solution.py:295
  104.8 10.4 %all-to-all-done.2.got_ref = bf16[8,16,1024]{2,1,0:T(8,128)(2,1)S(1)} async-done(((bf16[8,16,1024]{2,1,0:T(8,128)(2,1)}), bf16[8,16,1024]{2,1,0:T(8,128)(2,1)S(1)}, u32[]{:S(2)}, u32[]{:S(2)}) %all-to-all-start.2) | async-done | bytes 262176 | tf_op jit(solution)/shard_map/all_to_all | solution.py:295
  (29 shorter events, 4.5 us)
Async XLA Ops:
  0.6 65.5 %collective-permute-start.7 = (bf16[2048,768]{1,0:T(8,128)(2,1)}, bf16[2048,768]{1,0:T(8,128)(2,1)}, u32[]{:S(2)}, u32[]{:S(2)}) collective-permute-start(bf16[2048,768]{1,0:T(8,128)(2,1)} %bitcast.8), channel_id=1, source_target_pairs={{0,128},{128,0},{1,129},{129,1},{2,130},{130,2},{3,131},{131,3},{4... | collective-permute-start | bytes 9437192 | tf_op jit(solution)/shard_map/ppermute | solution.py:262
  3.4 1.1 copy-start
  4.5 1.0 copy-start.2
  5.6 51.2 %copy-start.1 = (bf16[128,3072]{1,0:T(8,128)(2,1)S(1)}, bf16[128,3072]{1,0:T(8,128)(2,1)}, u32[]{:S(2)}) copy-start(bf16[128,3072]{1,0:T(8,128)(2,1)} %near_ref) | copy-start | bytes 2359300
  5.6 51.2 %copy-start.3 = (bf16[128,2048]{1,0:T(8,128)(2,1)S(1)}, bf16[128,2048]{1,0:T(8,128)(2,1)}, u32[]{:S(2)}) copy-start(bf16[128,2048]{1,0:T(8,128)(2,1)} %acts_hbm.1) | copy-start | bytes 1572868
  6.1 9.7 %collective-permute-start = (bf16[2,128,128]{2,1,0:T(8,128)(2,1)S(1)}, bf16[2,128,128]{2,1,0:T(8,128)(2,1)S(1)}, u32[]{:S(2)}, u32[]{:S(2)}) collective-permute-start(bf16[2,128,128]{2,1,0:T(8,128)(2,1)S(1)} %get-tuple-element.24), channel_id=1, source_target_pairs={{0,17},{1,16},{2,19},{3,18},{4,21},{5,20},{6,23},{7,22},{8,25},{9,... | collective-permute-start | bytes 196616 | tf_op jit(solution)/shard_map/ppermute | solution.py:266
  15.7 12.4 %collective-permute-start.1 = (bf16[2,128,128]{2,1,0:T(8,128)(2,1)S(1)}, bf16[2,128,128]{2,1,0:T(8,128)(2,1)S(1)}, u32[]{:S(2)}, u32[]{:S(2)}) collective-permute-start(bf16[2,128,128]{2,1,0:T(8,128)(2,1)S(1)} %fusion), channel_id=1, source_target_pairs={{0,35},{1,34},{2,33},{3,32},{4,39},{5,38},{6,37},{7,36},{8,43},{9,... | collective-permute-start | bytes 196616 | tf_op jit(solution)/shard_map/ppermute | solution.py:266
  20.4 9.9 %collective-permute-start.2 = (bf16[16,1536]{1,0:T(8,128)(2,1)S(1)}, bf16[16,1536]{1,0:T(8,128)(2,1)S(1)}, u32[]{:S(2)}, u32[]{:S(2)}) collective-permute-start(bf16[16,1536]{1,0:T(8,128)(2,1)S(1)} %dynamic_slice.3), channel_id=1, source_target_pairs={{0,256},{256,0},{1,257},{257,1},{2,258},{258,2},{3,259},{259,3},{4... | collective-permute-start | bytes 147464 | tf_op jit(solution)/shard_map/ppermute | solution.py:262
  31.1 30.1 %all-to-all-start = ((bf16[8,16,1536]{2,1,0:T(8,128)(2,1)}), bf16[8,16,1536]{2,1,0:T(8,128)(2,1)S(1)}, u32[]{:S(2)}, u32[]{:S(2)}) async-start(bf16[8,16,1536]{2,1,0:T(8,128)(2,1)} %broadcast_in_dim.2), calls=%async_computation | async-start | bytes 786432 | tf_op jit(solution)/shard_map/all_to_all | solution.py:282
  39.2 13.2 %collective-permute-start.5 = (bf16[128,128]{1,0:T(8,128)(2,1)S(1)}, bf16[128,128]{1,0:T(8,128)(2,1)S(1)}, u32[]{:S(2)}, u32[]{:S(2)}) collective-permute-start(bf16[128,128]{1,0:T(8,128)(2,1)S(1)} %slice_bitcast_fusion), channel_id=1, source_target_pairs={{0,12},{1,13},{2,14},{3,15},{4,8},{5,9},{6,10},{7,11},{8,4},{9,5},... | collective-permute-start | bytes 98312 | tf_op jit(solution)/shard_map/ppermute | solution.py:266
  44.7 7.7 %collective-permute-start.4 = (bf16[128,128]{1,0:T(8,128)(2,1)S(1)}, bf16[128,128]{1,0:T(8,128)(2,1)S(1)}, u32[]{:S(2)}, u32[]{:S(2)}) collective-permute-start(bf16[128,128]{1,0:T(8,128)(2,1)S(1)} %slice_bitcast_fusion), channel_id=1, source_target_pairs={{0,8},{1,9},{2,10},{3,11},{4,12},{5,13},{6,14},{7,15},{8,0},{9,1},... | collective-permute-start | bytes 98312 | tf_op jit(solution)/shard_map/ppermute | solution.py:266
  46.6 10.1 %collective-permute-start.3 = (bf16[2,128,128]{2,1,0:T(8,128)(2,1)S(1)}, bf16[2,128,128]{2,1,0:T(8,128)(2,1)S(1)}, u32[]{:S(2)}, u32[]{:S(2)}) collective-permute-start(bf16[2,128,128]{2,1,0:T(8,128)(2,1)S(1)} %get-tuple-element.26), channel_id=1, source_target_pairs={{0,116},{1,117},{2,118},{3,119},{4,112},{5,113},{6,114},{7,115},{8... | collective-permute-start | bytes 196616 | tf_op jit(solution)/shard_map/ppermute | solution.py:266
  52.5 13.7 %copy-start.4 = (s32[4]{0:T(128)}, s32[4]{0:T(128)S(1)}, u32[]{:S(2)}) copy-start(s32[4]{0:T(128)S(1)} %pad_add_fusion.place) | copy-start | bytes 52
  60.3 1.0 copy-start.6
  61.2 4.9 %copy-start.7 = (bf16[8,16,1536]{2,1,0:T(8,128)(2,1)}, bf16[8,16,1536]{2,1,0:T(8,128)(2,1)S(1)}, u32[]{:S(2)}) copy-start(bf16[8,16,1536]{2,1,0:T(8,128)(2,1)S(1)} %all-to-all-done.far_ref) | copy-start | bytes 1179652
  61.2 4.8 %collective-permute-start.6 = (f32[64,4096]{1,0:T(8,128)}, f32[64,4096]{1,0:T(8,128)S(1)}, u32[]{:S(2)}, u32[]{:S(2)}) collective-permute-start(f32[64,4096]{1,0:T(8,128)} %copy-done.6), channel_id=1, source_target_pairs={{0,128},{128,0},{1,129},{129,1},{2,130},{130,2},{3,131},{131,3},{4... | collective-permute-start | bytes 3145736 | tf_op jit(solution)/shard_map/ppermute | solution.py:262
  72.7 19.5 %all-to-all-start.1 = ((bf16[4,128,1024]{2,1,0:T(8,128)(2,1)}), bf16[4,128,1024]{2,1,0:T(8,128)(2,1)S(1)}, u32[]{:S(2)}, u32[]{:S(2)}) async-start(bf16[4,128,1024]{2,1,0:T(8,128)(2,1)} %shard_map.61), calls=%async_computation.1 | async-start | bytes 2097152 | tf_op jit(solution)/shard_map/all_to_all | solution.py:290
  78.0 16.2 %collective-permute-start.8 = (bf16[32,4096]{1,0:T(8,128)(2,1)S(1)}, bf16[32,4096]{1,0:T(8,128)(2,1)S(1)}, u32[]{:S(2)}, u32[]{:S(2)}) collective-permute-start(bf16[32,4096]{1,0:T(8,128)(2,1)S(1)} %get-tuple-element.35), channel_id=1, source_target_pairs={{0,256},{256,0},{1,257},{257,1},{2,258},{258,2},{3,259},{259,3},{4... | collective-permute-start | bytes 786440 | tf_op jit(solution)/shard_map/ppermute | solution.py:262
  92.2 0.7 copy-start.5
  94.2 21.0 %all-to-all-start.2 = ((bf16[8,16,1024]{2,1,0:T(8,128)(2,1)}), bf16[8,16,1024]{2,1,0:T(8,128)(2,1)S(1)}, u32[]{:S(2)}, u32[]{:S(2)}) async-start(bf16[8,16,1024]{2,1,0:T(8,128)(2,1)} %bitcast.6), calls=%async_computation.2 | async-start | bytes 524288 | tf_op jit(solution)/shard_map/all_to_all | solution.py:295
